TPU v7x, 32 devices: a whole 2x2x4 slice. The times are simulated.
32 devices in a mesh: dp: 8 (over y, x, core), hid: 4 (over z).
Axes of the slice: x: 2, y: 2, z: 4, core: 2. Of those that a mesh axis runs over, the one named last changes fastest.
Arguments:
- tokens: bfloat16 [192, 196, 384], P('dp'), may hold values from -6 to 6
- masks: int32 [192, 196], P('dp'), may hold values 0 or 1
- cotangent: bfloat16 [192, 196, 384], P('dp'), may hold values from -6 to 6
- aff_scale: float32 [2, 2, 384], replicated, may hold values from 0.25 to 1.75
- aff_shift: float32 [2, 2, 384], replicated, may hold values from -3 to 3
- layer_scale: float32 [2, 2, 384], replicated, may hold values from 0.25 to 1.75
- crosspatch_weight: bfloat16 [2, 196, 196], replicated, may hold values from -0.4375 to 0.4375
- cross_bias: float32 [2, 196], replicated, may hold values from -3 to 3
- fc1_weight: bfloat16 [2, 384, 1536], P(None, 'dp', 'hid'), may hold values from -0.3125 to 0.3125
- fc1_bias: float32 [2, 1536], replicated, may hold values from -3 to 3
- fc2_weight: bfloat16 [2, 384, 1536], P(None, 'dp', 'hid'), may hold values from -0.15625 to 0.15625
- fc2_bias: float32 [2, 384], replicated, may hold values from -2 to 2
Outputs:
- output: bfloat16 [192, 196, 384], P('dp')
- tokens_grad: bfloat16 [192, 196, 384], P('dp')
- aff_scale_grad: float32 [2, 2, 384], replicated
- aff_shift_grad: float32 [2, 2, 384], replicated
- layer_scale_grad: float32 [2, 2, 384], replicated
- cross_weight_grad: float32 [2, 196, 196], replicated
- cross_bias_grad: float32 [2, 196], replicated
- fc1_weight_grad: float32 [2, 384, 1536], P(None, 'dp', 'hid')
- fc1_bias_grad: float32 [2, 1536], P(None, 'hid')
- fc2_weight_grad: float32 [2, 384, 1536], P(None, 'dp', 'hid')
- fc2_bias_grad: float32 [2, 384], replicated
All inputs are finite; a program needn't handle non-finite values. No bound on the sum of `masks` on one device may be relied on, other than what follows from the above.
Results may differ from a plain program's by a relative error of at most 0.02.
Values may be sent and summed in bfloat16 or wider, within the bound.
No kernel may reach another device: no remote copies, remote signals or barrier semaphores. Data moves between devices by JAX's collectives and lax.ppermute only.
A program may use at most 256 MiB of HBM per device.

v0:
```python
import functools

import jax
import jax.numpy as jnp
from jax import lax
from jax.experimental import pallas as pl
from jax.experimental.pallas import tpu as pltpu
from jax.sharding import PartitionSpec as P

BF = jnp.bfloat16
F32 = jnp.float32
NN = (((1,), (0,)), ((), ()))
NT = (((1,), (1,)), ((), ()))
TN = (((0,), (0,)), ((), ()))
SQRT_HALF = 0.7071067811865476
PDF_SCALE = 0.3989422804014327
S0, T0, S1, T1, LS0, LS1, B2, B1 = range(8)
STEP = 4
GROUP = 8


def dot(a, b, dims):
    return lax.dot_general(a, b, dims, preferred_element_type=F32)


def round_up(n, k):
    return (n + k - 1) // k * k


class Sizes:
    def __init__(self, tokens, fc1, n_dp, n_hid):
        self.count, self.patches, self.width = tokens.shape
        self.layers, self.shard, self.own = fc1.shape
        self.n_dp, self.n_hid = n_dp, n_hid
        self.hidden = self.own * n_hid
        self.rows = round_up(self.patches, 8)
        self.depth = round_up(self.patches + 2, 16)
        self.m = STEP * self.rows
        self.small = self.rows + 16
        self.blocks = self.shard % 16 == 0 and self.own % 128 == 0


def kernel_body(sz, kept, names, *args):
    r = dict(zip(names, args))
    meta = r["meta"]
    step = pl.program_id(0)
    last = pl.num_programs(0) - 1
    layers, rows, patches, depth, m = sz.layers, sz.rows, sz.patches, sz.depth, sz.m
    alone = kept != sz.own
    whole = patches // 16 * 16
    pair = 2 * rows
    blocks = [slice(i, min(i + pair, m)) for i in range(0, m, pair)]
    lane = lax.broadcasted_iota(jnp.int32, (1, depth), 1)
    columns = pl.ds(pl.multiple_of(meta[1] * kept, 128), kept)
    mine = pl.ds(pl.multiple_of(meta[2] * sz.own, 128), sz.own)
    theirs = pl.ds(pl.multiple_of(meta[3] * sz.own, 128), sz.own)
    x, grad, gw = r["x"], r["grad"], r["gw"]

    @pl.when(step == 0)
    def _():
        if sz.blocks:
            for l in range(layers):
                for i in range(2):
                    for half in range(2):
                        src = r[f"w{i}part{half}_{l}"]
                        n_part = src.shape[0]
                        for k in range(n_part):
                            at = meta[4 + i * sz.n_dp + half * n_part + k] * sz.shard
                            at = pl.ds(pl.multiple_of(at, 16), sz.shard)
                            pltpu.make_async_copy(
                                src.at[k], r["w"].at[i, l, at], r["arrive"].at[i, l]
                            ).start()
        for name in ("gwc", "gsum", "gb1"):
            r[name][...] = jnp.zeros_like(r[name])
        for name in ("tok", "cot"):
            staged = r[name + "f"]
            for c in range(sz.width // 128):
                part = r[name][:, :, c * 128 : (c + 1) * 128].astype(F32)
                staged[c, : patches * GROUP, :] = part.reshape(patches * GROUP, 128)
                staged[c, patches * GROUP :, :] = jnp.zeros(((rows - patches) * GROUP, 128), F32)
        if alone:
            gw[...] = jnp.zeros_like(gw)
        else:
            pltpu.make_async_copy(r["carry"], gw, r["carried"]).start()

    def weight_ready(i, l):
        if sz.blocks:

            @pl.when(step == 0)
            def _():
                ref = r["w"].at[i, l]
                pltpu.make_async_copy(ref, ref, r["arrive"].at[i, l]).wait()

    def weight(i, l):
        return r["w"][i, l]

    def row(name, l, k):
        return r[name][l, k : k + 1, :]

    def image(g):
        return slice(g * rows, (g + 1) * rows)

    def add(l, kind, v):
        r["gsum"][l, kind] += jnp.sum(v.reshape(v.shape[0] // 8, 8, v.shape[1]), axis=0)

    def unstage(name, g):
        at = pl.ds(step * STEP + g, rows, stride=GROUP)
        return jnp.concatenate([r[name][c, at, :] for c in range(sz.width // 128)], axis=1)

    def stage(name, g, v):
        at = pl.ds(step * STEP + g, rows, stride=GROUP)
        for c in range(sz.width // 128):
            r[name][c, at, :] = v[:, c * 128 : (c + 1) * 128]

    for g in range(STEP):
        x[0, image(g), :] = unstage("tokf", g)
    def forward(l, _):
        mid, mixed, crossed = r["mid"], r["mixed"], r["crossed"]
        for g in range(STEP):
            x_in = x[l, image(g), :]
            v = x_in * row("scale", l, 0) + row("shift", l, 0)
            mixed[l, g, :whole, :] = v[:whole].astype(BF)
            left = lax.broadcasted_iota(jnp.int32, (rows - whole, 1), 0) + whole
            tail = jnp.where(left < patches, v[whole:], 1.0)
            if depth > rows:
                tail = jnp.concatenate([tail, jnp.ones((depth - rows, sz.width), F32)], axis=0)
            mixed[l, g, whole:, :] = tail.astype(BF)
            wk = r["wc"][l] * jnp.where(lane < patches, r["keep"][g], 1.0).astype(BF)
            c = dot(wk, mixed[l, g], NN)
            crossed[l, g, :rows, :] = c.astype(BF)
            mid[l, image(g), :] = x_in + row("ls", l, 0) * c
        for at in blocks:
            v = mid[l, at, :] * row("scale", l, 1) + row("shift", l, 1)
            r["normed"][l, at, :] = v.astype(BF)
        weight_ready(0, l)
        for at in blocks:
            h = dot(r["normed"][l, at, :], weight(0, l), NN) + r["b1"][l]
            phi = 0.5 + 0.5 * lax.erf(h * SQRT_HALF)
            r["act"][l, at, :] = (h * phi).astype(BF)
            r["h"][l, at, :] = h.astype(BF)
            r["phi"][l, at, :] = phi.astype(BF)
        weight_ready(1, l)
        for at in blocks:
            branch = dot(r["act"][l, at, :], weight(1, l), NT) + r["b2"][l]
            r["branch"][l, at, :] = branch.astype(BF)
            x[l + 1, at, :] = mid[l, at, :] + row("ls", l, 1) * branch
    lax.fori_loop(0, layers, forward, None)
    for g in range(STEP):
        stage("tokf", g, x[layers, image(g), :])
        grad[image(g), :] = unstage("cotf", g)

    if not alone:

        @pl.when(step == 0)
        def _():
            pltpu.make_async_copy(r["carry"], gw, r["carried"]).wait()

    def backward(back, _):
        l = layers - 1 - back
        for at in blocks:
            g_out = grad[at, :]
            add(l, LS1, g_out * r["branch"][l, at, :].astype(F32))
            bg = row("ls", l, 1) * g_out
            add(l, B2, bg)
            r["bg"][at, :] = bg.astype(BF)
        for at in blocks:
            act_grad = dot(r["bg"][at, :], weight(1, l), NN)
            h = r["h"][l, at, :].astype(F32)
            slope = r["phi"][l, at, :].astype(F32) + h * (jnp.exp(h * h * -0.5) * PDF_SCALE)
            r["pg"][at, :] = (act_grad * slope).astype(BF)
        pg = r["pg"][:, columns]
        r["gb1"][l] += jnp.sum(pg.astype(F32).reshape(m // 8, 8, kept), axis=0)
        gw[0, l] += dot(r["normed"][l], pg, TN)
        gw[1, l] += dot(r["bg"][...], r["act"][l, :, columns], TN)
        for at in blocks:
            normed_grad = dot(r["pg"][at, :], weight(0, l), NT)
            add(l, S1, normed_grad * r["mid"][l, at, :])
            add(l, T1, normed_grad)
            grad[at, :] += row("scale", l, 1) * normed_grad
        for g in range(STEP):
            at = image(g)
            keep = r["keep"][g]
            mg = grad[at, :]
            add(l, LS0, mg * r["crossed"][l, g, :rows, :].astype(F32))
            cg = (row("ls", l, 0) * mg).astype(BF)
            r["gwc"][l] += dot(cg, r["mixed"][l, g], NT) * jnp.where(lane < patches, keep, 1.0)
            wk = r["wc"][l] * jnp.where(lane < patches, keep, 0.0).astype(BF)
            mixed_grad = dot(wk, cg, TN)[:rows]
            add(l, S0, mixed_grad * x[l, at, :])
            add(l, T0, mixed_grad)
            grad[at, :] = mg + row("scale", l, 0) * mixed_grad
    lax.fori_loop(0, layers, backward, None)
    for g in range(STEP):
        stage("cotf", g, grad[image(g), :])

    @pl.when(step == last)
    def _():
        def write_small(ref, wanted):
            for l in range(layers):
                sums = [jnp.sum(r["gsum"][l, k], axis=0, keepdims=True) for k in range(B1)]
                sums.append(jnp.sum(r["gb1"][l, :, wanted], axis=0, keepdims=True))
                table = jnp.concatenate(sums, axis=0)
                table = jnp.pad(table, ((0, 0), (0, 512 - sz.width)))
                gwc = jnp.pad(r["gwc"][l], ((0, 0), (0, 256 - depth)))
                full = jnp.concatenate([gwc, table[:, :256], table[:, 256:]], axis=0)
                ref[l] = full.astype(BF)

        for name, staged in (("out", "tokf"), ("tgrad", "cotf")):
            for c in range(sz.width // 128):
                v = r[staged][c, : patches * GROUP, :].reshape(patches, GROUP, 128)
                r[name][:, :, c * 128 : (c + 1) * 128] = v.astype(BF)

        def write_rows(ref, k, i, place, wanted):
            for l in range(layers):
                ref[k, l] = gw[i, l, place, wanted].astype(BF)

        if alone:
            write_small(r["small"], mine)
            write_small(r["send"], theirs)
            for i in range(2):
                for l in range(layers):
                    r["own"][i, l] = gw[i, l, :, mine]
                for k in range(sz.n_dp if sz.blocks else 1):
                    size = sz.shard if sz.blocks else sz.width
                    write_rows(r[f"blocks{i}"], k, i, slice(k * size, (k + 1) * size), theirs)
        else:
            write_small(r["small"], slice(None))
            for i in range(2):
                if sz.blocks:
                    for k in range(sz.n_dp):
                        at = meta[4 + (2 + i) * sz.n_dp + k] * sz.shard
                        at = pl.ds(pl.multiple_of(at, 16), sz.shard)
                        write_rows(r[f"blocks{i}"], k, i, at, slice(None))
                else:
                    write_rows(r[f"blocks{i}"], 0, i, slice(None), slice(None))


def run(sz, alone, meta, common, weights, carry=None):
    steps = GROUP // STEP
    w, m, layers = sz.width, sz.m, sz.layers
    kept = 2 * sz.own if alone else sz.own
    vmem = pl.BlockSpec(memory_space=pltpu.VMEM)
    anywhere = pl.BlockSpec(memory_space=pl.ANY)
    images = (sz.patches, GROUP, w)

    def group_spec(where):
        return pl.BlockSpec(
            images, lambda i, meta: (0, where(meta), 0), pipeline_mode=pl.Buffered(1)
        )

    def fixed_spec(block):
        return pl.BlockSpec(
            block, lambda i, meta: (0,) * len(block), pipeline_mode=pl.Buffered(1)
        )

    def in_all(meta):
        return meta[0]

    def in_part(meta):
        return 0

    keep_spec = pl.BlockSpec((STEP, 1, sz.depth), lambda i, meta: (meta[0] * steps + i, 0, 0))
    ins = [
        ("tok", common["tok"], group_spec(in_all)),
        ("cot", common["cot"], group_spec(in_all)),
        ("keep", common["keep"], keep_spec),
    ]
    for name in ("scale", "shift", "ls", "wc", "b1", "b2"):
        ins.append((name, common[name], vmem))
    scratch = []
    if sz.blocks:
        for l in range(layers):
            for i in range(2):
                for half in range(2):
                    ins.append((f"w{i}part{half}_{l}", weights[l][i][half], anywhere))
        scratch.append(("w", pltpu.VMEM((2, layers, w, sz.hidden), BF)))
        scratch.append(("arrive", pltpu.SemaphoreType.DMA((2, layers))))
    else:
        ins.append(("w", weights, vmem))
    if not alone:
        ins.append(("carry", carry, anywhere))
        scratch.append(("carried", pltpu.SemaphoreType.DMA))

    where, count = (in_part, GROUP) if alone else (in_all, sz.count)
    outs = [
        ("out", (sz.patches, count, w), BF, group_spec(where)),
        ("tgrad", (sz.patches, count, w), BF, group_spec(where)),
    ]
    small = (layers, sz.small, 256)
    block = (sz.n_dp, layers, sz.shard, sz.own) if sz.blocks else (1, layers, w, sz.own)
    outs.append(("small", small, BF, fixed_spec(small)))
    outs.append(("blocks0", block, BF, fixed_spec(block)))
    outs.append(("blocks1", block, BF, fixed_spec(block)))
    if alone:
        outs.append(("send", small, BF, fixed_spec(small)))
        own = (2, layers, w, sz.own)
        outs.append(("own", own, F32, fixed_spec(own)))
    for name, shape, dtype in (
        ("x", (layers + 1, m, w), F32),
        ("mid", (layers, m, w), F32),
        ("crossed", (layers, STEP, sz.depth, w), BF),
        ("mixed", (layers, STEP, sz.depth, w), BF),
        ("normed", (layers, m, w), BF),
        ("h", (layers, m, sz.hidden), BF),
        ("phi", (layers, m, sz.hidden), BF),
        ("act", (layers, m, sz.hidden), BF),
        ("branch", (layers, m, w), BF),
        ("grad", (m, w), F32),
        ("bg", (m, w), BF),
        ("pg", (m, sz.hidden), BF),
        ("gw", (2, layers, w, kept), F32),
        ("gwc", (layers, sz.rows, sz.depth), F32),
        ("gsum", (layers, B1, 8, w), F32),
        ("gb1", (layers, 8, kept), F32),
        ("tokf", (w // 128, GROUP * sz.rows, 128), F32),
        ("cotf", (w // 128, GROUP * sz.rows, 128), F32),
    ):
        scratch.append((name, pltpu.VMEM(shape, dtype)))
    names = ("meta",) + tuple(e[0] for e in ins + outs + scratch)
    flops = steps * m * 24 * w * sz.hidden
    results = pl.pallas_call(
        functools.partial(kernel_body, sz, kept, names),
        grid_spec=pltpu.PrefetchScalarGridSpec(
            num_scalar_prefetch=1,
            grid=(steps,),
            in_specs=[e[2] for e in ins],
            out_specs=[e[3] for e in outs],
            scratch_shapes=[e[1] for e in scratch],
        ),
        out_shape=[jax.ShapeDtypeStruct(e[1], e[2]) for e in outs],
        compiler_params=pltpu.CompilerParams(vmem_limit_bytes=60 * 2**20),
        cost_estimate=pl.CostEstimate(flops=flops, bytes_accessed=flops // 400, transcendentals=0),
    )(meta, *[e[1] for e in ins])
    return {e[0]: value for e, value in zip(outs, results)}


def swap(x, axis, k):
    n = lax.axis_size(axis)
    return lax.ppermute(x, axis, [(i, i ^ k) for i in range(n)])


def powers(n):
    return [2**k for k in range(1, n.bit_length() - 1)]


def gather_weights(sz, w1, w2):
    both = jnp.stack([w1, w2])
    parts = [both] + [swap(both, "hid", k) for k in range(1, sz.n_hid)]
    hid = lax.axis_index("hid")
    columns = []
    for j in range(sz.n_hid):
        v = parts[j]
        for h in range(1, sz.n_hid):
            v = jnp.where(hid == h, parts[j ^ h], v)
        columns.append(v)
    full = jnp.concatenate(columns, axis=2)
    got = [full[i][None] for i in range(2)]
    bits = powers(sz.n_dp)
    for step in range(len(bits)):
        moved = [swap(got[0], "dp", bits[step]), swap(got[1], "dp", bits[-1 - step])]
        got = [jnp.concatenate([g, v]) for g, v in zip(got, moved)]
    other = [swap(g, "dp", 1) for g in got]
    orders = []
    for seq in (bits, bits[::-1]):
        order = [0]
        for b in seq:
            order += [o ^ b for o in order]
        orders.append(order + [o ^ 1 for o in order])
    return got, other, orders


def exchange_orders(n_dp):
    bits = powers(n_dp)
    result = []
    for seq in ([1] + bits, [1] + bits[::-1]):
        order = [0]
        for b in reversed(seq):
            order = order + [o ^ b for o in order]
        result.append((seq, order))
    return result


def scatter_step(blocks, bit):
    n = blocks.shape[0] // 2
    got = swap(blocks[n:].astype(BF), "dp", bit)
    return blocks[:n].astype(F32) + got.astype(F32)


def on_device(
    tokens,
    masks,
    cotangent,
    aff_scale,
    aff_shift,
    layer_scale,
    crosspatch_weight,
    cross_bias,
    fc1_weight,
    fc1_bias,
    fc2_weight,
    fc2_bias,
):
    n_dp, n_hid = lax.axis_size("dp"), lax.axis_size("hid")
    sz = Sizes(tokens, fc1_weight, n_dp, n_hid)
    layers, patches = sz.layers, sz.patches
    me, hid = lax.axis_index("dp"), lax.axis_index("hid")
    half = hid % 2

    weights = []
    for l in range(layers):
        got, other, orders = gather_weights(sz, fc1_weight[l], fc2_weight[l])
        if sz.blocks:
            weights.append([(got[i], other[i]) for i in range(2)])
        else:
            ready = []
            for i in range(2):
                w = jnp.concatenate([got[i], other[i]])
                at = jnp.zeros(n_dp, jnp.int32).at[jnp.array(orders[i])].set(jnp.arange(n_dp))
                w = w[at[jnp.arange(n_dp) ^ me]]
                ready.append(w.reshape(sz.width, sz.hidden))
            weights.append(jnp.stack(ready))
    if not sz.blocks:
        weights = jnp.stack(weights, axis=1)

    bias_hi = cross_bias.astype(BF)
    bias_lo = (cross_bias - bias_hi.astype(F32)).astype(BF)
    wc = jnp.concatenate([crosspatch_weight, bias_hi[:, :, None], bias_lo[:, :, None]], axis=2)
    wc = jnp.pad(wc, ((0, 0), (0, sz.rows - patches), (0, sz.depth - patches - 2)))
    keep = jnp.pad(masks.astype(F32)[:, None, :], ((0, 0), (0, 0), (0, sz.depth - patches)))
    common = {
        "tok": tokens.transpose(1, 0, 2),
        "cot": cotangent.transpose(1, 0, 2),
        "keep": keep,
        "scale": aff_scale,
        "shift": aff_shift,
        "ls": layer_scale,
        "wc": wc,
        "b1": fc1_bias[:, None, :],
        "b2": fc2_bias[:, None, :],
    }
    exchanges = exchange_orders(n_dp)
    places = [me ^ k for k in orders[0] + orders[1]]
    places += [me ^ k for k in exchanges[0][1] + exchanges[1][1]]

    def meta(first, column):
        return jnp.stack([first, column, half, 1 - half] + places).astype(jnp.int32)

    first = run(sz, True, meta(half, hid // 2), common, weights)
    sent_out = swap(first["out"], "hid", 1)
    sent_grad = swap(first["tgrad"], "hid", 1)
    sent_small = swap(first["send"], "hid", 1)

    def by_owner(blocks):
        if sz.blocks:
            return blocks
        return jnp.moveaxis(blocks.reshape(layers, n_dp, sz.shard, sz.own), 1, 0)

    theirs = jnp.stack([by_owner(first[f"blocks{i}"]) for i in range(2)], axis=1)
    theirs = lax.all_to_all(theirs, "dp", split_axis=0, concat_axis=0, tiled=True)
    theirs = theirs.astype(F32).sum(axis=0).astype(BF)

    rest = run(sz, False, meta(jnp.int32(2), hid), common, weights, first["own"])
    gw = [by_owner(rest[f"blocks{i}"]) for i in range(2)]
    theirs, gw, small_rest = lax.optimization_barrier((theirs, gw, rest["small"]))
    theirs = swap(theirs, "hid", 1)
    if not sz.blocks:
        gw = [gw[i][jnp.array(exchanges[i][1]) ^ me] for i in range(2)]
    alone_small = first["small"].astype(F32) + sent_small.astype(F32)
    small = (alone_small + small_rest.astype(F32)).astype(BF)
    small = [small[l] for l in range(layers)]
    for k in range(len(exchanges[0][0])):
        gw = [scatter_step(gw[i], exchanges[i][0][k]) for i in range(2)]
        for l in range(layers):
            other = swap(small[l].astype(BF), "dp", exchanges[l % 2][0][k])
            small[l] = small[l].astype(BF).astype(F32) + other.astype(F32)
        if k == 0:
            gw, small, sent_out, sent_grad = lax.optimization_barrier(
                (gw, small, sent_out, sent_grad)
            )
    gw = [gw[i][0] + theirs[i].astype(F32) for i in range(2)]
    small = jnp.stack(small)
    gwc = small[:, :patches, :patches]
    sums = jnp.concatenate(
        [small[:, sz.rows : sz.rows + 8], small[:, sz.rows + 8 :, : sz.width - 256]], axis=2
    )

    def put(all_images, mine, theirs):
        all_images = lax.dynamic_update_slice_in_dim(all_images, mine, half * GROUP, axis=1)
        all_images = lax.dynamic_update_slice_in_dim(
            all_images, theirs, (1 - half) * GROUP, axis=1
        )
        return all_images.transpose(1, 0, 2)

    return (
        put(rest["out"], first["out"], sent_out),
        put(rest["tgrad"], first["tgrad"], sent_grad),
        jnp.stack([sums[:, S0], sums[:, S1]], axis=1),
        jnp.stack([sums[:, T0], sums[:, T1]], axis=1),
        jnp.stack([sums[:, LS0], sums[:, LS1]], axis=1),
        gwc,
        small[:, :patches, patches],
        gw[0],
        sums[:, B1],
        gw[1],
        sums[:, B2],
    )


def solution(mesh):
    return jax.shard_map(
        on_device,
        mesh=mesh,
        in_specs=(
            P("dp", None, None),
            P("dp", None),
            P("dp", None, None),
            P(),
            P(),
            P(),
            P(),
            P(),
            P(None, "dp", "hid"),
            P(),
            P(None, "dp", "hid"),
            P(),
        ),
        out_specs=(
            P("dp", None, None),
            P("dp", None, None),
            P(),
            P(),
            P(),
            P(),
            P(),
            P(None, "dp", "hid"),
            P(None, "hid"),
            P(None, "dp", "hid"),
            P(),
        ),
        check_vma=False,
    )
```

profile of v0, /device:TPU:0, one launch (start us, length us, event | category | flops | bytes accessed | tf_op | source)
XLA Modules:
  0.0 175.2 jit_solution(15230955657170250899)
XLA Ops:
  0.6 0.8 fusion.25
  1.5 4.1 %collective-permute-start.10 = (bf16[2,48,384]{2,1,0:T(8,128)(2,1)S(1)}, bf16[2,48,384]{2,1,0:T(8,128)(2,1)S(1)}, u32[]{:S(2)}, u32[]{:S(2)}) collective-permute-start(bf16[2,48,384]{2,1,0:T(8,128)(2,1)S(1)} %pad_maximum_fusion.13), channel_id=1, source_target_pairs={{0,2},{1,3},{2,0},{3,1},{4,6},{5,7},{6,4},{7,5},{8,10},{9,11},{10,... | collective-permute-start | bytes 221192 | tf_op jit(solution)/shard_map/ppermute | solution.py:339
  5.6 1.6 collective-permute-start.11
  7.2 3.9 %collective-permute-start = (bf16[2,48,384]{2,1,0:T(8,128)(2,1)S(1)}, bf16[2,48,384]{2,1,0:T(8,128)(2,1)S(1)}, u32[]{:S(2)}, u32[]{:S(2)}) collective-permute-start(bf16[2,48,384]{2,1,0:T(8,128)(2,1)S(1)} %pad_maximum_fusion.12), channel_id=1, source_target_pairs={{0,3},{1,2},{2,1},{3,0},{4,7},{5,6},{6,5},{7,4},{8,11},{9,10},{10,... | collective-permute-start | bytes 221192 | tf_op jit(solution)/shard_map/ppermute | solution.py:339
  11.1 0.6 collective-permute-start.2
  11.7 2.4 %collective-permute-done.9 = bf16[2,48,384]{2,1,0:T(8,128)(2,1)S(1)} collective-permute-done((bf16[2,48,384]{2,1,0:T(8,128)(2,1)S(1)}, bf16[2,48,384]{2,1,0:T(8,128)(2,1)S(1)}, u32[]{:S(2)}, u32[]{:S(2)}) %collective-permute-start.9) | collective-permute-done | bytes 73760 | tf_op jit(solution)/shard_map/ppermute | solution.py:339
  14.2 1.6 collective-permute-start.15
  15.8 1.5 collective-permute-start.12
  17.3 1.7 collective-permute-done.1
  19.1 1.8 %collective-permute-start.6 = (bf16[1,48,1536]{2,1,0:T(8,128)(2,1)S(1)}, bf16[1,48,1536]{2,1,0:T(8,128)(2,1)S(1)}, u32[]{:S(2)}, u32[]{:S(2)}) collective-permute-start(bf16[1,48,1536]{2,1,0:T(8,128)(2,1)S(1)} %get-tuple-element.114), channel_id=1, source_target_pairs={{0,16},{4,20},{8,24},{12,28},{16,0},{20,4},{24,8},{28,12},{1,17},{... | collective-permute-start | bytes 442376 | tf_op jit(solution)/shard_map/ppermute | solution.py:339
  20.9 1.5 collective-permute-start.3
  23.5 1.7 collective-permute-done.6
  25.2 1.7 collective-permute-start.7
  26.9 0.8 collective-permute-done.3
  27.8 1.6 collective-permute-start.4
  29.3 4.7 %collective-permute-done.16 = bf16[2,48,1536]{2,1,0:T(8,128)(2,1)S(1)} collective-permute-done((bf16[2,48,1536]{2,1,0:T(8,128)(2,1)S(1)}, bf16[2,48,1536]{2,1,0:T(8,128)(2,1)S(1)}, u32[]{:S(2)}, u32[]{:S(2)}) %collective-permute-start.16) | collective-permute-done | bytes 294944 | tf_op jit(solution)/shard_map/ppermute | solution.py:339
  34.8 3.1 %collective-permute-done.7 = bf16[2,48,1536]{2,1,0:T(8,128)(2,1)S(1)} collective-permute-done((bf16[2,48,1536]{2,1,0:T(8,128)(2,1)S(1)}, bf16[2,48,1536]{2,1,0:T(8,128)(2,1)S(1)}, u32[]{:S(2)}, u32[]{:S(2)}) %collective-permute-start.7) | collective-permute-done | bytes 294944 | tf_op jit(solution)/shard_map/ppermute | solution.py:339
  40.3 0.6 pad.8.args_3_
  41.0 0.7 stack.65.args_0_
  41.7 0.6 stack.61.args_0_
  42.3 0.8 fusion.9.args_7_
  43.2 45.8 %shard_map.203 = (bf16[196,8,384]{2,1,0:T(8,128)(2,1)}, bf16[196,8,384]{2,1,0:T(8,128)(2,1)}, bf16[2,216,256]{2,1,0:T(8,128)(2,1)}, bf16[8,2,48,384]{3,2,1,0:T(8...) custom-call(s32[36]{0:T(128)} %stack.65.args_0_, ...), custom_call_target="tpu_custom_call" | custom-call | flops 22649241600 | bytes 56623104 | tf_op jit(solution)/shard_map/pallas_call | solution.py:321
  89.0 1.4 pad_maximum_fusion
  90.4 1.2 copy.36
  91.5 3.8 %all-to-all-start = ((bf16[8,2,2,48,384]{4,3,2,1,0:T(8,128)(2,1)}), bf16[8,2,2,48,384]{4,3,2,1,0:T(8,128)(2,1)S(1)}, u32[]{:S(2)}, u32[]{:S(2)}) async-start(bf16[8,2,2,48,384]{4,3,2,1,0:T(8,128)(2,1)} %copy.36), calls=%async_computation | async-start | bytes 2359296 | tf_op jit(solution)/shard_map/all_to_all | solution.py:459
  95.3 2.4 %collective-permute-start.20 = (bf16[2,216,256]{2,1,0:T(8,128)(2,1)}, bf16[2,216,256]{2,1,0:T(8,128)(2,1)S(1)}, u32[]{:S(2)}, u32[]{:S(2)}) collective-permute-start(bf16[2,216,256]{2,1,0:T(8,128)(2,1)} %get-tuple-element.44), channel_id=1, source_target_pairs={{0,1},{1,0},{2,3},{3,2},{4,5},{5,4},{6,7},{7,6},{8,9},{9,8},{10,11... | collective-permute-start | bytes 663560 | tf_op jit(solution)/shard_map/ppermute | solution.py:339
  97.8 1.9 %collective-permute-start.24 = (bf16[196,8,384]{2,1,0:T(8,128)(2,1)}, bf16[196,8,384]{2,1,0:T(8,128)(2,1)}, u32[]{:S(2)}, u32[]{:S(2)}) collective-permute-start(bf16[196,8,384]{2,1,0:T(8,128)(2,1)} %get-tuple-element.46), channel_id=1, source_target_pairs={{0,1},{1,0},{2,3},{3,2},{4,5},{5,4},{6,7},{7,6},{8,9},{9,8},{10,11... | collective-permute-start | bytes 3612680 | tf_op jit(solution)/shard_map/ppermute | solution.py:339
  99.8 42.5 %shard_map.204 = (bf16[196,24,384]{2,1,0:T(8,128)(2,1)}, bf16[196,24,384]{2,1,0:T(8,128)(2,1)}, bf16[2,216,256]{2,1,0:T(8,128)(2,1)}, bf16[8,2,48,384]{3,2,1,0:T(8,128)(2,1)}, bf16[8,2,48,384]{3,2,1,0:T(8,128)(2,1)}) custom-call(s32[36]{0:T(128)} %stack.61.args_0_, bf16[196,24,384]{2,1,0:T(8,128)(2,1)} %bitcast.49, bf16[196,24,384]{2,1,0:T(8,128)(2,1)} %bitcast.51, ...), custom_call_target="tpu_custom_call" | custom-call | flops 22649241600 | bytes 56623104 | tf_op jit(solution)/shard_map/pallas_call | solution.py:321
  142.3 2.5 %constant_dynamic-update-slice_fusion.1 = bf16[196,24,384]{2,1,0:T(8,128)(2,1)} fusion(bf16[196,24,384]{2,1,0:T(8,128)(2,1)} %get-tuple-element.48, bf16[196,8,384]{2,1,0:T(8,128)(2,1)} %get-tuple-element.46, s32[]{:T(128)S(6)} %select_n.152), kind=kLoop, calls=%fused_computation.86 | loop fusion | bytes 2408452 | tf_op jit(solution)/shard_map/dynamic_update_slice | solution.py:488
  144.8 0.8 reduce_sum.12
  145.6 0.7 copy-done.7
  146.3 1.1 add_convert_fusion
  148.0 1.0 slice.120
  149.2 2.4 %constant_dynamic-update-slice_fusion.3 = bf16[196,24,384]{2,1,0:T(8,128)(2,1)} fusion(bf16[196,24,384]{2,1,0:T(8,128)(2,1)} %get-tuple-element.34, bf16[196,8,384]{2,1,0:T(8,128)(2,1)} %get-tuple-element.35, s32[]{:T(128)S(6)} %select_n.152), kind=kLoop, calls=%fused_computation.88 | loop fusion | bytes 2408452 | tf_op jit(solution)/shard_map/dynamic_update_slice | solution.py:488
  152.4 0.9 collective-permute-done.18
  153.4 2.3 %collective-permute-done.24 = bf16[196,8,384]{2,1,0:T(8,128)(2,1)} collective-permute-done((bf16[196,8,384]{2,1,0:T(8,128)(2,1)}, bf16[196,8,384]{2,1,0:T(8,128)(2,1)}, u32[]{:S(2)}, u32[]{:S(2)}) %collective-permute-start.24) | collective-permute-done | bytes 1204256 | tf_op jit(solution)/shard_map/ppermute | solution.py:339
  155.7 1.7 collective-permute-start.25
  157.4 1.5 collective-permute-start.27
  158.9 0.6 collective-permute-start.29
  160.0 2.4 %constant_dynamic-update-slice_fusion = bf16[196,24,384]{2,1,0:T(8,128)(2,1)} fusion(bf16[196,24,384]{2,1,0:T(8,128)(2,1)} %constant_dynamic-update-slice_fusion.1, bf16[196,8,384]{2,1,0:T(8,128)(2,1)} %collective-permute-done.24, s32[]{:T(128)S(6)} %select_n.153), kind=kLoop, calls=%fused_computation.85 | loop fusion | bytes 2408452 | tf_op jit(solution)/shard_map/dynamic_update_slice | solution.py:489
  162.4 1.1 constant_dynamic-update-slice_fusion.2
  163.6 1.8 %collective-permute-start.26 = (bf16[216,256]{1,0:T(8,128)(2,1)S(1)}, bf16[216,256]{1,0:T(8,128)(2,1)S(1)}, u32[]{:S(2)}, u32[]{:S(2)}) collective-permute-start(bf16[216,256]{1,0:T(8,128)(2,1)S(1)} %add_convert_fusion.2), channel_id=1, source_target_pairs={{0,16},{4,20},{8,24},{12,28},{16,0},{20,4},{24,8},{28,12},{1,17},{... | collective-permute-start | bytes 331784 | tf_op jit(solution)/shard_map/ppermute | solution.py:339
  165.4 1.5 collective-permute-start.28
  168.0 1.1 collective-permute-done.26
  169.2 1.0 collective-permute-done.28
  172.6 1.0 copy.37
  173.6 0.8 fusion.10
  174.4 0.8 fusion.12
  (114 shorter events, 10.2 us)
Async XLA Ops:
  1.5 9.6 %collective-permute-start.10 = (bf16[2,48,384]{2,1,0:T(8,128)(2,1)S(1)}, bf16[2,48,384]{2,1,0:T(8,128)(2,1)S(1)}, u32[]{:S(2)}, u32[]{:S(2)}) collective-permute-start(bf16[2,48,384]{2,1,0:T(8,128)(2,1)S(1)} %pad_maximum_fusion.13), channel_id=1, source_target_pairs={{0,2},{1,3},{2,0},{3,1},{4,6},{5,7},{6,4},{7,5},{8,10},{9,11},{10,... | collective-permute-start | bytes 221192 | tf_op jit(solution)/shard_map/ppermute | solution.py:339
  5.6 6.1 %collective-permute-start.11 = (bf16[2,48,384]{2,1,0:T(8,128)(2,1)S(1)}, bf16[2,48,384]{2,1,0:T(8,128)(2,1)S(1)}, u32[]{:S(2)}, u32[]{:S(2)}) collective-permute-start(bf16[2,48,384]{2,1,0:T(8,128)(2,1)S(1)} %pad_maximum_fusion.13), channel_id=1, source_target_pairs={{0,1},{1,0},{2,3},{3,2},{4,5},{5,4},{6,7},{7,6},{8,9},{9,8},{10,11... | collective-permute-start | bytes 221192 | tf_op jit(solution)/shard_map/ppermute | solution.py:339
  7.2 6.9 %collective-permute-start.9 = (bf16[2,48,384]{2,1,0:T(8,128)(2,1)S(1)}, bf16[2,48,384]{2,1,0:T(8,128)(2,1)S(1)}, u32[]{:S(2)}, u32[]{:S(2)}) collective-permute-start(bf16[2,48,384]{2,1,0:T(8,128)(2,1)S(1)} %pad_maximum_fusion.13), channel_id=1, source_target_pairs={{0,3},{1,2},{2,1},{3,0},{4,7},{5,6},{6,5},{7,4},{8,11},{9,10},{10,... | collective-permute-start | bytes 221192 | tf_op jit(solution)/shard_map/ppermute | solution.py:339
  7.2 10.1 %collective-permute-start = (bf16[2,48,384]{2,1,0:T(8,128)(2,1)S(1)}, bf16[2,48,384]{2,1,0:T(8,128)(2,1)S(1)}, u32[]{:S(2)}, u32[]{:S(2)}) collective-permute-start(bf16[2,48,384]{2,1,0:T(8,128)(2,1)S(1)} %pad_maximum_fusion.12), channel_id=1, source_target_pairs={{0,3},{1,2},{2,1},{3,0},{4,7},{5,6},{6,5},{7,4},{8,11},{9,10},{10,... | collective-permute-start | bytes 221192 | tf_op jit(solution)/shard_map/ppermute | solution.py:339
  11.1 7.9 %collective-permute-start.1 = (bf16[2,48,384]{2,1,0:T(8,128)(2,1)S(1)}, bf16[2,48,384]{2,1,0:T(8,128)(2,1)S(1)}, u32[]{:S(2)}, u32[]{:S(2)}) collective-permute-start(bf16[2,48,384]{2,1,0:T(8,128)(2,1)S(1)} %pad_maximum_fusion.12), channel_id=1, source_target_pairs={{0,2},{1,3},{2,0},{3,1},{4,6},{5,7},{6,4},{7,5},{8,10},{9,11},{10,... | collective-permute-start | bytes 221192 | tf_op jit(solution)/shard_map/ppermute | solution.py:339
  11.1 7.9 %collective-permute-start.2 = (bf16[2,48,384]{2,1,0:T(8,128)(2,1)S(1)}, bf16[2,48,384]{2,1,0:T(8,128)(2,1)S(1)}, u32[]{:S(2)}, u32[]{:S(2)}) collective-permute-start(bf16[2,48,384]{2,1,0:T(8,128)(2,1)S(1)} %pad_maximum_fusion.12), channel_id=1, source_target_pairs={{0,1},{1,0},{2,3},{3,2},{4,5},{5,4},{6,7},{7,6},{8,9},{9,8},{10,11... | collective-permute-start | bytes 221192 | tf_op jit(solution)/shard_map/ppermute | solution.py:339
  14.2 8.2 %collective-permute-start.15 = (bf16[1,48,1536]{2,1,0:T(8,128)(2,1)S(1)}, bf16[1,48,1536]{2,1,0:T(8,128)(2,1)S(1)}, u32[]{:S(2)}, u32[]{:S(2)}) collective-permute-start(bf16[1,48,1536]{2,1,0:T(8,128)(2,1)S(1)} %get-tuple-element.108), channel_id=1, source_target_pairs={{0,16},{4,20},{8,24},{12,28},{16,0},{20,4},{24,8},{28,12},{1,17},{... | collective-permute-start | bytes 442376 | tf_op jit(solution)/shard_map/ppermute | solution.py:339
  15.8 7.3 %collective-permute-start.12 = (bf16[1,48,1536]{2,1,0:T(8,128)(2,1)S(1)}, bf16[1,48,1536]{2,1,0:T(8,128)(2,1)S(1)}, u32[]{:S(2)}, u32[]{:S(2)}) collective-permute-start(bf16[1,48,1536]{2,1,0:T(8,128)(2,1)S(1)} %get-tuple-element.109), channel_id=1, source_target_pairs={{0,8},{4,12},{8,0},{12,4},{16,24},{20,28},{24,16},{28,20},{1,9},{5... | collective-permute-start | bytes 442376 | tf_op jit(solution)/shard_map/ppermute | solution.py:339
  19.1 19.6 %copy-start.13 = (f32[2,196]{1,0:T(2,128)S(1)}, f32[2,196]{1,0:T(2,128)}, u32[]{:S(2)}) copy-start(f32[2,196]{1,0:T(2,128)} %param.19) | copy-start | bytes 4708
  19.1 6.0 %collective-permute-start.6 = (bf16[1,48,1536]{2,1,0:T(8,128)(2,1)S(1)}, bf16[1,48,1536]{2,1,0:T(8,128)(2,1)S(1)}, u32[]{:S(2)}, u32[]{:S(2)}) collective-permute-start(bf16[1,48,1536]{2,1,0:T(8,128)(2,1)S(1)} %get-tuple-element.114), channel_id=1, source_target_pairs={{0,16},{4,20},{8,24},{12,28},{16,0},{20,4},{24,8},{28,12},{1,17},{... | collective-permute-start | bytes 442376 | tf_op jit(solution)/shard_map/ppermute | solution.py:339
  20.9 18.1 %copy-start.8 = (bf16[2,196,196]{2,0,1:T(2,128)(2,1)S(1)}, bf16[2,196,196]{2,0,1:T(2,128)(2,1)}, u32[]{:S(2)}) copy-start(bf16[2,196,196]{2,0,1:T(2,128)(2,1)} %param.18) | copy-start | bytes 460996
  20.9 6.8 %collective-permute-start.3 = (bf16[1,48,1536]{2,1,0:T(8,128)(2,1)S(1)}, bf16[1,48,1536]{2,1,0:T(8,128)(2,1)S(1)}, u32[]{:S(2)}, u32[]{:S(2)}) collective-permute-start(bf16[1,48,1536]{2,1,0:T(8,128)(2,1)S(1)} %get-tuple-element.115), channel_id=1, source_target_pairs={{0,8},{4,12},{8,0},{12,4},{16,24},{20,28},{24,16},{28,20},{1,9},{5... | collective-permute-start | bytes 442376 | tf_op jit(solution)/shard_map/ppermute | solution.py:339
  22.5 16.6 %copy-start.10 = (s32[24,196]{1,0:T(8,128)S(1)}, s32[24,196]{1,0:T(8,128)}, u32[]{:S(2)}) copy-start(s32[24,196]{1,0:T(8,128)} %param.13) | copy-start | bytes 56452
  22.5 16.7 %copy-start.11 = (f32[2,1536]{1,0:T(2,128)S(1)}, f32[2,1536]{1,0:T(2,128)}, u32[]{:S(2)}) copy-start(f32[2,1536]{1,0:T(2,128)} %param.21) | copy-start | bytes 36868
  22.5 17.3 %copy-start.12 = (f32[2,384]{1,0:T(2,128)S(1)}, f32[2,384]{1,0:T(2,128)}, u32[]{:S(2)}) copy-start(f32[2,384]{1,0:T(2,128)} %param.23) | copy-start | bytes 9220
  22.5 11.5 %collective-permute-start.16 = (bf16[2,48,1536]{2,1,0:T(8,128)(2,1)S(1)}, bf16[2,48,1536]{2,1,0:T(8,128)(2,1)S(1)}, u32[]{:S(2)}, u32[]{:S(2)}) collective-permute-start(bf16[2,48,1536]{2,1,0:T(8,128)(2,1)S(1)} %pad_maximum_fusion.10), channel_id=1, source_target_pairs={{0,8},{4,12},{8,0},{12,4},{16,24},{20,28},{24,16},{28,20},{1,9},{5... | collective-permute-start | bytes 884744 | tf_op jit(solution)/shard_map/ppermute | solution.py:339
  23.1 11.1 %collective-permute-start.13 = (bf16[2,48,1536]{2,1,0:T(8,128)(2,1)S(1)}, bf16[2,48,1536]{2,1,0:T(8,128)(2,1)S(1)}, u32[]{:S(2)}, u32[]{:S(2)}) collective-permute-start(bf16[2,48,1536]{2,1,0:T(8,128)(2,1)S(1)} %pad_maximum_fusion.9), channel_id=1, source_target_pairs={{0,16},{4,20},{8,24},{12,28},{16,0},{20,4},{24,8},{28,12},{1,17},{... | collective-permute-start | bytes 884744 | tf_op jit(solution)/shard_map/ppermute | solution.py:339
  25.2 12.7 %collective-permute-start.7 = (bf16[2,48,1536]{2,1,0:T(8,128)(2,1)S(1)}, bf16[2,48,1536]{2,1,0:T(8,128)(2,1)S(1)}, u32[]{:S(2)}, u32[]{:S(2)}) collective-permute-start(bf16[2,48,1536]{2,1,0:T(8,128)(2,1)S(1)} %pad_maximum_fusion.7), channel_id=1, source_target_pairs={{0,8},{4,12},{8,0},{12,4},{16,24},{20,28},{24,16},{28,20},{1,9},{5... | collective-permute-start | bytes 884744 | tf_op jit(solution)/shard_map/ppermute | solution.py:339
  27.8 10.3 %collective-permute-start.4 = (bf16[2,48,1536]{2,1,0:T(8,128)(2,1)S(1)}, bf16[2,48,1536]{2,1,0:T(8,128)(2,1)S(1)}, u32[]{:S(2)}, u32[]{:S(2)}) collective-permute-start(bf16[2,48,1536]{2,1,0:T(8,128)(2,1)S(1)} %pad_maximum_fusion.6), channel_id=1, source_target_pairs={{0,16},{4,20},{8,24},{12,28},{16,0},{20,4},{24,8},{28,12},{1,17},{... | collective-permute-start | bytes 884744 | tf_op jit(solution)/shard_map/ppermute | solution.py:339
  34.1 9.1 %copy-start = (bf16[4,48,1536]{2,1,0:T(8,128)(2,1)}, bf16[4,48,1536]{2,1,0:T(8,128)(2,1)S(1)}, u32[]{:S(2)}) copy-start(bf16[4,48,1536]{2,1,0:T(8,128)(2,1)S(1)} %pad_maximum_fusion.4.args_16_) | copy-start | bytes 1769476
  34.1 9.0 %collective-permute-start.17 = (bf16[4,48,1536]{2,1,0:T(8,128)(2,1)S(1)}, bf16[4,48,1536]{2,1,0:T(8,128)(2,1)}, u32[]{:S(2)}, u32[]{:S(2)}) collective-permute-start(bf16[4,48,1536]{2,1,0:T(8,128)(2,1)S(1)} %pad_maximum_fusion.4.args_16_), channel_id=1, source_target_pairs={{0,4},{4,0},{8,12},{12,8},{16,20},{20,16},{24,28},{28,24},{1,5},{5... | collective-permute-start | bytes 1769480 | tf_op jit(solution)/shard_map/ppermute | solution.py:339
  34.3 8.9 %copy-start.1 = (bf16[4,48,1536]{2,1,0:T(8,128)(2,1)}, bf16[4,48,1536]{2,1,0:T(8,128)(2,1)S(1)}, u32[]{:S(2)}) copy-start(bf16[4,48,1536]{2,1,0:T(8,128)(2,1)S(1)} %pad_maximum_fusion.3.args_14_) | copy-start | bytes 1769476
  34.3 8.9 %collective-permute-start.14 = (bf16[4,48,1536]{2,1,0:T(8,128)(2,1)S(1)}, bf16[4,48,1536]{2,1,0:T(8,128)(2,1)}, u32[]{:S(2)}, u32[]{:S(2)}) collective-permute-start(bf16[4,48,1536]{2,1,0:T(8,128)(2,1)S(1)} %pad_maximum_fusion.3.args_14_), channel_id=1, source_target_pairs={{0,4},{4,0},{8,12},{12,8},{16,20},{20,16},{24,28},{28,24},{1,5},{5... | collective-permute-start | bytes 1769480 | tf_op jit(solution)/shard_map/ppermute | solution.py:339
  38.0 5.2 %copy-start.2 = (bf16[4,48,1536]{2,1,0:T(8,128)(2,1)}, bf16[4,48,1536]{2,1,0:T(8,128)(2,1)S(1)}, u32[]{:S(2)}) copy-start(bf16[4,48,1536]{2,1,0:T(8,128)(2,1)S(1)} %pad_maximum_fusion.2.args_12_) | copy-start | bytes 1769476
  38.0 5.2 %collective-permute-start.8 = (bf16[4,48,1536]{2,1,0:T(8,128)(2,1)S(1)}, bf16[4,48,1536]{2,1,0:T(8,128)(2,1)}, u32[]{:S(2)}, u32[]{:S(2)}) collective-permute-start(bf16[4,48,1536]{2,1,0:T(8,128)(2,1)S(1)} %pad_maximum_fusion.2.args_12_), channel_id=1, source_target_pairs={{0,4},{4,0},{8,12},{12,8},{16,20},{20,16},{24,28},{28,24},{1,5},{5... | collective-permute-start | bytes 1769480 | tf_op jit(solution)/shard_map/ppermute | solution.py:339
  38.1 5.1 %copy-start.3 = (bf16[4,48,1536]{2,1,0:T(8,128)(2,1)}, bf16[4,48,1536]{2,1,0:T(8,128)(2,1)S(1)}, u32[]{:S(2)}) copy-start(bf16[4,48,1536]{2,1,0:T(8,128)(2,1)S(1)} %pad_maximum_fusion.1.args_10_) | copy-start | bytes 1769476
  38.1 5.0 %collective-permute-start.5 = (bf16[4,48,1536]{2,1,0:T(8,128)(2,1)S(1)}, bf16[4,48,1536]{2,1,0:T(8,128)(2,1)}, u32[]{:S(2)}, u32[]{:S(2)}) collective-permute-start(bf16[4,48,1536]{2,1,0:T(8,128)(2,1)S(1)} %pad_maximum_fusion.1.args_10_), channel_id=1, source_target_pairs={{0,4},{4,0},{8,12},{12,8},{16,20},{20,16},{24,28},{28,24},{1,5},{5... | collective-permute-start | bytes 1769480 | tf_op jit(solution)/shard_map/ppermute | solution.py:339
  91.5 53.2 %all-to-all-start = ((bf16[8,2,2,48,384]{4,3,2,1,0:T(8,128)(2,1)}), bf16[8,2,2,48,384]{4,3,2,1,0:T(8,128)(2,1)S(1)}, u32[]{:S(2)}, u32[]{:S(2)}) async-start(bf16[8,2,2,48,384]{4,3,2,1,0:T(8,128)(2,1)} %copy.36), calls=%async_computation | async-start | bytes 2359296 | tf_op jit(solution)/shard_map/all_to_all | solution.py:459
  95.3 50.3 %collective-permute-start.20 = (bf16[2,216,256]{2,1,0:T(8,128)(2,1)}, bf16[2,216,256]{2,1,0:T(8,128)(2,1)S(1)}, u32[]{:S(2)}, u32[]{:S(2)}) collective-permute-start(bf16[2,216,256]{2,1,0:T(8,128)(2,1)} %get-tuple-element.44), channel_id=1, source_target_pairs={{0,1},{1,0},{2,3},{3,2},{4,5},{5,4},{6,7},{7,6},{8,9},{9,8},{10,11... | collective-permute-start | bytes 663560 | tf_op jit(solution)/shard_map/ppermute | solution.py:339
  97.7 55.7 %collective-permute-start.23 = (bf16[196,8,384]{2,1,0:T(8,128)(2,1)}, bf16[196,8,384]{2,1,0:T(8,128)(2,1)S(1)}, u32[]{:S(2)}, u32[]{:S(2)}) collective-permute-start(bf16[196,8,384]{2,1,0:T(8,128)(2,1)} %get-tuple-element.35), channel_id=1, source_target_pairs={{0,1},{1,0},{2,3},{3,2},{4,5},{5,4},{6,7},{7,6},{8,9},{9,8},{10,11... | collective-permute-start | bytes 3612680 | tf_op jit(solution)/shard_map/ppermute | solution.py:339
  97.8 57.9 %collective-permute-start.24 = (bf16[196,8,384]{2,1,0:T(8,128)(2,1)}, bf16[196,8,384]{2,1,0:T(8,128)(2,1)}, u32[]{:S(2)}, u32[]{:S(2)}) collective-permute-start(bf16[196,8,384]{2,1,0:T(8,128)(2,1)} %get-tuple-element.46), channel_id=1, source_target_pairs={{0,1},{1,0},{2,3},{3,2},{4,5},{5,4},{6,7},{7,6},{8,9},{9,8},{10,11... | collective-permute-start | bytes 3612680 | tf_op jit(solution)/shard_map/ppermute | solution.py:339
  142.2 4.1 %copy-start.6 = (bf16[2,216,256]{2,1,0:T(8,128)(2,1)S(1)}, bf16[2,216,256]{2,1,0:T(8,128)(2,1)}, u32[]{:S(2)}) copy-start(bf16[2,216,256]{2,1,0:T(8,128)(2,1)} %get-tuple-element.43) | copy-start | bytes 663556
  142.2 9.4 %copy-start.4 = (bf16[8,2,48,384]{3,2,1,0:T(8,128)(2,1)S(1)}, bf16[8,2,48,384]{3,2,1,0:T(8,128)(2,1)}, u32[]{:S(2)}) copy-start(bf16[8,2,48,384]{3,2,1,0:T(8,128)(2,1)} %get-tuple-element.41) | copy-start | bytes 1769476
  145.6 6.6 %copy-start.9 = (bf16[2,2,48,384]{3,2,1,0:T(8,128)(2,1)S(1)}, bf16[2,2,48,384]{3,2,1,0:T(8,128)(2,1)}, u32[]{:S(2)}) copy-start(bf16[2,2,48,384]{3,2,1,0:T(8,128)(2,1)} %reduce_sum.12) | copy-start | bytes 442372
  145.6 6.8 %copy-start.5 = (bf16[8,2,48,384]{3,2,1,0:T(8,128)(2,1)S(1)}, bf16[8,2,48,384]{3,2,1,0:T(8,128)(2,1)}, u32[]{:S(2)}) copy-start(bf16[8,2,48,384]{3,2,1,0:T(8,128)(2,1)} %get-tuple-element.42) | copy-start | bytes 1769476
  147.5 4.2 %collective-permute-start.21 = (bf16[216,256]{1,0:T(8,128)(2,1)S(1)}, bf16[216,256]{1,0:T(8,128)(2,1)S(1)}, u32[]{:S(2)}, u32[]{:S(2)}) collective-permute-start(bf16[216,256]{1,0:T(8,128)(2,1)S(1)} %get-tuple-element.123), channel_id=1, source_target_pairs={{0,4},{4,0},{8,12},{12,8},{16,20},{20,16},{24,28},{28,24},{1,5},{5... | collective-permute-start | bytes 331784 | tf_op jit(solution)/shard_map/ppermute | solution.py:339
  147.6 4.6 %collective-permute-start.22 = (bf16[216,256]{1,0:T(8,128)(2,1)S(1)}, bf16[216,256]{1,0:T(8,128)(2,1)S(1)}, u32[]{:S(2)}, u32[]{:S(2)}) collective-permute-start(bf16[216,256]{1,0:T(8,128)(2,1)S(1)} %get-tuple-element.122), channel_id=1, source_target_pairs={{0,4},{4,0},{8,12},{12,8},{16,20},{20,16},{24,28},{28,24},{1,5},{5... | collective-permute-start | bytes 331784 | tf_op jit(solution)/shard_map/ppermute | solution.py:339
  149.0 3.3 %collective-permute-start.19 = (bf16[4,2,48,384]{3,2,1,0:T(8,128)(2,1)S(1)}, bf16[4,2,48,384]{3,2,1,0:T(8,128)(2,1)S(1)}, u32[]{:S(2)}, u32[]{:S(2)}) collective-permute-start(bf16[4,2,48,384]{3,2,1,0:T(8,128)(2,1)S(1)} %slice.120), channel_id=1, source_target_pairs={{0,4},{4,0},{8,12},{12,8},{16,20},{20,16},{24,28},{28,24},{1,5},{5... | collective-permute-start | bytes 884744 | tf_op jit(solution)/shard_map/ppermute | solution.py:339
  151.7 1.7 collective-permute-start.18
  152.2 22.3 %collective-permute-start.31 = (bf16[2,2,48,384]{3,2,1,0:T(8,128)(2,1)S(1)}, bf16[2,2,48,384]{3,2,1,0:T(8,128)(2,1)S(1)}, u32[]{:S(2)}, u32[]{:S(2)}) collective-permute-start(bf16[2,2,48,384]{3,2,1,0:T(8,128)(2,1)S(1)} %copy-done.9), channel_id=1, source_target_pairs={{0,1},{1,0},{2,3},{3,2},{4,5},{5,4},{6,7},{7,6},{8,9},{9,8},{10,11... | collective-permute-start | bytes 442376 | tf_op jit(solution)/shard_map/ppermute | solution.py:339
  155.7 7.8 %collective-permute-start.25 = (bf16[216,256]{1,0:T(8,128)(2,1)S(1)}, bf16[216,256]{1,0:T(8,128)(2,1)S(1)}, u32[]{:S(2)}, u32[]{:S(2)}) collective-permute-start(bf16[216,256]{1,0:T(8,128)(2,1)S(1)} %get-tuple-element.50), channel_id=1, source_target_pairs={{0,8},{4,12},{8,0},{12,4},{16,24},{20,28},{24,16},{28,20},{1,9},{5... | collective-permute-start | bytes 331784 | tf_op jit(solution)/shard_map/ppermute | solution.py:339
  157.4 7.9 %collective-permute-start.27 = (bf16[216,256]{1,0:T(8,128)(2,1)S(1)}, bf16[216,256]{1,0:T(8,128)(2,1)S(1)}, u32[]{:S(2)}, u32[]{:S(2)}) collective-permute-start(bf16[216,256]{1,0:T(8,128)(2,1)S(1)} %get-tuple-element.51), channel_id=1, source_target_pairs={{0,16},{4,20},{8,24},{12,28},{16,0},{20,4},{24,8},{28,12},{1,17},{... | collective-permute-start | bytes 331784 | tf_op jit(solution)/shard_map/ppermute | solution.py:339
  158.9 8.0 %collective-permute-start.29 = (bf16[2,2,48,384]{3,2,1,0:T(8,128)(2,1)S(1)}, bf16[2,2,48,384]{3,2,1,0:T(8,128)(2,1)S(1)}, u32[]{:S(2)}, u32[]{:S(2)}) collective-permute-start(bf16[2,2,48,384]{3,2,1,0:T(8,128)(2,1)S(1)} %slice.196), channel_id=1, source_target_pairs={{0,8},{4,12},{8,0},{12,4},{16,24},{20,28},{24,16},{28,20},{1,9},{5... | collective-permute-start | bytes 442376 | tf_op jit(solution)/shard_map/ppermute | solution.py:339
  159.6 8.0 %collective-permute-start.32 = (bf16[2,2,48,384]{3,2,1,0:T(8,128)(2,1)S(1)}, bf16[2,2,48,384]{3,2,1,0:T(8,128)(2,1)S(1)}, u32[]{:S(2)}, u32[]{:S(2)}) collective-permute-start(bf16[2,2,48,384]{3,2,1,0:T(8,128)(2,1)S(1)} %slice.195), channel_id=1, source_target_pairs={{0,16},{4,20},{8,24},{12,28},{16,0},{20,4},{24,8},{28,12},{1,17},{... | collective-permute-start | bytes 442376 | tf_op jit(solution)/shard_map/ppermute | solution.py:339
  163.6 5.6 %collective-permute-start.26 = (bf16[216,256]{1,0:T(8,128)(2,1)S(1)}, bf16[216,256]{1,0:T(8,128)(2,1)S(1)}, u32[]{:S(2)}, u32[]{:S(2)}) collective-permute-start(bf16[216,256]{1,0:T(8,128)(2,1)S(1)} %add_convert_fusion.2), channel_id=1, source_target_pairs={{0,16},{4,20},{8,24},{12,28},{16,0},{20,4},{24,8},{28,12},{1,17},{... | collective-permute-start | bytes 331784 | tf_op jit(solution)/shard_map/ppermute | solution.py:339
  165.4 4.8 %collective-permute-start.28 = (bf16[216,256]{1,0:T(8,128)(2,1)S(1)}, bf16[216,256]{1,0:T(8,128)(2,1)S(1)}, u32[]{:S(2)}, u32[]{:S(2)}) collective-permute-start(bf16[216,256]{1,0:T(8,128)(2,1)S(1)} %add_convert_fusion.1), channel_id=1, source_target_pairs={{0,8},{4,12},{8,0},{12,4},{16,24},{20,28},{24,16},{28,20},{1,9},{5... | collective-permute-start | bytes 331784 | tf_op jit(solution)/shard_map/ppermute | solution.py:339
  167.0 7.5 %collective-permute-start.30 = (bf16[1,2,48,384]{3,2,1,0:T(8,128)(2,1)S(1)}, bf16[1,2,48,384]{3,2,1,0:T(8,128)(2,1)S(1)}, u32[]{:S(2)}, u32[]{:S(2)}) collective-permute-start(bf16[1,2,48,384]{3,2,1,0:T(8,128)(2,1)S(1)} %slice.198), channel_id=1, source_target_pairs={{0,16},{4,20},{8,24},{12,28},{16,0},{20,4},{24,8},{28,12},{1,17},{... | collective-permute-start | bytes 221192 | tf_op jit(solution)/shard_map/ppermute | solution.py:339
  167.6 6.8 %collective-permute-start.33 = (bf16[1,2,48,384]{3,2,1,0:T(8,128)(2,1)S(1)}, bf16[1,2,48,384]{3,2,1,0:T(8,128)(2,1)S(1)}, u32[]{:S(2)}, u32[]{:S(2)}) collective-permute-start(bf16[1,2,48,384]{3,2,1,0:T(8,128)(2,1)S(1)} %slice.197), channel_id=1, source_target_pairs={{0,8},{4,12},{8,0},{12,4},{16,24},{20,28},{24,16},{28,20},{1,9},{5... | collective-permute-start | bytes 221192 | tf_op jit(solution)/shard_map/ppermute | solution.py:339
  (1 other events, 0.7 us)
where the time goes:
time: 176 us; the launch traced here: 175 us
  Pallas kernels  88.2 us (50%)
  starting transfers between devices  40.1 us (23%)
  waiting for transfers between devices  19.7 us (11%)
  local copies, waits for them, and re-layouts  18 us (10%)
  other arithmetic  7.96 us (5%)
    pallas_call x2, Pallas kernels, run(): pl.pallas_call(functools.partial(kernel_body, sz, kept, names), grid_spec...  88.2 us
    ppermute x34, starting transfers between devices, swap(): return lax.ppermute(x, axis, [(i, i ^ k) for i in range(n)])  36.4 us
    ppermute x34, waiting for transfers between devices, swap(): return lax.ppermute(x, axis, [(i, i ^ k) for i in range(n)])  19.7 us
    dynamic_update_slice x2, local copies, waits for them, and re-layouts, put(): lax.dynamic_update_slice_in_dim(all_images, mine, half * GROUP, axis=1)  4.92 us
    all_to_all x1, starting transfers between devices, on_device(): lax.all_to_all(theirs, 'dp', split_axis=0, concat_axis=0, tiled=True)  3.78 us
    dynamic_update_slice x2, local copies, waits for them, and re-layouts, put(): lax.dynamic_update_slice_in_dim(all_images, theirs, (1 - half) * GROUP, a...  3.56 us
  transfers between devices with their start and end apart: 35, of which 10 were waited for; matrix products, arithmetic and copies ran while one was open for 12% of the time, Pallas kernels for 24%

commit v1 on v0

--- a/solution.py
+++ b/solution.py
@@ -14,6 +14,7 @@
 TN = (((0,), (0,)), ((), ()))
 SQRT_HALF = 0.7071067811865476
 PDF_SCALE = 0.3989422804014327
+HALF_LOG2E = -0.7213475204444817
 S0, T0, S1, T1, LS0, LS1, B2, B1 = range(8)
 STEP = 4
 GROUP = 8
@@ -56,6 +57,40 @@
     theirs = pl.ds(pl.multiple_of(meta[3] * sz.own, 128), sz.own)
     x, grad, gw = r["x"], r["grad"], r["gw"]
 
+    group = pl.ds(pl.multiple_of(meta[0] * GROUP, GROUP), GROUP)
+    buffers = {"tok": r["tokb"], "cot": r["cotb"]}
+
+    cut = patches // 2
+    results = (("out", "tok", 0, patches), ("tgrad", "cot", 0, cut), ("tgrad", "cot", cut, patches))
+
+    def deliver(i):
+        name, source, start, stop = results[i]
+        place = r[f"{name}{i}"] if alone else r[name].at[start:stop, group, :]
+        return pltpu.make_async_copy(buffers[source].at[start:stop], place, r["moved"].at[i])
+
+    def bring(i):
+        name, _, start, stop = results[i]
+        place = r["pass_" + name].at[start:stop]
+        return pltpu.make_async_copy(r[f"own_{name}{i}"], place, r["passed"].at[i])
+
+    def pass_on(i):
+        name, _, start, stop = results[i]
+        at = pl.ds(pl.multiple_of(meta[2] * GROUP, GROUP), GROUP)
+        source, place = r["pass_" + name].at[start:stop], r[name].at[start:stop, at, :]
+        return pltpu.make_async_copy(source, place, r["passed"].at[i])
+
+    def to_staging(name):
+        staged = r[name + "f"]
+        for c in range(sz.width // 128):
+            part = r[name][:, :, c * 128 : (c + 1) * 128].astype(F32)
+            staged[c, : patches * GROUP, :] = part.reshape(patches * GROUP, 128)
+            staged[c, patches * GROUP :, :] = jnp.zeros(((rows - patches) * GROUP, 128), F32)
+
+    def from_staging(name):
+        for c in range(sz.width // 128):
+            v = r[name + "f"][c, : patches * GROUP, :].reshape(patches, GROUP, 128)
+            buffers[name][:, :, c * 128 : (c + 1) * 128] = v.astype(BF)
+
     @pl.when(step == 0)
     def _():
         if sz.blocks:
@@ -70,18 +105,17 @@
                             pltpu.make_async_copy(
                                 src.at[k], r["w"].at[i, l, at], r["arrive"].at[i, l]
                             ).start()
-        for name in ("gwc", "gsum", "gb1"):
+        if not alone:
+            pltpu.make_async_copy(r["carry"], gw, r["carried"]).start()
+            for i in range(3):
+                bring(i).start()
+        for name in ("gwc", "gsum", "gb1") + (("gw",) if alone else ()):
             r[name][...] = jnp.zeros_like(r[name])
-        for name in ("tok", "cot"):
-            staged = r[name + "f"]
-            for c in range(sz.width // 128):
-                part = r[name][:, :, c * 128 : (c + 1) * 128].astype(F32)
-                staged[c, : patches * GROUP, :] = part.reshape(patches * GROUP, 128)
-                staged[c, patches * GROUP :, :] = jnp.zeros(((rows - patches) * GROUP, 128), F32)
-        if alone:
-            gw[...] = jnp.zeros_like(gw)
-        else:
-            pltpu.make_async_copy(r["carry"], gw, r["carried"]).start()
+        to_staging("tok")
+        to_staging("cot")
+        for l in range(layers):
+            r["b1s"][l] = r["b1"][l : l + 1, :]
+            r["b2s"][l] = r["b2"][l : l + 1, :]
 
     def weight_ready(i, l):
         if sz.blocks:
@@ -114,7 +148,14 @@
 
     for g in range(STEP):
         x[0, image(g), :] = unstage("tokf", g)
+    share = STEP // layers
+
+    def rows_of(g):
+        return pl.ds(pl.multiple_of(g * rows, 8), rows)
+
     def forward(l, _):
+        for g in range(share):
+            grad[rows_of(l * share + g), :] = unstage("cotf", l * share + g)
         mid, mixed, crossed = r["mid"], r["mixed"], r["crossed"]
         for g in range(STEP):
             x_in = x[l, image(g), :]
@@ -134,29 +175,33 @@
             r["normed"][l, at, :] = v.astype(BF)
         weight_ready(0, l)
         for at in blocks:
-            h = dot(r["normed"][l, at, :], weight(0, l), NN) + r["b1"][l]
+            h = dot(r["normed"][l, at, :], weight(0, l), NN) + r["b1s"][l]
             phi = 0.5 + 0.5 * lax.erf(h * SQRT_HALF)
             r["act"][l, at, :] = (h * phi).astype(BF)
             r["h"][l, at, :] = h.astype(BF)
             r["phi"][l, at, :] = phi.astype(BF)
         weight_ready(1, l)
         for at in blocks:
-            branch = dot(r["act"][l, at, :], weight(1, l), NT) + r["b2"][l]
+            branch = dot(r["act"][l, at, :], weight(1, l), NT) + r["b2s"][l]
             r["branch"][l, at, :] = branch.astype(BF)
             x[l + 1, at, :] = mid[l, at, :] + row("ls", l, 1) * branch
     lax.fori_loop(0, layers, forward, None)
-    for g in range(STEP):
-        stage("tokf", g, x[layers, image(g), :])
-        grad[image(g), :] = unstage("cotf", g)
-
-    if not alone:
-
-        @pl.when(step == 0)
-        def _():
+    @pl.when(step == 0)
+    def _():
+        if not alone:
             pltpu.make_async_copy(r["carry"], gw, r["carried"]).wait()
+
+    @pl.when(step == last)
+    def _():
+        if not alone:
+            for i in range(3):
+                bring(i).wait()
+                pass_on(i).start()
 
     def backward(back, _):
         l = layers - 1 - back
+        for g in range(share):
+            stage("tokf", back * share + g, x[layers, rows_of(back * share + g), :])
         for at in blocks:
             g_out = grad[at, :]
             add(l, LS1, g_out * r["branch"][l, at, :].astype(F32))
@@ -165,9 +210,9 @@
             r["bg"][at, :] = bg.astype(BF)
         for at in blocks:
             act_grad = dot(r["bg"][at, :], weight(1, l), NN)
-            h = r["h"][l, at, :].astype(F32)
-            slope = r["phi"][l, at, :].astype(F32) + h * (jnp.exp(h * h * -0.5) * PDF_SCALE)
-            r["pg"][at, :] = (act_grad * slope).astype(BF)
+            h = r["h"][l, at, :]
+            density = jnp.exp2(h * h * BF(HALF_LOG2E)) * BF(PDF_SCALE)
+            r["pg"][at, :] = act_grad.astype(BF) * (r["phi"][l, at, :] + h * density)
         pg = r["pg"][:, columns]
         r["gb1"][l] += jnp.sum(pg.astype(F32).reshape(m // 8, 8, kept), axis=0)
         gw[0, l] += dot(r["normed"][l], pg, TN)
@@ -205,14 +250,11 @@
                 full = jnp.concatenate([gwc, table[:, :256], table[:, 256:]], axis=0)
                 ref[l] = full.astype(BF)
 
-        for name, staged in (("out", "tokf"), ("tgrad", "cotf")):
-            for c in range(sz.width // 128):
-                v = r[staged][c, : patches * GROUP, :].reshape(patches, GROUP, 128)
-                r[name][:, :, c * 128 : (c + 1) * 128] = v.astype(BF)
-
-        def write_rows(ref, k, i, place, wanted):
-            for l in range(layers):
-                ref[k, l] = gw[i, l, place, wanted].astype(BF)
+        from_staging("tok")
+        deliver(0).start()
+        from_staging("cot")
+        deliver(1).start()
+        deliver(2).start()
 
         if alone:
             write_small(r["small"], mine)
@@ -220,22 +262,31 @@
             for i in range(2):
                 for l in range(layers):
                     r["own"][i, l] = gw[i, l, :, mine]
-                for k in range(sz.n_dp if sz.blocks else 1):
-                    size = sz.shard if sz.blocks else sz.width
-                    write_rows(r[f"blocks{i}"], k, i, slice(k * size, (k + 1) * size), theirs)
+                    for k in range(sz.n_dp if sz.blocks else 1):
+                        size = sz.shard if sz.blocks else sz.width
+                        place = slice(k * size, (k + 1) * size)
+                        r["blocks"][k, i, l] = gw[i, l, place, theirs].astype(BF)
         else:
             write_small(r["small"], slice(None))
             for i in range(2):
                 if sz.blocks:
+                    n = sz.n_dp // 2
                     for k in range(sz.n_dp):
                         at = meta[4 + (2 + i) * sz.n_dp + k] * sz.shard
                         at = pl.ds(pl.multiple_of(at, 16), sz.shard)
-                        write_rows(r[f"blocks{i}"], k, i, at, slice(None))
+                        ref = r[f"stay{i}"] if k < n else r[f"leave{i}"]
+                        for l in range(layers):
+                            ref[k % n, l] = gw[i, l, at, :].astype(BF)
                 else:
-                    write_rows(r[f"blocks{i}"], 0, i, slice(None), slice(None))
-
-
-def run(sz, alone, meta, common, weights, carry=None):
+                    for l in range(layers):
+                        r[f"stay{i}"][0, l] = gw[i, l].astype(BF)
+            for i in range(3):
+                pass_on(i).wait()
+        for i in range(3):
+            deliver(i).wait()
+
+
+def run(sz, alone, meta, common, weights, first=None):
     steps = GROUP // STEP
     w, m, layers = sz.width, sz.m, sz.layers
     kept = 2 * sz.own if alone else sz.own
@@ -243,26 +294,19 @@
     anywhere = pl.BlockSpec(memory_space=pl.ANY)
     images = (sz.patches, GROUP, w)
 
-    def group_spec(where):
-        return pl.BlockSpec(
-            images, lambda i, meta: (0, where(meta), 0), pipeline_mode=pl.Buffered(1)
-        )
+    group_spec = pl.BlockSpec(
+        images, lambda i, meta: (0, meta[0], 0), pipeline_mode=pl.Buffered(1)
+    )
 
     def fixed_spec(block):
         return pl.BlockSpec(
             block, lambda i, meta: (0,) * len(block), pipeline_mode=pl.Buffered(1)
         )
 
-    def in_all(meta):
-        return meta[0]
-
-    def in_part(meta):
-        return 0
-
     keep_spec = pl.BlockSpec((STEP, 1, sz.depth), lambda i, meta: (meta[0] * steps + i, 0, 0))
     ins = [
-        ("tok", common["tok"], group_spec(in_all)),
-        ("cot", common["cot"], group_spec(in_all)),
+        ("tok", common["tok"], group_spec),
+        ("cot", common["cot"], group_spec),
         ("keep", common["keep"], keep_spec),
     ]
     for name in ("scale", "shift", "ls", "wc", "b1", "b2"):
@@ -278,20 +322,30 @@
     else:
         ins.append(("w", weights, vmem))
     if not alone:
-        ins.append(("carry", carry, anywhere))
+        ins.append(("carry", first["own"], anywhere))
+        for name in ("out0", "tgrad1", "tgrad2"):
+            ins.append(("own_" + name, first[name], anywhere))
+        scratch.append(("passed", pltpu.SemaphoreType.DMA((3,))))
+        scratch.append(("pass_out", pltpu.VMEM(images, BF)))
+        scratch.append(("pass_tgrad", pltpu.VMEM(images, BF)))
         scratch.append(("carried", pltpu.SemaphoreType.DMA))
 
-    where, count = (in_part, GROUP) if alone else (in_all, sz.count)
-    outs = [
-        ("out", (sz.patches, count, w), BF, group_spec(where)),
-        ("tgrad", (sz.patches, count, w), BF, group_spec(where)),
-    ]
+    if alone:
+        cut = sz.patches // 2
+        parts = (("out0", sz.patches), ("tgrad1", cut), ("tgrad2", sz.patches - cut))
+        outs = [(name, (n, GROUP, w), BF, anywhere) for name, n in parts]
+    else:
+        outs = [(name, (sz.patches, sz.count, w), BF, anywhere) for name in ("out", "tgrad")]
     small = (layers, sz.small, 256)
-    block = (sz.n_dp, layers, sz.shard, sz.own) if sz.blocks else (1, layers, w, sz.own)
+    block = (layers, sz.shard, sz.own) if sz.blocks else (layers, w, sz.own)
+    n_blocks = sz.n_dp if sz.blocks else 1
     outs.append(("small", small, BF, fixed_spec(small)))
-    outs.append(("blocks0", block, BF, fixed_spec(block)))
-    outs.append(("blocks1", block, BF, fixed_spec(block)))
-    if alone:
+    if not alone:
+        part = ((n_blocks + 1) // 2,) + block
+        for name in ("stay0", "stay1") + (("leave0", "leave1") if sz.blocks else ()):
+            outs.append((name, part, BF, fixed_spec(part)))
+    else:
+        outs.append(("blocks", (n_blocks, 2) + block, BF, fixed_spec((n_blocks, 2) + block)))
         outs.append(("send", small, BF, fixed_spec(small)))
         own = (2, layers, w, sz.own)
         outs.append(("own", own, F32, fixed_spec(own)))
@@ -312,10 +366,15 @@
         ("gwc", (layers, sz.rows, sz.depth), F32),
         ("gsum", (layers, B1, 8, w), F32),
         ("gb1", (layers, 8, kept), F32),
+        ("b1s", (layers, 1, sz.hidden), F32),
+        ("b2s", (layers, 1, w), F32),
+        ("tokb", images, BF),
+        ("cotb", images, BF),
         ("tokf", (w // 128, GROUP * sz.rows, 128), F32),
         ("cotf", (w // 128, GROUP * sz.rows, 128), F32),
     ):
         scratch.append((name, pltpu.VMEM(shape, dtype)))
+    scratch.append(("moved", pltpu.SemaphoreType.DMA((3,))))
     names = ("meta",) + tuple(e[0] for e in ins + outs + scratch)
     flops = steps * m * 24 * w * sz.hidden
     results = pl.pallas_call(
@@ -343,7 +402,7 @@
     return [2**k for k in range(1, n.bit_length() - 1)]
 
 
-def gather_weights(sz, w1, w2):
+def gather_columns(sz, w1, w2):
     both = jnp.stack([w1, w2])
     parts = [both] + [swap(both, "hid", k) for k in range(1, sz.n_hid)]
     hid = lax.axis_index("hid")
@@ -353,7 +412,10 @@
         for h in range(1, sz.n_hid):
             v = jnp.where(hid == h, parts[j ^ h], v)
         columns.append(v)
-    full = jnp.concatenate(columns, axis=2)
+    return jnp.concatenate(columns, axis=2)
+
+
+def gather_rows(sz, full):
     got = [full[i][None] for i in range(2)]
     bits = powers(sz.n_dp)
     for step in range(len(bits)):
@@ -380,10 +442,76 @@
     return result
 
 
-def scatter_step(blocks, bit):
+def scatter_step(stay, leave, bit):
+    got = swap(leave, "dp", bit)
+    return stay.astype(F32) + got.astype(F32)
+
+
+def halves(blocks):
     n = blocks.shape[0] // 2
-    got = swap(blocks[n:].astype(BF), "dp", bit)
-    return blocks[:n].astype(F32) + got.astype(F32)
+    return blocks[:n], blocks[n:].astype(BF)
+
+
+def finish_body(sz, *refs):
+    (meta, keep0, keep1, got0, got1, theirs, small, got_s0, got_s1) = refs[:9]
+    sent = refs[9:12]
+    (out, tgrad, scale, shift, ls, gwc, gb, w1, b1, w2, b2, pass0, pass1, pass2, moved) = refs[14:]
+    place = pl.ds(pl.multiple_of(meta[0] * GROUP, GROUP), GROUP)
+    cut = sz.patches // 2
+    spots = (out.at[:, place, :], tgrad.at[:cut, place, :], tgrad.at[cut:, place, :])
+    brought, copies = [], []
+    for i, buffer in enumerate((pass0, pass1, pass2)):
+        brought.append(pltpu.make_async_copy(sent[i], buffer, moved.at[i]))
+        copies.append(pltpu.make_async_copy(buffer, spots[i], moved.at[i]))
+        brought[i].start()
+    w1[...] = keep0[0] + got0[0].astype(F32) + theirs[0].astype(F32)
+    w2[...] = keep1[0] + got1[0].astype(F32) + theirs[1].astype(F32)
+    for i in range(3):
+        brought[i].wait()
+        copies[i].start()
+    for l, got in enumerate((got_s0, got_s1)):
+        total = small[l].astype(F32) + got[...].astype(F32)
+        gwc[:, l, :] = total[: sz.patches, : sz.patches]
+        lane = sz.patches // 128 * 128
+        gb[l : l + 1, :] = total[:, lane : lane + 128].T[
+            sz.patches - lane : sz.patches - lane + 1, : sz.patches
+        ]
+        low, high = total[sz.rows : sz.rows + 8], total[sz.rows + 8 : sz.rows + 16]
+        table = jnp.concatenate([low, high[:, : sz.width - 256]], axis=1)
+        for ref, kinds in ((scale, (S0, S1)), (shift, (T0, T1)), (ls, (LS0, LS1))):
+            for k, kind in enumerate(kinds):
+                ref[l, k : k + 1, :] = table[kind : kind + 1]
+        b1[l : l + 1, :] = table[B1 : B1 + 1]
+        b2[l : l + 1, :] = table[B2 : B2 + 1]
+    for c in copies:
+        c.wait()
+
+
+def finish(sz, meta, keep, got, theirs, small, got_small, sent, out, tgrad):
+    vmem = pl.BlockSpec(memory_space=pltpu.VMEM)
+    anywhere = pl.BlockSpec(memory_space=pl.ANY)
+    layers, w, p = sz.layers, sz.width, sz.patches
+    vec = (layers, 2, w)
+    shapes = [vec, vec, vec, (p, layers, p), (layers, p)]
+    shapes += [(layers, sz.shard, sz.own), (layers, sz.own)] + [
+        (layers, sz.shard, sz.own),
+        (layers, w),
+    ]
+    whole = jax.ShapeDtypeStruct(out.shape, BF)
+    return pl.pallas_call(
+        functools.partial(finish_body, sz),
+        grid_spec=pltpu.PrefetchScalarGridSpec(
+            num_scalar_prefetch=1,
+            grid=(),
+            in_specs=[vmem] * 8 + [anywhere] * 5,
+            out_specs=[anywhere] * 2 + [vmem] * 9,
+            scratch_shapes=[pltpu.VMEM(v.shape, BF) for v in sent]
+            + [pltpu.SemaphoreType.DMA((3,))],
+        ),
+        out_shape=[whole, whole] + [jax.ShapeDtypeStruct(s, F32) for s in shapes],
+        input_output_aliases={12: 0, 13: 1},
+        compiler_params=pltpu.CompilerParams(vmem_limit_bytes=32 * 2**20),
+    )(meta, *keep, *got, theirs, small, *got_small, *sent, out, tgrad)
 
 
 def on_device(
@@ -406,9 +534,18 @@
     me, hid = lax.axis_index("dp"), lax.axis_index("hid")
     half = hid % 2
 
+    bias_hi = cross_bias.astype(BF)
+    bias_lo = (cross_bias - bias_hi.astype(F32)).astype(BF)
+    wc = jnp.concatenate([crosspatch_weight, bias_hi[:, :, None], bias_lo[:, :, None]], axis=2)
+    wc = jnp.pad(wc, ((0, 0), (0, sz.rows - patches), (0, sz.depth - patches - 2)))
+    keep = jnp.pad(masks.astype(F32)[:, None, :], ((0, 0), (0, 0), (0, sz.depth - patches)))
+
     weights = []
     for l in range(layers):
-        got, other, orders = gather_weights(sz, fc1_weight[l], fc2_weight[l])
+        full = gather_columns(sz, fc1_weight[l], fc2_weight[l])
+        if l == 0:
+            full, wc, keep = lax.optimization_barrier((full, wc, keep))
+        got, other, orders = gather_rows(sz, full)
         if sz.blocks:
             weights.append([(got[i], other[i]) for i in range(2)])
         else:
@@ -422,11 +559,6 @@
     if not sz.blocks:
         weights = jnp.stack(weights, axis=1)
 
-    bias_hi = cross_bias.astype(BF)
-    bias_lo = (cross_bias - bias_hi.astype(F32)).astype(BF)
-    wc = jnp.concatenate([crosspatch_weight, bias_hi[:, :, None], bias_lo[:, :, None]], axis=2)
-    wc = jnp.pad(wc, ((0, 0), (0, sz.rows - patches), (0, sz.depth - patches - 2)))
-    keep = jnp.pad(masks.astype(F32)[:, None, :], ((0, 0), (0, 0), (0, sz.depth - patches)))
     common = {
         "tok": tokens.transpose(1, 0, 2),
         "cot": cotangent.transpose(1, 0, 2),
@@ -435,8 +567,8 @@
         "shift": aff_shift,
         "ls": layer_scale,
         "wc": wc,
-        "b1": fc1_bias[:, None, :],
-        "b2": fc2_bias[:, None, :],
+        "b1": fc1_bias,
+        "b2": fc2_bias,
     }
     exchanges = exchange_orders(n_dp)
     places = [me ^ k for k in orders[0] + orders[1]]
@@ -446,63 +578,62 @@
         return jnp.stack([first, column, half, 1 - half] + places).astype(jnp.int32)
 
     first = run(sz, True, meta(half, hid // 2), common, weights)
-    sent_out = swap(first["out"], "hid", 1)
-    sent_grad = swap(first["tgrad"], "hid", 1)
+    sent = [swap(first[name], "hid", 1) for name in ("out0", "tgrad1", "tgrad2")]
     sent_small = swap(first["send"], "hid", 1)
 
-    def by_owner(blocks):
-        if sz.blocks:
-            return blocks
-        return jnp.moveaxis(blocks.reshape(layers, n_dp, sz.shard, sz.own), 1, 0)
-
-    theirs = jnp.stack([by_owner(first[f"blocks{i}"]) for i in range(2)], axis=1)
+    theirs = first["blocks"]
+    if not sz.blocks:
+        theirs = theirs.reshape(2, layers, n_dp, sz.shard, sz.own)
+        theirs = jnp.moveaxis(theirs, 2, 0)
     theirs = lax.all_to_all(theirs, "dp", split_axis=0, concat_axis=0, tiled=True)
-    theirs = theirs.astype(F32).sum(axis=0).astype(BF)
-
-    rest = run(sz, False, meta(jnp.int32(2), hid), common, weights, first["own"])
-    gw = [by_owner(rest[f"blocks{i}"]) for i in range(2)]
-    theirs, gw, small_rest = lax.optimization_barrier((theirs, gw, rest["small"]))
-    theirs = swap(theirs, "hid", 1)
-    if not sz.blocks:
-        gw = [gw[i][jnp.array(exchanges[i][1]) ^ me] for i in range(2)]
+
+    rest = run(sz, False, meta(jnp.int32(2), hid), common, weights, first)
+    small_rest = rest["small"]
+    if sz.blocks:
+        gw = [(rest[f"stay{i}"], rest[f"leave{i}"]) for i in range(2)]
+    else:
+        gw = [rest[f"stay{i}"].reshape(layers, n_dp, sz.shard, sz.own) for i in range(2)]
+        gw = [jnp.moveaxis(g, 1, 0)[jnp.array(e[1]) ^ me] for g, e in zip(gw, exchanges)]
+        gw = [halves(g) for g in gw]
+    gw, theirs, sent[:2] = lax.optimization_barrier((gw, theirs, sent[:2]))
     alone_small = first["small"].astype(F32) + sent_small.astype(F32)
     small = (alone_small + small_rest.astype(F32)).astype(BF)
     small = [small[l] for l in range(layers)]
-    for k in range(len(exchanges[0][0])):
-        gw = [scatter_step(gw[i], exchanges[i][0][k]) for i in range(2)]
+    phases = len(exchanges[0][0])
+    for k in range(phases - 1):
+        gw = [scatter_step(*gw[i], exchanges[i][0][k]) for i in range(2)]
         for l in range(layers):
-            other = swap(small[l].astype(BF), "dp", exchanges[l % 2][0][k])
-            small[l] = small[l].astype(BF).astype(F32) + other.astype(F32)
+            other = swap(small[l], "dp", exchanges[l % 2][0][k])
+            small[l] = (small[l].astype(F32) + other.astype(F32)).astype(BF)
         if k == 0:
-            gw, small, sent_out, sent_grad = lax.optimization_barrier(
-                (gw, small, sent_out, sent_grad)
-            )
-    gw = [gw[i][0] + theirs[i].astype(F32) for i in range(2)]
-    small = jnp.stack(small)
-    gwc = small[:, :patches, :patches]
-    sums = jnp.concatenate(
-        [small[:, sz.rows : sz.rows + 8], small[:, sz.rows + 8 :, : sz.width - 256]], axis=2
+            theirs = swap(theirs.astype(F32).sum(axis=0).astype(BF), "hid", 1)
+        gw = [halves(g) for g in gw]
+    got = [swap(gw[i][1], "dp", exchanges[i][0][-1]) for i in range(2)]
+    got_small = [swap(small[l], "dp", exchanges[l % 2][0][-1]) for l in range(layers)]
+    out, tgrad, scale, shift, ls, gwc, gb, w1, b1, w2, b2 = finish(
+        sz,
+        jnp.stack([1 - half]).astype(jnp.int32),
+        [g[0] for g in gw],
+        got,
+        theirs,
+        jnp.stack(small),
+        got_small,
+        sent,
+        rest["out"],
+        rest["tgrad"],
     )
-
-    def put(all_images, mine, theirs):
-        all_images = lax.dynamic_update_slice_in_dim(all_images, mine, half * GROUP, axis=1)
-        all_images = lax.dynamic_update_slice_in_dim(
-            all_images, theirs, (1 - half) * GROUP, axis=1
-        )
-        return all_images.transpose(1, 0, 2)
-
     return (
-        put(rest["out"], first["out"], sent_out),
-        put(rest["tgrad"], first["tgrad"], sent_grad),
-        jnp.stack([sums[:, S0], sums[:, S1]], axis=1),
-        jnp.stack([sums[:, T0], sums[:, T1]], axis=1),
-        jnp.stack([sums[:, LS0], sums[:, LS1]], axis=1),
-        gwc,
-        small[:, :patches, patches],
-        gw[0],
-        sums[:, B1],
-        gw[1],
-        sums[:, B2],
+        out.transpose(1, 0, 2),
+        tgrad.transpose(1, 0, 2),
+        scale,
+        shift,
+        ls,
+        gwc.transpose(1, 0, 2),
+        gb,
+        w1,
+        b1,
+        w2,
+        b2,
     )
 
 

time: 176 us -> 169 us (0.960)
  local copies, waits for them, and re-layouts: 18 us -> 4.4 us
  starting transfers between devices: 40.1 us -> 45 us
  waiting for transfers between devices: 19.7 us -> 22.9 us
    dynamic_update_slice x4 -> x0, local copies, waits for them, and re-layouts: 8.48 us -> none  [the longest x2 4.92 us: put(): lax.dynamic_update_slice_in_dim(all_images, mine, half * GROUP, axis=1)]
    pallas_call x2, Pallas kernels: 88.2 us -> 83.6 us  [run(): pl.pallas_call(functools.partial(kernel_body, sz, kept, names), grid_spec...]
    ppermute x34 -> x35, starting transfers between devices: 36.4 us -> 40.6 us  [swap(): return lax.ppermute(x, axis, [(i, i ^ k) for i in range(n)])]
    ppermute x34 -> x35, waiting for transfers between devices: 19.7 us -> 22.9 us  [swap(): return lax.ppermute(x, axis, [(i, i ^ k) for i in range(n)])]
    pallas_call x0 -> x1, Pallas kernels: none -> 2.88 us  [finish(): pl.pallas_call(functools.partial(finish_body, sz), grid_spec=pltpu.Prefet...]
    another operation x8 -> x3, other arithmetic: 2.71 us -> 0.05 us  [the longest x2 0.03 us: gather_columns(): both = jnp.stack([w1, w2])]
    unnamed x32 -> x19, local copies, waits for them, and re-layouts: 2.89 us -> 1.06 us
  transfers between devices with their start and end apart: 35 -> 36, of which waited for: 10 -> 14; matrix products, arithmetic and copies ran while one was open for 12% -> 7% of each run, Pallas kernels for 24% -> 24%
where the time goes in v1:
time: 169 us; the launch traced here: 168 us
  Pallas kernels  86.5 us (51%)
  starting transfers between devices  45 us (27%)
  waiting for transfers between devices  22.9 us (14%)
  other arithmetic  8.31 us (5%)
  local copies, waits for them, and re-layouts  4.4 us (3%)
    pallas_call x2, Pallas kernels, run(): pl.pallas_call(functools.partial(kernel_body, sz, kept, names), grid_spec...  83.6 us
    ppermute x35, starting transfers between devices, swap(): return lax.ppermute(x, axis, [(i, i ^ k) for i in range(n)])  40.6 us
    ppermute x35, waiting for transfers between devices, swap(): return lax.ppermute(x, axis, [(i, i ^ k) for i in range(n)])  22.9 us
    all_to_all x1, starting transfers between devices, on_device(): lax.all_to_all(theirs, 'dp', split_axis=0, concat_axis=0, tiled=True)  4.48 us
  transfers between devices with their start and end apart: 36, of which 14 were waited for; matrix products, arithmetic and copies ran while one was open for 7% of the time, Pallas kernels for 24%

profile of v1, /device:TPU:0, one launch (start us, length us, event | category | flops | bytes accessed | tf_op | source)
XLA Modules:
  0.0 168.5 jit_solution(15630016019367024609)
XLA Ops:
  0.6 0.8 fusion.12
  1.5 4.1 %collective-permute-start.10 = (bf16[2,48,384]{2,1,0:T(8,128)(2,1)S(1)}, bf16[2,48,384]{2,1,0:T(8,128)(2,1)S(1)}, u32[]{:S(2)}, u32[]{:S(2)}) collective-permute-start(bf16[2,48,384]{2,1,0:T(8,128)(2,1)S(1)} %pad_maximum_fusion.12), channel_id=1, source_target_pairs={{0,2},{1,3},{2,0},{3,1},{4,6},{5,7},{6,4},{7,5},{8,10},{9,11},{10,... | collective-permute-start | bytes 221192 | tf_op jit(solution)/shard_map/ppermute | solution.py:398
  5.6 1.6 collective-permute-start.11
  7.2 3.9 %collective-permute-start = (bf16[2,48,384]{2,1,0:T(8,128)(2,1)S(1)}, bf16[2,48,384]{2,1,0:T(8,128)(2,1)S(1)}, u32[]{:S(2)}, u32[]{:S(2)}) collective-permute-start(bf16[2,48,384]{2,1,0:T(8,128)(2,1)S(1)} %pad_maximum_fusion.11), channel_id=1, source_target_pairs={{0,3},{1,2},{2,1},{3,0},{4,7},{5,6},{6,5},{7,4},{8,11},{9,10},{10,... | collective-permute-start | bytes 221192 | tf_op jit(solution)/shard_map/ppermute | solution.py:398
  11.1 0.8 convert_bitcast_fusion
  12.2 1.0 copy.29
  13.2 0.7 convert_element_type.91
  14.6 0.8 fusion.8.args_7_
  15.4 0.6 collective-permute-start.2
  16.1 1.7 %collective-permute-start.15 = (bf16[1,48,1536]{2,1,0:T(8,128)(2,1)S(1)}, bf16[1,48,1536]{2,1,0:T(8,128)(2,1)S(1)}, u32[]{:S(2)}, u32[]{:S(2)}) collective-permute-start(bf16[1,48,1536]{2,1,0:T(8,128)(2,1)S(1)} %get-tuple-element.81), channel_id=1, source_target_pairs={{0,16},{4,20},{8,24},{12,28},{16,0},{20,4},{24,8},{28,12},{1,17},{... | collective-permute-start | bytes 442376 | tf_op jit(solution)/shard_map/ppermute | solution.py:398
  17.9 1.5 collective-permute-start.12
  19.9 1.8 %collective-permute-start.6 = (bf16[1,48,1536]{2,1,0:T(8,128)(2,1)S(1)}, bf16[1,48,1536]{2,1,0:T(8,128)(2,1)S(1)}, u32[]{:S(2)}, u32[]{:S(2)}) collective-permute-start(bf16[1,48,1536]{2,1,0:T(8,128)(2,1)S(1)} %get-tuple-element.87), channel_id=1, source_target_pairs={{0,16},{4,20},{8,24},{12,28},{16,0},{20,4},{24,8},{28,12},{1,17},{... | collective-permute-start | bytes 442376 | tf_op jit(solution)/shard_map/ppermute | solution.py:398
  21.7 1.5 collective-permute-start.3
  24.0 1.3 collective-permute-start.13
  25.4 1.1 collective-permute-done.6
  26.5 2.0 %collective-permute-start.7 = (bf16[2,48,1536]{2,1,0:T(8,128)(2,1)S(1)}, bf16[2,48,1536]{2,1,0:T(8,128)(2,1)S(1)}, u32[]{:S(2)}, u32[]{:S(2)}) collective-permute-start(bf16[2,48,1536]{2,1,0:T(8,128)(2,1)S(1)} %pad_maximum_fusion.6), channel_id=1, source_target_pairs={{0,8},{4,12},{8,0},{12,4},{16,24},{20,28},{24,16},{28,20},{1,9},{5... | collective-permute-start | bytes 884744 | tf_op jit(solution)/shard_map/ppermute | solution.py:398
  28.5 1.7 collective-permute-start.4
  30.2 4.6 %collective-permute-done.16 = bf16[2,48,1536]{2,1,0:T(8,128)(2,1)S(1)} collective-permute-done((bf16[2,48,1536]{2,1,0:T(8,128)(2,1)S(1)}, bf16[2,48,1536]{2,1,0:T(8,128)(2,1)S(1)}, u32[]{:S(2)}, u32[]{:S(2)}) %collective-permute-start.16) | collective-permute-done | bytes 294944 | tf_op jit(solution)/shard_map/ppermute | solution.py:398
  35.6 3.2 %collective-permute-done.7 = bf16[2,48,1536]{2,1,0:T(8,128)(2,1)S(1)} collective-permute-done((bf16[2,48,1536]{2,1,0:T(8,128)(2,1)S(1)}, bf16[2,48,1536]{2,1,0:T(8,128)(2,1)S(1)}, u32[]{:S(2)}, u32[]{:S(2)}) %collective-permute-start.7) | collective-permute-done | bytes 294944 | tf_op jit(solution)/shard_map/ppermute | solution.py:398
  39.6 0.7 stack.53.args_0_
  40.3 0.7 stack.49.args_0_
  41.1 0.8 collective-permute-done.5.args_11_
  42.0 43.3 %shard_map.203 = (bf16[196,8,384]{2,1,0:T(8,128)(2,1)}, bf16[98,8,384]{2,1,0:T(8,128)(2,1)}, bf16[98,8,384]{2,1,0:T(8,128)(2,1)}, bf16[2,216,256]{2,1,0:T(8,128)...) custom-call(s32[36]{0:T(128)} %stack.53.args_0_, ...), custom_call_target="tpu_custom_call" | custom-call | flops 22649241600 | bytes 56623104 | tf_op jit(solution)/shard_map/pallas_call | solution.py:380
  85.3 1.5 collective-permute-start.27
  87.4 1.4 collective-permute-start.19
  88.9 4.5 %all-to-all-start = ((bf16[8,2,2,48,384]{4,3,2,1,0:T(8,128)(2,1)}), bf16[8,2,2,48,384]{4,3,2,1,0:T(8,128)(2,1)}, u32[]{:S(2)}, u32[]{:S(2)}) async-start(bf16[8,2,2,48,384]{4,3,2,1,0:T(8,128)(2,1)} %get-tuple-element.57), calls=%async_computation | async-start | bytes 2359296 | tf_op jit(solution)/shard_map/all_to_all | solution.py:588
  93.3 40.3 %shard_map.204 = (bf16[196,24,384]{2,1,0:T(8,128)(2,1)}, bf16[196,24,384]{2,1,0:T(8,128)(2,1)}, bf16[2,216,256]{2,1,0:T(8,128)(2,1)}, bf16[4,2,48,384]{3,2,1,0:T...) custom-call(s32[36]{0:T(128)} %stack.49.args_0_, ...), custom_call_target="tpu_custom_call" | custom-call | flops 22649241600 | bytes 56623104 | tf_op jit(solution)/shard_map/pallas_call | solution.py:380
  133.7 1.1 add_convert_fusion
  135.4 0.8 collective-permute-done.28
  136.4 1.7 %collective-permute-start.29 = (bf16[216,256]{1,0:T(8,128)(2,1)S(1)}, bf16[216,256]{1,0:T(8,128)(2,1)S(1)}, u32[]{:S(2)}, u32[]{:S(2)}) collective-permute-start(bf16[216,256]{1,0:T(8,128)(2,1)S(1)} %get-tuple-element.93), channel_id=1, source_target_pairs={{0,8},{4,12},{8,0},{12,4},{16,24},{20,28},{24,16},{28,20},{1,9},{5... | collective-permute-start | bytes 331784 | tf_op jit(solution)/shard_map/ppermute | solution.py:398
  138.1 0.6 collective-permute-start.34
  138.8 1.5 collective-permute-start.31
  140.4 1.4 collective-permute-done.29
  141.8 1.7 %collective-permute-start.32 = (bf16[216,256]{1,0:T(8,128)(2,1)S(1)}, bf16[216,256]{1,0:T(8,128)(2,1)S(1)}, u32[]{:S(2)}, u32[]{:S(2)}) collective-permute-start(bf16[216,256]{1,0:T(8,128)(2,1)S(1)} %add_convert_fusion.3), channel_id=1, source_target_pairs={{0,16},{4,20},{8,24},{12,28},{16,0},{20,4},{24,8},{28,12},{1,17},{... | collective-permute-start | bytes 331784 | tf_op jit(solution)/shard_map/ppermute | solution.py:398
  143.6 1.5 collective-permute-start.33
  145.2 2.1 %reduce_sum.12 = bf16[2,2,48,384]{3,2,1,0:T(8,128)(2,1)} reduce(bf16[8,2,2,48,384]{4,3,2,1,0:T(8,128)(2,1)} %all-to-all-done, bf16[]{:T(256)} %constant.50.clone.1), dimensions={0}, to_apply=%region_0.1 | reduce | flops 516096 | bytes 1327106 | tf_op jit(solution)/shard_map/reduce_sum | solution.py:609
  147.3 0.6 collective-permute-start.26
  147.9 1.0 convert_add_fusion
  149.0 1.3 collective-permute-start.23
  150.3 1.0 convert_add_fusion.1
  151.4 3.4 %collective-permute-done.23 = bf16[2,2,48,384]{3,2,1,0:T(8,128)(2,1)S(1)} collective-permute-done((bf16[2,2,48,384]{3,2,1,0:T(8,128)(2,1)S(1)}, bf16[2,2,48,384]{3,2,1,0:T(8,128)(2,1)S(1)}, u32[]{:S(2)}, u32[]{:S(2)}) %collective-permute-start.23) | collective-permute-done | bytes 147488 | tf_op jit(solution)/shard_map/ppermute | solution.py:398
  154.8 0.7 collective-permute-start.21
  155.5 4.4 %collective-permute-done.21 = bf16[2,2,48,384]{3,2,1,0:T(8,128)(2,1)S(1)} collective-permute-done((bf16[2,2,48,384]{3,2,1,0:T(8,128)(2,1)S(1)}, bf16[2,2,48,384]{3,2,1,0:T(8,128)(2,1)S(1)}, u32[]{:S(2)}, u32[]{:S(2)}) %collective-permute-start.21) | collective-permute-done | bytes 147488 | tf_op jit(solution)/shard_map/ppermute | solution.py:398
  159.9 0.7 collective-permute-start.25
  160.7 2.4 %collective-permute-start.24 = (bf16[1,2,48,384]{3,2,1,0:T(8,128)(2,1)S(1)}, bf16[1,2,48,384]{3,2,1,0:T(8,128)(2,1)S(1)}, u32[]{:S(2)}, u32[]{:S(2)}) collective-permute-start(bf16[1,2,48,384]{3,2,1,0:T(8,128)(2,1)S(1)} %slice.103), channel_id=1, source_target_pairs={{0,16},{4,20},{8,24},{12,28},{16,0},{20,4},{24,8},{28,12},{1,17},{... | collective-permute-start | bytes 221192 | tf_op jit(solution)/shard_map/ppermute | solution.py:398
  163.2 1.1 collective-permute-done.25.refs_4_
  164.3 1.1 collective-permute-done.24.refs_3_
  165.4 2.9 %shard_map.205 = (bf16[196,24,384]{2,1,0:T(8,128)(2,1)}, bf16[196,24,384]{2,1,0:T(8,128)(2,1)}, f32[2,2,384]{2,1,0:T(2,128)}, f32[2,2,384]{2,1,0:T(2,128)}, f32[...) custom-call(s32[1]{0:T(128)} %bitcast.refs_0_, ...), custom_call_target="tpu_custom_call", output_to_operand_aliasing={{0}: (12, {}), {1}: (13, {})} | custom-call | tf_op jit(solution)/shard_map/pallas_call | solution.py:501
  (89 shorter events, 6.0 us)
Async XLA Ops:
  1.5 13.9 %collective-permute-start.10 = (bf16[2,48,384]{2,1,0:T(8,128)(2,1)S(1)}, bf16[2,48,384]{2,1,0:T(8,128)(2,1)S(1)}, u32[]{:S(2)}, u32[]{:S(2)}) collective-permute-start(bf16[2,48,384]{2,1,0:T(8,128)(2,1)S(1)} %pad_maximum_fusion.12), channel_id=1, source_target_pairs={{0,2},{1,3},{2,0},{3,1},{4,6},{5,7},{6,4},{7,5},{8,10},{9,11},{10,... | collective-permute-start | bytes 221192 | tf_op jit(solution)/shard_map/ppermute | solution.py:398
  5.6 10.4 %collective-permute-start.11 = (bf16[2,48,384]{2,1,0:T(8,128)(2,1)S(1)}, bf16[2,48,384]{2,1,0:T(8,128)(2,1)S(1)}, u32[]{:S(2)}, u32[]{:S(2)}) collective-permute-start(bf16[2,48,384]{2,1,0:T(8,128)(2,1)S(1)} %pad_maximum_fusion.12), channel_id=1, source_target_pairs={{0,1},{1,0},{2,3},{3,2},{4,5},{5,4},{6,7},{7,6},{8,9},{9,8},{10,11... | collective-permute-start | bytes 221192 | tf_op jit(solution)/shard_map/ppermute | solution.py:398
  7.2 8.8 %collective-permute-start.9 = (bf16[2,48,384]{2,1,0:T(8,128)(2,1)S(1)}, bf16[2,48,384]{2,1,0:T(8,128)(2,1)S(1)}, u32[]{:S(2)}, u32[]{:S(2)}) collective-permute-start(bf16[2,48,384]{2,1,0:T(8,128)(2,1)S(1)} %pad_maximum_fusion.12), channel_id=1, source_target_pairs={{0,3},{1,2},{2,1},{3,0},{4,7},{5,6},{6,5},{7,4},{8,11},{9,10},{10,... | collective-permute-start | bytes 221192 | tf_op jit(solution)/shard_map/ppermute | solution.py:398
  7.2 12.2 %collective-permute-start = (bf16[2,48,384]{2,1,0:T(8,128)(2,1)S(1)}, bf16[2,48,384]{2,1,0:T(8,128)(2,1)S(1)}, u32[]{:S(2)}, u32[]{:S(2)}) collective-permute-start(bf16[2,48,384]{2,1,0:T(8,128)(2,1)S(1)} %pad_maximum_fusion.11), channel_id=1, source_target_pairs={{0,3},{1,2},{2,1},{3,0},{4,7},{5,6},{6,5},{7,4},{8,11},{9,10},{10,... | collective-permute-start | bytes 221192 | tf_op jit(solution)/shard_map/ppermute | solution.py:398
  11.1 8.3 %collective-permute-start.1 = (bf16[2,48,384]{2,1,0:T(8,128)(2,1)S(1)}, bf16[2,48,384]{2,1,0:T(8,128)(2,1)S(1)}, u32[]{:S(2)}, u32[]{:S(2)}) collective-permute-start(bf16[2,48,384]{2,1,0:T(8,128)(2,1)S(1)} %pad_maximum_fusion.11), channel_id=1, source_target_pairs={{0,2},{1,3},{2,0},{3,1},{4,6},{5,7},{6,4},{7,5},{8,10},{9,11},{10,... | collective-permute-start | bytes 221192 | tf_op jit(solution)/shard_map/ppermute | solution.py:398
  15.4 4.4 %collective-permute-start.2 = (bf16[2,48,384]{2,1,0:T(8,128)(2,1)S(1)}, bf16[2,48,384]{2,1,0:T(8,128)(2,1)S(1)}, u32[]{:S(2)}, u32[]{:S(2)}) collective-permute-start(bf16[2,48,384]{2,1,0:T(8,128)(2,1)S(1)} %pad_maximum_fusion.11), channel_id=1, source_target_pairs={{0,1},{1,0},{2,3},{3,2},{4,5},{5,4},{6,7},{7,6},{8,9},{9,8},{10,11... | collective-permute-start | bytes 221192 | tf_op jit(solution)/shard_map/ppermute | solution.py:398
  16.1 7.1 %collective-permute-start.15 = (bf16[1,48,1536]{2,1,0:T(8,128)(2,1)S(1)}, bf16[1,48,1536]{2,1,0:T(8,128)(2,1)S(1)}, u32[]{:S(2)}, u32[]{:S(2)}) collective-permute-start(bf16[1,48,1536]{2,1,0:T(8,128)(2,1)S(1)} %get-tuple-element.81), channel_id=1, source_target_pairs={{0,16},{4,20},{8,24},{12,28},{16,0},{20,4},{24,8},{28,12},{1,17},{... | collective-permute-start | bytes 442376 | tf_op jit(solution)/shard_map/ppermute | solution.py:398
  17.9 6.1 %collective-permute-start.12 = (bf16[1,48,1536]{2,1,0:T(8,128)(2,1)S(1)}, bf16[1,48,1536]{2,1,0:T(8,128)(2,1)S(1)}, u32[]{:S(2)}, u32[]{:S(2)}) collective-permute-start(bf16[1,48,1536]{2,1,0:T(8,128)(2,1)S(1)} %get-tuple-element.82), channel_id=1, source_target_pairs={{0,8},{4,12},{8,0},{12,4},{16,24},{20,28},{24,16},{28,20},{1,9},{5... | collective-permute-start | bytes 442376 | tf_op jit(solution)/shard_map/ppermute | solution.py:398
  19.9 6.6 %collective-permute-start.6 = (bf16[1,48,1536]{2,1,0:T(8,128)(2,1)S(1)}, bf16[1,48,1536]{2,1,0:T(8,128)(2,1)S(1)}, u32[]{:S(2)}, u32[]{:S(2)}) collective-permute-start(bf16[1,48,1536]{2,1,0:T(8,128)(2,1)S(1)} %get-tuple-element.87), channel_id=1, source_target_pairs={{0,16},{4,20},{8,24},{12,28},{16,0},{20,4},{24,8},{28,12},{1,17},{... | collective-permute-start | bytes 442376 | tf_op jit(solution)/shard_map/ppermute | solution.py:398
  21.7 6.8 %collective-permute-start.3 = (bf16[1,48,1536]{2,1,0:T(8,128)(2,1)S(1)}, bf16[1,48,1536]{2,1,0:T(8,128)(2,1)S(1)}, u32[]{:S(2)}, u32[]{:S(2)}) collective-permute-start(bf16[1,48,1536]{2,1,0:T(8,128)(2,1)S(1)} %get-tuple-element.88), channel_id=1, source_target_pairs={{0,8},{4,12},{8,0},{12,4},{16,24},{20,28},{24,16},{28,20},{1,9},{5... | collective-permute-start | bytes 442376 | tf_op jit(solution)/shard_map/ppermute | solution.py:398
  23.2 11.6 %collective-permute-start.16 = (bf16[2,48,1536]{2,1,0:T(8,128)(2,1)S(1)}, bf16[2,48,1536]{2,1,0:T(8,128)(2,1)S(1)}, u32[]{:S(2)}, u32[]{:S(2)}) collective-permute-start(bf16[2,48,1536]{2,1,0:T(8,128)(2,1)S(1)} %pad_maximum_fusion.9), channel_id=1, source_target_pairs={{0,8},{4,12},{8,0},{12,4},{16,24},{20,28},{24,16},{28,20},{1,9},{5... | collective-permute-start | bytes 884744 | tf_op jit(solution)/shard_map/ppermute | solution.py:398
  24.0 11.0 %collective-permute-start.13 = (bf16[2,48,1536]{2,1,0:T(8,128)(2,1)S(1)}, bf16[2,48,1536]{2,1,0:T(8,128)(2,1)S(1)}, u32[]{:S(2)}, u32[]{:S(2)}) collective-permute-start(bf16[2,48,1536]{2,1,0:T(8,128)(2,1)S(1)} %pad_maximum_fusion.8), channel_id=1, source_target_pairs={{0,16},{4,20},{8,24},{12,28},{16,0},{20,4},{24,8},{28,12},{1,17},{... | collective-permute-start | bytes 884744 | tf_op jit(solution)/shard_map/ppermute | solution.py:398
  26.5 12.3 %collective-permute-start.7 = (bf16[2,48,1536]{2,1,0:T(8,128)(2,1)S(1)}, bf16[2,48,1536]{2,1,0:T(8,128)(2,1)S(1)}, u32[]{:S(2)}, u32[]{:S(2)}) collective-permute-start(bf16[2,48,1536]{2,1,0:T(8,128)(2,1)S(1)} %pad_maximum_fusion.6), channel_id=1, source_target_pairs={{0,8},{4,12},{8,0},{12,4},{16,24},{20,28},{24,16},{28,20},{1,9},{5... | collective-permute-start | bytes 884744 | tf_op jit(solution)/shard_map/ppermute | solution.py:398
  28.5 10.4 %collective-permute-start.4 = (bf16[2,48,1536]{2,1,0:T(8,128)(2,1)S(1)}, bf16[2,48,1536]{2,1,0:T(8,128)(2,1)S(1)}, u32[]{:S(2)}, u32[]{:S(2)}) collective-permute-start(bf16[2,48,1536]{2,1,0:T(8,128)(2,1)S(1)} %pad_maximum_fusion.5), channel_id=1, source_target_pairs={{0,16},{4,20},{8,24},{12,28},{16,0},{20,4},{24,8},{28,12},{1,17},{... | collective-permute-start | bytes 884744 | tf_op jit(solution)/shard_map/ppermute | solution.py:398
  34.9 7.1 %copy-start = (bf16[4,48,1536]{2,1,0:T(8,128)(2,1)}, bf16[4,48,1536]{2,1,0:T(8,128)(2,1)S(1)}, u32[]{:S(2)}) copy-start(bf16[4,48,1536]{2,1,0:T(8,128)(2,1)S(1)} %pad_maximum_fusion.3.args_16_) | copy-start | bytes 1769476
  34.9 6.1 %collective-permute-start.17 = (bf16[4,48,1536]{2,1,0:T(8,128)(2,1)S(1)}, bf16[4,48,1536]{2,1,0:T(8,128)(2,1)S(1)}, u32[]{:S(2)}, u32[]{:S(2)}) collective-permute-start(bf16[4,48,1536]{2,1,0:T(8,128)(2,1)S(1)} %pad_maximum_fusion.3.args_16_), channel_id=1, source_target_pairs={{0,4},{4,0},{8,12},{12,8},{16,20},{20,16},{24,28},{28,24},{1,5},{5... | collective-permute-start | bytes 1769480 | tf_op jit(solution)/shard_map/ppermute | solution.py:398
  35.0 6.9 %copy-start.1 = (bf16[4,48,1536]{2,1,0:T(8,128)(2,1)}, bf16[4,48,1536]{2,1,0:T(8,128)(2,1)S(1)}, u32[]{:S(2)}) copy-start(bf16[4,48,1536]{2,1,0:T(8,128)(2,1)S(1)} %pad_maximum_fusion.2.args_14_) | copy-start | bytes 1769476
  35.1 5.9 %collective-permute-start.14 = (bf16[4,48,1536]{2,1,0:T(8,128)(2,1)S(1)}, bf16[4,48,1536]{2,1,0:T(8,128)(2,1)S(1)}, u32[]{:S(2)}, u32[]{:S(2)}) collective-permute-start(bf16[4,48,1536]{2,1,0:T(8,128)(2,1)S(1)} %pad_maximum_fusion.2.args_14_), channel_id=1, source_target_pairs={{0,4},{4,0},{8,12},{12,8},{16,20},{20,16},{24,28},{28,24},{1,5},{5... | collective-permute-start | bytes 1769480 | tf_op jit(solution)/shard_map/ppermute | solution.py:398
  38.9 3.1 %copy-start.2 = (bf16[4,48,1536]{2,1,0:T(8,128)(2,1)}, bf16[4,48,1536]{2,1,0:T(8,128)(2,1)S(1)}, u32[]{:S(2)}) copy-start(bf16[4,48,1536]{2,1,0:T(8,128)(2,1)S(1)} %pad_maximum_fusion.1.args_12_) | copy-start | bytes 1769476
  38.9 2.2 %collective-permute-start.8 = (bf16[4,48,1536]{2,1,0:T(8,128)(2,1)S(1)}, bf16[4,48,1536]{2,1,0:T(8,128)(2,1)}, u32[]{:S(2)}, u32[]{:S(2)}) collective-permute-start(bf16[4,48,1536]{2,1,0:T(8,128)(2,1)S(1)} %pad_maximum_fusion.1.args_12_), channel_id=1, source_target_pairs={{0,4},{4,0},{8,12},{12,8},{16,20},{20,16},{24,28},{28,24},{1,5},{5... | collective-permute-start | bytes 1769480 | tf_op jit(solution)/shard_map/ppermute | solution.py:398
  39.0 2.9 %copy-start.3 = (bf16[4,48,1536]{2,1,0:T(8,128)(2,1)}, bf16[4,48,1536]{2,1,0:T(8,128)(2,1)S(1)}, u32[]{:S(2)}) copy-start(bf16[4,48,1536]{2,1,0:T(8,128)(2,1)S(1)} %pad_maximum_fusion.args_10_) | copy-start | bytes 1769476
  39.1 2.9 %collective-permute-start.5 = (bf16[4,48,1536]{2,1,0:T(8,128)(2,1)S(1)}, bf16[4,48,1536]{2,1,0:T(8,128)(2,1)}, u32[]{:S(2)}, u32[]{:S(2)}) collective-permute-start(bf16[4,48,1536]{2,1,0:T(8,128)(2,1)S(1)} %pad_maximum_fusion.args_10_), channel_id=1, source_target_pairs={{0,4},{4,0},{8,12},{12,8},{16,20},{20,16},{24,28},{28,24},{1,5},{5... | collective-permute-start | bytes 1769480 | tf_op jit(solution)/shard_map/ppermute | solution.py:398
  41.0 1.0 copy-start.7
  41.0 1.0 copy-start.8
  85.3 48.4 %collective-permute-start.27 = (bf16[2,216,256]{2,1,0:T(8,128)(2,1)}, bf16[2,216,256]{2,1,0:T(8,128)(2,1)S(1)}, u32[]{:S(2)}, u32[]{:S(2)}) collective-permute-start(bf16[2,216,256]{2,1,0:T(8,128)(2,1)} %get-tuple-element.64), channel_id=1, source_target_pairs={{0,1},{1,0},{2,3},{3,2},{4,5},{5,4},{6,7},{7,6},{8,9},{9,8},{10,11... | collective-permute-start | bytes 663560 | tf_op jit(solution)/shard_map/ppermute | solution.py:398
  86.8 53.5 %collective-permute-start.18 = (bf16[196,8,384]{2,1,0:T(8,128)(2,1)}, bf16[196,8,384]{2,1,0:T(8,128)(2,1)S(1)}, u32[]{:S(2)}, u32[]{:S(2)}) collective-permute-start(bf16[196,8,384]{2,1,0:T(8,128)(2,1)} %get-tuple-element.50.args_19_), channel_id=1, source_target_pairs={{0,1},{1,0},{2,3},{3,2},{4,5},{5,4},{6,7},{7,6},{8,9},{9,8},{10,11... | collective-permute-start | bytes 3612680 | tf_op jit(solution)/shard_map/ppermute | solution.py:398
  87.4 52.9 %collective-permute-start.19 = (bf16[98,8,384]{2,1,0:T(8,128)(2,1)}, bf16[98,8,384]{2,1,0:T(8,128)(2,1)S(1)}, u32[]{:S(2)}, u32[]{:S(2)}) collective-permute-start(bf16[98,8,384]{2,1,0:T(8,128)(2,1)} %get-tuple-element.51.args_20_), channel_id=1, source_target_pairs={{0,1},{1,0},{2,3},{3,2},{4,5},{5,4},{6,7},{7,6},{8,9},{9,8},{10,11... | collective-permute-start | bytes 1806344 | tf_op jit(solution)/shard_map/ppermute | solution.py:398
  88.9 51.4 %all-to-all-start = ((bf16[8,2,2,48,384]{4,3,2,1,0:T(8,128)(2,1)}), bf16[8,2,2,48,384]{4,3,2,1,0:T(8,128)(2,1)}, u32[]{:S(2)}, u32[]{:S(2)}) async-start(bf16[8,2,2,48,384]{4,3,2,1,0:T(8,128)(2,1)} %get-tuple-element.57), calls=%async_computation | async-start | bytes 2359296 | tf_op jit(solution)/shard_map/all_to_all | solution.py:588
  93.3 40.4 %copy-start.6 = (bf16[2,216,256]{2,1,0:T(8,128)(2,1)S(1)}, bf16[2,216,256]{2,1,0:T(8,128)(2,1)}, u32[]{:S(2)}) copy-start(bf16[2,216,256]{2,1,0:T(8,128)(2,1)} %get-tuple-element.63) | copy-start | bytes 663556
  133.7 14.3 %copy-start.5 = (bf16[4,2,48,384]{3,2,1,0:T(8,128)(2,1)S(1)}, bf16[4,2,48,384]{3,2,1,0:T(8,128)(2,1)}, u32[]{:S(2)}) copy-start(bf16[4,2,48,384]{3,2,1,0:T(8,128)(2,1)} %get-tuple-element.60) | copy-start | bytes 884740
  133.7 16.7 %copy-start.4 = (bf16[4,2,48,384]{3,2,1,0:T(8,128)(2,1)S(1)}, bf16[4,2,48,384]{3,2,1,0:T(8,128)(2,1)}, u32[]{:S(2)}) copy-start(bf16[4,2,48,384]{3,2,1,0:T(8,128)(2,1)} %get-tuple-element.58) | copy-start | bytes 884740
  134.8 1.4 collective-permute-start.28
  135.0 1.4 collective-permute-start.30
  136.4 5.4 %collective-permute-start.29 = (bf16[216,256]{1,0:T(8,128)(2,1)S(1)}, bf16[216,256]{1,0:T(8,128)(2,1)S(1)}, u32[]{:S(2)}, u32[]{:S(2)}) collective-permute-start(bf16[216,256]{1,0:T(8,128)(2,1)S(1)} %get-tuple-element.93), channel_id=1, source_target_pairs={{0,8},{4,12},{8,0},{12,4},{16,24},{20,28},{24,16},{28,20},{1,9},{5... | collective-permute-start | bytes 331784 | tf_op jit(solution)/shard_map/ppermute | solution.py:398
  138.1 25.0 %collective-permute-start.34 = (bf16[98,8,384]{2,1,0:T(8,128)(2,1)}, bf16[98,8,384]{2,1,0:T(8,128)(2,1)S(1)}, u32[]{:S(2)}, u32[]{:S(2)}) collective-permute-start(bf16[98,8,384]{2,1,0:T(8,128)(2,1)} %get-tuple-element.52.args_21_), channel_id=1, source_target_pairs={{0,1},{1,0},{2,3},{3,2},{4,5},{5,4},{6,7},{7,6},{8,9},{9,8},{10,11... | collective-permute-start | bytes 1806344 | tf_op jit(solution)/shard_map/ppermute | solution.py:398
  138.8 4.8 %collective-permute-start.31 = (bf16[216,256]{1,0:T(8,128)(2,1)S(1)}, bf16[216,256]{1,0:T(8,128)(2,1)S(1)}, u32[]{:S(2)}, u32[]{:S(2)}) collective-permute-start(bf16[216,256]{1,0:T(8,128)(2,1)S(1)} %get-tuple-element.94), channel_id=1, source_target_pairs={{0,16},{4,20},{8,24},{12,28},{16,0},{20,4},{24,8},{28,12},{1,17},{... | collective-permute-start | bytes 331784 | tf_op jit(solution)/shard_map/ppermute | solution.py:398
  140.3 7.0 %collective-permute-start.22 = (bf16[4,2,48,384]{3,2,1,0:T(8,128)(2,1)}, bf16[4,2,48,384]{3,2,1,0:T(8,128)(2,1)}, u32[]{:S(2)}, u32[]{:S(2)}) collective-permute-start(bf16[4,2,48,384]{3,2,1,0:T(8,128)(2,1)} %get-tuple-element.61), channel_id=1, source_target_pairs={{0,4},{4,0},{8,12},{12,8},{16,20},{20,16},{24,28},{28,24},{1,5},{5... | collective-permute-start | bytes 884744 | tf_op jit(solution)/shard_map/ppermute | solution.py:398
  141.8 18.8 %collective-permute-start.32 = (bf16[216,256]{1,0:T(8,128)(2,1)S(1)}, bf16[216,256]{1,0:T(8,128)(2,1)S(1)}, u32[]{:S(2)}, u32[]{:S(2)}) collective-permute-start(bf16[216,256]{1,0:T(8,128)(2,1)S(1)} %add_convert_fusion.3), channel_id=1, source_target_pairs={{0,16},{4,20},{8,24},{12,28},{16,0},{20,4},{24,8},{28,12},{1,17},{... | collective-permute-start | bytes 331784 | tf_op jit(solution)/shard_map/ppermute | solution.py:398
  143.6 5.4 %collective-permute-start.20 = (bf16[4,2,48,384]{3,2,1,0:T(8,128)(2,1)}, bf16[4,2,48,384]{3,2,1,0:T(8,128)(2,1)}, u32[]{:S(2)}, u32[]{:S(2)}) collective-permute-start(bf16[4,2,48,384]{3,2,1,0:T(8,128)(2,1)} %get-tuple-element.59), channel_id=1, source_target_pairs={{0,4},{4,0},{8,12},{12,8},{16,20},{20,16},{24,28},{28,24},{1,5},{5... | collective-permute-start | bytes 884744 | tf_op jit(solution)/shard_map/ppermute | solution.py:398
  143.6 19.5 %collective-permute-start.33 = (bf16[216,256]{1,0:T(8,128)(2,1)S(1)}, bf16[216,256]{1,0:T(8,128)(2,1)S(1)}, u32[]{:S(2)}, u32[]{:S(2)}) collective-permute-start(bf16[216,256]{1,0:T(8,128)(2,1)S(1)} %add_convert_fusion.1), channel_id=1, source_target_pairs={{0,8},{4,12},{8,0},{12,4},{16,24},{20,28},{24,16},{28,20},{1,9},{5... | collective-permute-start | bytes 331784 | tf_op jit(solution)/shard_map/ppermute | solution.py:398
  147.3 15.9 %collective-permute-start.26 = (bf16[2,2,48,384]{3,2,1,0:T(8,128)(2,1)}, bf16[2,2,48,384]{3,2,1,0:T(8,128)(2,1)S(1)}, u32[]{:S(2)}, u32[]{:S(2)}) collective-permute-start(bf16[2,2,48,384]{3,2,1,0:T(8,128)(2,1)} %reduce_sum.12), channel_id=1, source_target_pairs={{0,1},{1,0},{2,3},{3,2},{4,5},{5,4},{6,7},{7,6},{8,9},{9,8},{10,11... | collective-permute-start | bytes 442376 | tf_op jit(solution)/shard_map/ppermute | solution.py:398
  149.0 5.8 %collective-permute-start.23 = (bf16[2,2,48,384]{3,2,1,0:T(8,128)(2,1)S(1)}, bf16[2,2,48,384]{3,2,1,0:T(8,128)(2,1)S(1)}, u32[]{:S(2)}, u32[]{:S(2)}) collective-permute-start(bf16[2,2,48,384]{3,2,1,0:T(8,128)(2,1)S(1)} %slice.100), channel_id=1, source_target_pairs={{0,16},{4,20},{8,24},{12,28},{16,0},{20,4},{24,8},{28,12},{1,17},{... | collective-permute-start | bytes 442376 | tf_op jit(solution)/shard_map/ppermute | solution.py:398
  154.8 5.1 %collective-permute-start.21 = (bf16[2,2,48,384]{3,2,1,0:T(8,128)(2,1)S(1)}, bf16[2,2,48,384]{3,2,1,0:T(8,128)(2,1)S(1)}, u32[]{:S(2)}, u32[]{:S(2)}) collective-permute-start(bf16[2,2,48,384]{3,2,1,0:T(8,128)(2,1)S(1)} %slice.101), channel_id=1, source_target_pairs={{0,8},{4,12},{8,0},{12,4},{16,24},{20,28},{24,16},{28,20},{1,9},{5... | collective-permute-start | bytes 442376 | tf_op jit(solution)/shard_map/ppermute | solution.py:398
  159.9 4.4 %collective-permute-start.25 = (bf16[1,2,48,384]{3,2,1,0:T(8,128)(2,1)S(1)}, bf16[1,2,48,384]{3,2,1,0:T(8,128)(2,1)S(1)}, u32[]{:S(2)}, u32[]{:S(2)}) collective-permute-start(bf16[1,2,48,384]{3,2,1,0:T(8,128)(2,1)S(1)} %slice.102), channel_id=1, source_target_pairs={{0,8},{4,12},{8,0},{12,4},{16,24},{20,28},{24,16},{28,20},{1,9},{5... | collective-permute-start | bytes 221192 | tf_op jit(solution)/shard_map/ppermute | solution.py:398
  160.7 4.7 %collective-permute-start.24 = (bf16[1,2,48,384]{3,2,1,0:T(8,128)(2,1)S(1)}, bf16[1,2,48,384]{3,2,1,0:T(8,128)(2,1)S(1)}, u32[]{:S(2)}, u32[]{:S(2)}) collective-permute-start(bf16[1,2,48,384]{3,2,1,0:T(8,128)(2,1)S(1)} %slice.103), channel_id=1, source_target_pairs={{0,16},{4,20},{8,24},{12,28},{16,0},{20,4},{24,8},{28,12},{1,17},{... | collective-permute-start | bytes 221192 | tf_op jit(solution)/shard_map/ppermute | solution.py:398

commit v2 on v1

--- a/solution.py
+++ b/solution.py
@@ -37,8 +37,19 @@
         self.rows = round_up(self.patches, 8)
         self.depth = round_up(self.patches + 2, 16)
         self.m = STEP * self.rows
-        self.small = self.rows + 16
+        self.tall = round_up(-(-2 * self.rows // 3), 8)
+        self.small = self.tall + 8
+        self.slot = self.layers * self.shard
         self.blocks = self.shard % 16 == 0 and self.own % 128 == 0
+
+
+def sent_spots(sz):
+    p, cut = sz.patches, sz.patches // 2
+    return ((0, 0, p), (0, p, p + cut), (1, 0, p - cut))
+
+
+def first_group(alone, meta):
+    return meta[0] if alone else 2
 
 
 def kernel_body(sz, kept, names, *args):
@@ -52,30 +63,35 @@
     pair = 2 * rows
     blocks = [slice(i, min(i + pair, m)) for i in range(0, m, pair)]
     lane = lax.broadcasted_iota(jnp.int32, (1, depth), 1)
-    columns = pl.ds(pl.multiple_of(meta[1] * kept, 128), kept)
-    mine = pl.ds(pl.multiple_of(meta[2] * sz.own, 128), sz.own)
+    columns = pl.ds(pl.multiple_of(meta[1 if alone else 2] * kept, 128), kept)
+    mine = pl.ds(pl.multiple_of(meta[0] * sz.own, 128), sz.own)
     theirs = pl.ds(pl.multiple_of(meta[3] * sz.own, 128), sz.own)
     x, grad, gw = r["x"], r["grad"], r["gw"]
 
-    group = pl.ds(pl.multiple_of(meta[0] * GROUP, GROUP), GROUP)
+    group = pl.ds(pl.multiple_of(first_group(alone, meta) * GROUP, GROUP), GROUP)
     buffers = {"tok": r["tokb"], "cot": r["cotb"]}
 
     cut = patches // 2
     results = (("out", "tok", 0, patches), ("tgrad", "cot", 0, cut), ("tgrad", "cot", cut, patches))
+    spots = sent_spots(sz)
 
     def deliver(i):
         name, source, start, stop = results[i]
-        place = r[f"{name}{i}"] if alone else r[name].at[start:stop, group, :]
+        if alone:
+            place = r[f"sent{spots[i][0]}"].at[spots[i][1] : spots[i][2]]
+        else:
+            place = r[name].at[start:stop, group, :]
         return pltpu.make_async_copy(buffers[source].at[start:stop], place, r["moved"].at[i])
 
     def bring(i):
         name, _, start, stop = results[i]
         place = r["pass_" + name].at[start:stop]
-        return pltpu.make_async_copy(r[f"own_{name}{i}"], place, r["passed"].at[i])
+        source = r[f"own{spots[i][0]}"].at[spots[i][1] : spots[i][2]]
+        return pltpu.make_async_copy(source, place, r["passed"].at[i])
 
     def pass_on(i):
         name, _, start, stop = results[i]
-        at = pl.ds(pl.multiple_of(meta[2] * GROUP, GROUP), GROUP)
+        at = pl.ds(pl.multiple_of(meta[0] * GROUP, GROUP), GROUP)
         source, place = r["pass_" + name].at[start:stop], r[name].at[start:stop, at, :]
         return pltpu.make_async_copy(source, place, r["passed"].at[i])
 
@@ -111,6 +127,22 @@
                 bring(i).start()
         for name in ("gwc", "gsum", "gb1") + (("gw",) if alone else ()):
             r[name][...] = jnp.zeros_like(r[name])
+        r["keep"][...] = jnp.zeros_like(r["keep"])
+        first_image = first_group(alone, meta) * GROUP
+        for g in range(GROUP):
+            r["keep"][g, :, :patches] = r["masks"][pl.ds(first_image + g, 1), :].astype(F32)
+        wc = r["wc"]
+        wc[...] = jnp.zeros_like(wc)
+        r["bias"][...] = jnp.zeros_like(r["bias"])
+        for l in range(layers):
+            r["bias"][:, :patches] = jnp.broadcast_to(r["cb"][l : l + 1, :], (128, patches))
+            column = r["bias"][...].T[:rows, : depth - 128]
+            high = column.astype(BF)
+            low = (column - high.astype(F32)).astype(BF)
+            wc[l, :patches, :patches] = r["cw"][l]
+            at = lane[:, 128:]
+            extra = jnp.where(at == patches, high, jnp.where(at == patches + 1, low, 0.0))
+            wc[l, :, 128:] = wc[l, :, 128:] + extra.astype(BF)
         to_staging("tok")
         to_staging("cot")
         for l in range(layers):
@@ -127,6 +159,9 @@
 
     def weight(i, l):
         return r["w"][i, l]
+
+    def keep_of(g):
+        return r["keep"][step * STEP + g]
 
     def row(name, l, k):
         return r[name][l, k : k + 1, :]
@@ -166,7 +201,7 @@
             if depth > rows:
                 tail = jnp.concatenate([tail, jnp.ones((depth - rows, sz.width), F32)], axis=0)
             mixed[l, g, whole:, :] = tail.astype(BF)
-            wk = r["wc"][l] * jnp.where(lane < patches, r["keep"][g], 1.0).astype(BF)
+            wk = r["wc"][l] * jnp.where(lane < patches, keep_of(g), 1.0).astype(BF)
             c = dot(wk, mixed[l, g], NN)
             crossed[l, g, :rows, :] = c.astype(BF)
             mid[l, image(g), :] = x_in + row("ls", l, 0) * c
@@ -224,7 +259,7 @@
             grad[at, :] += row("scale", l, 1) * normed_grad
         for g in range(STEP):
             at = image(g)
-            keep = r["keep"][g]
+            keep = keep_of(g)
             mg = grad[at, :]
             add(l, LS0, mg * r["crossed"][l, g, :rows, :].astype(F32))
             cg = (row("ls", l, 0) * mg).astype(BF)
@@ -245,10 +280,19 @@
                 sums = [jnp.sum(r["gsum"][l, k], axis=0, keepdims=True) for k in range(B1)]
                 sums.append(jnp.sum(r["gb1"][l, :, wanted], axis=0, keepdims=True))
                 table = jnp.concatenate(sums, axis=0)
-                table = jnp.pad(table, ((0, 0), (0, 512 - sz.width)))
-                gwc = jnp.pad(r["gwc"][l], ((0, 0), (0, 256 - depth)))
-                full = jnp.concatenate([gwc, table[:, :256], table[:, 256:]], axis=0)
-                ref[l] = full.astype(BF)
+                low = r["gwc"][l, :, :128]
+                high = jnp.pad(r["gwc"][l, :, 128:], ((0, 0), (0, 256 - depth)))
+                a, b = sz.tall, 2 * sz.tall - rows
+                last_part = jnp.pad(high[b:], ((0, 3 * a - 2 * rows), (0, 0)))
+                middle = jnp.concatenate([low[a:], high[:b]], axis=0)
+                wide = jnp.concatenate([low[:a], middle, last_part], axis=1)
+                full = jnp.concatenate([wide, table], axis=0)
+                if ref.shape[1] == 8:
+                    n = sz.small // 8
+                    full = full.reshape(n, 8, sz.width)
+                    ref[l * n : (l + 1) * n] = full.astype(BF)
+                else:
+                    ref[l] = full.astype(BF)
 
         from_staging("tok")
         deliver(0).start()
@@ -258,7 +302,9 @@
 
         if alone:
             write_small(r["small"], mine)
-            write_small(r["send"], theirs)
+            write_small(r["sends"], theirs)
+            tail = spots[1][2]
+            pltpu.make_async_copy(r["sends"], r["sent0"].at[tail:], r["moved"].at[3]).start()
             for i in range(2):
                 for l in range(layers):
                     r["own"][i, l] = gw[i, l, :, mine]
@@ -276,14 +322,18 @@
                         at = pl.ds(pl.multiple_of(at, 16), sz.shard)
                         ref = r[f"stay{i}"] if k < n else r[f"leave{i}"]
                         for l in range(layers):
-                            ref[k % n, l] = gw[i, l, at, :].astype(BF)
+                            to = (k % n) * sz.slot + l * sz.shard
+                            ref[to : to + sz.shard, :] = gw[i, l, at, :].astype(BF)
                 else:
                     for l in range(layers):
-                        r[f"stay{i}"][0, l] = gw[i, l].astype(BF)
+                        r[f"stay{i}"][l * sz.width : (l + 1) * sz.width, :] = gw[i, l].astype(BF)
             for i in range(3):
                 pass_on(i).wait()
         for i in range(3):
             deliver(i).wait()
+        if alone:
+            tail = spots[1][2]
+            pltpu.make_async_copy(r["sends"], r["sent0"].at[tail:], r["moved"].at[3]).wait()
 
 
 def run(sz, alone, meta, common, weights, first=None):
@@ -295,7 +345,7 @@
     images = (sz.patches, GROUP, w)
 
     group_spec = pl.BlockSpec(
-        images, lambda i, meta: (0, meta[0], 0), pipeline_mode=pl.Buffered(1)
+        images, lambda i, meta: (0, first_group(alone, meta), 0), pipeline_mode=pl.Buffered(1)
     )
 
     def fixed_spec(block):
@@ -303,13 +353,11 @@
             block, lambda i, meta: (0,) * len(block), pipeline_mode=pl.Buffered(1)
         )
 
-    keep_spec = pl.BlockSpec((STEP, 1, sz.depth), lambda i, meta: (meta[0] * steps + i, 0, 0))
     ins = [
         ("tok", common["tok"], group_spec),
         ("cot", common["cot"], group_spec),
-        ("keep", common["keep"], keep_spec),
     ]
-    for name in ("scale", "shift", "ls", "wc", "b1", "b2"):
+    for name in ("masks", "scale", "shift", "ls", "cw", "cb", "b1", "b2"):
         ins.append((name, common[name], vmem))
     scratch = []
     if sz.blocks:
@@ -323,30 +371,30 @@
         ins.append(("w", weights, vmem))
     if not alone:
         ins.append(("carry", first["own"], anywhere))
-        for name in ("out0", "tgrad1", "tgrad2"):
-            ins.append(("own_" + name, first[name], anywhere))
+        for i in range(2):
+            ins.append((f"own{i}", first[f"sent{i}"], anywhere))
         scratch.append(("passed", pltpu.SemaphoreType.DMA((3,))))
         scratch.append(("pass_out", pltpu.VMEM(images, BF)))
         scratch.append(("pass_tgrad", pltpu.VMEM(images, BF)))
         scratch.append(("carried", pltpu.SemaphoreType.DMA))
 
     if alone:
-        cut = sz.patches // 2
-        parts = (("out0", sz.patches), ("tgrad1", cut), ("tgrad2", sz.patches - cut))
+        spots, packed = sent_spots(sz), layers * sz.small // GROUP
+        parts = (("sent0", spots[1][2] + packed), ("sent1", spots[2][2]))
         outs = [(name, (n, GROUP, w), BF, anywhere) for name, n in parts]
+        scratch.append(("sends", pltpu.VMEM((packed, GROUP, w), BF)))
     else:
         outs = [(name, (sz.patches, sz.count, w), BF, anywhere) for name in ("out", "tgrad")]
-    small = (layers, sz.small, 256)
+    small = (layers, sz.small, w)
     block = (layers, sz.shard, sz.own) if sz.blocks else (layers, w, sz.own)
     n_blocks = sz.n_dp if sz.blocks else 1
     outs.append(("small", small, BF, fixed_spec(small)))
     if not alone:
-        part = ((n_blocks + 1) // 2,) + block
+        part = ((n_blocks + 1) // 2 * block[0] * block[1], sz.own)
         for name in ("stay0", "stay1") + (("leave0", "leave1") if sz.blocks else ()):
             outs.append((name, part, BF, fixed_spec(part)))
     else:
         outs.append(("blocks", (n_blocks, 2) + block, BF, fixed_spec((n_blocks, 2) + block)))
-        outs.append(("send", small, BF, fixed_spec(small)))
         own = (2, layers, w, sz.own)
         outs.append(("own", own, F32, fixed_spec(own)))
     for name, shape, dtype in (
@@ -366,6 +414,9 @@
         ("gwc", (layers, sz.rows, sz.depth), F32),
         ("gsum", (layers, B1, 8, w), F32),
         ("gb1", (layers, 8, kept), F32),
+        ("keep", (GROUP, 1, sz.depth), F32),
+        ("wc", (layers, sz.rows, sz.depth), BF),
+        ("bias", (128, 256), F32),
         ("b1s", (layers, 1, sz.hidden), F32),
         ("b2s", (layers, 1, w), F32),
         ("tokb", images, BF),
@@ -374,7 +425,7 @@
         ("cotf", (w // 128, GROUP * sz.rows, 128), F32),
     ):
         scratch.append((name, pltpu.VMEM(shape, dtype)))
-    scratch.append(("moved", pltpu.SemaphoreType.DMA((3,))))
+    scratch.append(("moved", pltpu.SemaphoreType.DMA((4,))))
     names = ("meta",) + tuple(e[0] for e in ins + outs + scratch)
     flops = steps * m * 24 * w * sz.hidden
     results = pl.pallas_call(
@@ -421,14 +472,17 @@
     for step in range(len(bits)):
         moved = [swap(got[0], "dp", bits[step]), swap(got[1], "dp", bits[-1 - step])]
         got = [jnp.concatenate([g, v]) for g, v in zip(got, moved)]
-    other = [swap(g, "dp", 1) for g in got]
-    orders = []
+    return got
+
+
+def gather_orders(n_dp):
+    bits, orders = powers(n_dp), []
     for seq in (bits, bits[::-1]):
         order = [0]
         for b in seq:
             order += [o ^ b for o in order]
         orders.append(order + [o ^ 1 for o in order])
-    return got, other, orders
+    return orders
 
 
 def exchange_orders(n_dp):
@@ -442,76 +496,161 @@
     return result
 
 
-def scatter_step(stay, leave, bit):
-    got = swap(leave, "dp", bit)
-    return stay.astype(F32) + got.astype(F32)
-
-
-def halves(blocks):
-    n = blocks.shape[0] // 2
-    return blocks[:n], blocks[n:].astype(BF)
-
-
-def finish_body(sz, *refs):
-    (meta, keep0, keep1, got0, got1, theirs, small, got_s0, got_s1) = refs[:9]
-    sent = refs[9:12]
-    (out, tgrad, scale, shift, ls, gwc, gb, w1, b1, w2, b2, pass0, pass1, pass2, moved) = refs[14:]
-    place = pl.ds(pl.multiple_of(meta[0] * GROUP, GROUP), GROUP)
+def place_body(sz, meta, sent0, sent1, _, __, out, tgrad, pass0, pass1, pass2, moved):
+    place = pl.ds(pl.multiple_of(meta[3] * GROUP, GROUP), GROUP)
     cut = sz.patches // 2
-    spots = (out.at[:, place, :], tgrad.at[:cut, place, :], tgrad.at[cut:, place, :])
+    to = (out.at[:, place, :], tgrad.at[:cut, place, :], tgrad.at[cut:, place, :])
     brought, copies = [], []
     for i, buffer in enumerate((pass0, pass1, pass2)):
-        brought.append(pltpu.make_async_copy(sent[i], buffer, moved.at[i]))
-        copies.append(pltpu.make_async_copy(buffer, spots[i], moved.at[i]))
+        which, start, stop = sent_spots(sz)[i]
+        source = (sent0, sent1)[which].at[start:stop]
+        brought.append(pltpu.make_async_copy(source, buffer, moved.at[i]))
+        copies.append(pltpu.make_async_copy(buffer, to[i], moved.at[i]))
         brought[i].start()
-    w1[...] = keep0[0] + got0[0].astype(F32) + theirs[0].astype(F32)
-    w2[...] = keep1[0] + got1[0].astype(F32) + theirs[1].astype(F32)
     for i in range(3):
         brought[i].wait()
         copies[i].start()
-    for l, got in enumerate((got_s0, got_s1)):
-        total = small[l].astype(F32) + got[...].astype(F32)
-        gwc[:, l, :] = total[: sz.patches, : sz.patches]
-        lane = sz.patches // 128 * 128
-        gb[l : l + 1, :] = total[:, lane : lane + 128].T[
-            sz.patches - lane : sz.patches - lane + 1, : sz.patches
-        ]
-        low, high = total[sz.rows : sz.rows + 8], total[sz.rows + 8 : sz.rows + 16]
-        table = jnp.concatenate([low, high[:, : sz.width - 256]], axis=1)
+    for c in copies:
+        c.wait()
+
+
+def place_images(sz, meta, sent, out, tgrad):
+    anywhere = pl.BlockSpec(memory_space=pl.ANY)
+    whole = jax.ShapeDtypeStruct(out.shape, BF)
+    buffers = [(stop - start, GROUP, sz.width) for _, start, stop in sent_spots(sz)]
+    return pl.pallas_call(
+        functools.partial(place_body, sz),
+        grid_spec=pltpu.PrefetchScalarGridSpec(
+            num_scalar_prefetch=1,
+            grid=(),
+            in_specs=[anywhere] * 4,
+            out_specs=[anywhere] * 2,
+            scratch_shapes=[pltpu.VMEM(shape, BF) for shape in buffers]
+            + [pltpu.SemaphoreType.DMA((3,))],
+        ),
+        out_shape=[whole, whole],
+        input_output_aliases={3: 0, 4: 1},
+        compiler_params=pltpu.CompilerParams(vmem_limit_bytes=16 * 2**20),
+        cost_estimate=pl.CostEstimate(
+            flops=0, bytes_accessed=8 * out.size // 3, transcendentals=0
+        ),
+    )(meta, *sent, out, tgrad)
+
+
+def phase_body(sz, n, *refs):
+    stays, gots, smalls, got_smalls = refs[:2], refs[2:4], refs[4:6], refs[6:8]
+    keeps, pays = refs[8:10], refs[10:12]
+    cut = n // 2 * sz.slot
+    for i in range(2):
+        total = stays[i][: n * sz.slot].astype(F32) + gots[i][: n * sz.slot].astype(F32)
+        keeps[i][...] = total[:cut]
+        pays[i][: n * sz.slot - cut] = total[cut:].astype(BF)
+        own = smalls[i][smalls[i].shape[0] - sz.small :].astype(F32)
+        other = got_smalls[i][got_smalls[i].shape[0] - sz.small :].astype(F32)
+        pays[i][n * sz.slot - cut :] = (own + other).astype(BF)
+
+
+def first_phase_body(sz, n, *refs):
+    small, got_small, parts, total = refs[4], refs[5], refs[6], refs[11]
+    smalls, got_smalls = ([v.at[i] for i in range(2)] for v in (small, got_small))
+    phase_body(sz, n, *refs[:4], *smalls, *got_smalls, *refs[7:11])
+    for i in range(2):
+        v = parts[0, i].astype(F32)
+        for k in range(1, sz.n_dp):
+            v = v + parts[k, i].astype(F32)
+        total[i] = v.astype(BF).reshape(sz.slot, sz.own)
+
+
+def first_phase(sz, n, stays, gots, small, got_small, parts):
+    if sz.blocks:
+        cut = n // 2 * sz.slot
+        keep = jax.ShapeDtypeStruct((cut, sz.own), F32)
+        pay = jax.ShapeDtypeStruct((n * sz.slot - cut + sz.small, sz.own), BF)
+        total = jax.ShapeDtypeStruct((2, sz.slot, sz.own), BF)
+        out = pl.pallas_call(
+            functools.partial(first_phase_body, sz, n),
+            in_specs=[pl.BlockSpec(memory_space=pltpu.VMEM)] * 7,
+            out_specs=[pl.BlockSpec(memory_space=pltpu.VMEM)] * 5,
+            out_shape=[keep, keep, pay, pay, total],
+            compiler_params=pltpu.CompilerParams(vmem_limit_bytes=32 * 2**20),
+        )(*stays, *gots, small, got_small, parts)
+        return out[:2], out[2:4], out[4]
+    keeps, pays = phase(sz, n, stays, gots, small, got_small)
+    return keeps, pays, parts.astype(F32).sum(axis=0).astype(BF).reshape(2, sz.slot, sz.own)
+
+
+def phase(sz, n, stays, gots, smalls, got_smalls):
+    if sz.blocks:
+        cut = n // 2 * sz.slot
+        keep = jax.ShapeDtypeStruct((cut, sz.own), F32)
+        pay = jax.ShapeDtypeStruct((n * sz.slot - cut + sz.small, sz.own), BF)
+        out = pl.pallas_call(
+            functools.partial(phase_body, sz, n),
+            in_specs=[pl.BlockSpec(memory_space=pltpu.VMEM)] * 8,
+            out_specs=[pl.BlockSpec(memory_space=pltpu.VMEM)] * 4,
+            out_shape=[keep, keep, pay, pay],
+            compiler_params=pltpu.CompilerParams(vmem_limit_bytes=32 * 2**20),
+        )(*stays, *gots, *smalls, *got_smalls)
+        return out[:2], out[2:]
+    keeps, pays = [], []
+    for i in range(2):
+        total = stays[i].astype(F32) + gots[i][: n * sz.slot].astype(F32)
+        cut = n // 2 * sz.slot
+        own, other = smalls[i][-sz.small :].astype(F32), got_smalls[i][-sz.small :].astype(F32)
+        keeps.append(total[:cut])
+        pays.append(jnp.concatenate([total[cut:], own + other]).astype(BF))
+    return keeps, pays
+
+
+def finish_body(sz, *refs):
+    keeps, pays, gots, theirs = refs[0:2], refs[2:4], refs[4:6], refs[6]
+    (scale, shift, ls, gwc, gb, w1, b1, w2, b2) = refs[7:]
+    for i, ref in enumerate((w1, w2)):
+        total = keeps[i][...] + gots[i][: keeps[i].shape[0]].astype(F32)
+        ref[...] = total + theirs[i].astype(F32)
+    for l in range(2):
+        at = pays[l].shape[0] - sz.small
+        total = pays[l][at:].astype(F32) + gots[l][at:].astype(F32)
+        a, b = sz.tall, 2 * sz.tall - sz.rows
+        low = jnp.concatenate([total[:a, :128], total[: sz.rows - a, 128:256]], axis=0)
+        high = jnp.concatenate([total[sz.rows - a : a, 128:256], total[: sz.rows - b, 256:]], axis=0)
+        gwc[:, l, :] = jnp.concatenate([low, high], axis=1)[: sz.patches, : sz.patches]
+        lane = sz.patches - 128
+        gb[l : l + 1, :] = high.T[lane : lane + 1, : sz.patches]
+        table = total[a : a + 8]
         for ref, kinds in ((scale, (S0, S1)), (shift, (T0, T1)), (ls, (LS0, LS1))):
             for k, kind in enumerate(kinds):
                 ref[l, k : k + 1, :] = table[kind : kind + 1]
         b1[l : l + 1, :] = table[B1 : B1 + 1]
         b2[l : l + 1, :] = table[B2 : B2 + 1]
-    for c in copies:
-        c.wait()
-
-
-def finish(sz, meta, keep, got, theirs, small, got_small, sent, out, tgrad):
+
+
+def finish(sz, keeps, pays, gots, theirs):
     vmem = pl.BlockSpec(memory_space=pltpu.VMEM)
-    anywhere = pl.BlockSpec(memory_space=pl.ANY)
     layers, w, p = sz.layers, sz.width, sz.patches
-    vec = (layers, 2, w)
-    shapes = [vec, vec, vec, (p, layers, p), (layers, p)]
-    shapes += [(layers, sz.shard, sz.own), (layers, sz.own)] + [
-        (layers, sz.shard, sz.own),
-        (layers, w),
-    ]
-    whole = jax.ShapeDtypeStruct(out.shape, BF)
-    return pl.pallas_call(
-        functools.partial(finish_body, sz),
-        grid_spec=pltpu.PrefetchScalarGridSpec(
-            num_scalar_prefetch=1,
-            grid=(),
-            in_specs=[vmem] * 8 + [anywhere] * 5,
-            out_specs=[anywhere] * 2 + [vmem] * 9,
-            scratch_shapes=[pltpu.VMEM(v.shape, BF) for v in sent]
-            + [pltpu.SemaphoreType.DMA((3,))],
-        ),
-        out_shape=[whole, whole] + [jax.ShapeDtypeStruct(s, F32) for s in shapes],
-        input_output_aliases={12: 0, 13: 1},
-        compiler_params=pltpu.CompilerParams(vmem_limit_bytes=32 * 2**20),
-    )(meta, *keep, *got, theirs, small, *got_small, *sent, out, tgrad)
+    vec, rows = (layers, 2, w), (sz.slot, sz.own)
+    if sz.slot % 16:
+        gap = ((0, round_up(sz.slot, 16) - sz.slot), (0, 0))
+        pays, gots = (
+            [jnp.concatenate([jnp.pad(v[: sz.slot], gap), v[sz.slot :]]) for v in vs]
+            for vs in (pays, gots)
+        )
+        keeps = [jnp.pad(v, gap) for v in keeps]
+        theirs = jnp.pad(theirs, ((0, 0),) + gap)
+        rows = (round_up(sz.slot, 16), sz.own)
+    shapes = [vec, vec, vec, (p, layers, p), (layers, p), rows, (layers, sz.own), rows, (layers, w)]
+    result = list(
+        pl.pallas_call(
+            functools.partial(finish_body, sz),
+            in_specs=[vmem] * 7,
+            out_specs=[vmem] * 9,
+            out_shape=[jax.ShapeDtypeStruct(s, F32) for s in shapes],
+            compiler_params=pltpu.CompilerParams(vmem_limit_bytes=32 * 2**20),
+        )(*keeps, *pays, *gots, theirs)
+    )
+    for i in (5, 7):
+        result[i] = result[i][: sz.slot].reshape(layers, sz.shard, sz.own)
+    return result
 
 
 def on_device(
@@ -534,18 +673,17 @@
     me, hid = lax.axis_index("dp"), lax.axis_index("hid")
     half = hid % 2
 
-    bias_hi = cross_bias.astype(BF)
-    bias_lo = (cross_bias - bias_hi.astype(F32)).astype(BF)
-    wc = jnp.concatenate([crosspatch_weight, bias_hi[:, :, None], bias_lo[:, :, None]], axis=2)
-    wc = jnp.pad(wc, ((0, 0), (0, sz.rows - patches), (0, sz.depth - patches - 2)))
-    keep = jnp.pad(masks.astype(F32)[:, None, :], ((0, 0), (0, 0), (0, sz.depth - patches)))
+    orders, exchanges = gather_orders(n_dp), exchange_orders(n_dp)
+    places = [half, hid // 2, hid, 1 - half] + [me ^ k for k in orders[0] + orders[1]]
+    places += [me ^ k for k in exchanges[0][1] + exchanges[1][1]]
+    meta = jnp.stack(places).astype(jnp.int32)
 
     weights = []
     for l in range(layers):
-        full = gather_columns(sz, fc1_weight[l], fc2_weight[l])
+        got = gather_rows(sz, gather_columns(sz, fc1_weight[l], fc2_weight[l]))
         if l == 0:
-            full, wc, keep = lax.optimization_barrier((full, wc, keep))
-        got, other, orders = gather_rows(sz, full)
+            got, meta = lax.optimization_barrier((got, meta))
+        other = [swap(g, "dp", 1) for g in got]
         if sz.blocks:
             weights.append([(got[i], other[i]) for i in range(2)])
         else:
@@ -562,24 +700,17 @@
     common = {
         "tok": tokens.transpose(1, 0, 2),
         "cot": cotangent.transpose(1, 0, 2),
-        "keep": keep,
+        "masks": masks,
         "scale": aff_scale,
         "shift": aff_shift,
         "ls": layer_scale,
-        "wc": wc,
+        "cw": crosspatch_weight,
+        "cb": cross_bias,
         "b1": fc1_bias,
         "b2": fc2_bias,
     }
-    exchanges = exchange_orders(n_dp)
-    places = [me ^ k for k in orders[0] + orders[1]]
-    places += [me ^ k for k in exchanges[0][1] + exchanges[1][1]]
-
-    def meta(first, column):
-        return jnp.stack([first, column, half, 1 - half] + places).astype(jnp.int32)
-
-    first = run(sz, True, meta(half, hid // 2), common, weights)
-    sent = [swap(first[name], "hid", 1) for name in ("out0", "tgrad1", "tgrad2")]
-    sent_small = swap(first["send"], "hid", 1)
+    first = run(sz, True, meta, common, weights)
+    sent = [swap(first[f"sent{i}"], "hid", 1) for i in range(2)]
 
     theirs = first["blocks"]
     if not sz.blocks:
@@ -587,41 +718,31 @@
         theirs = jnp.moveaxis(theirs, 2, 0)
     theirs = lax.all_to_all(theirs, "dp", split_axis=0, concat_axis=0, tiled=True)
 
-    rest = run(sz, False, meta(jnp.int32(2), hid), common, weights, first)
-    small_rest = rest["small"]
+    rest = run(sz, False, meta, common, weights, first)
+    stays = [rest[f"stay{i}"] for i in range(2)]
     if sz.blocks:
-        gw = [(rest[f"stay{i}"], rest[f"leave{i}"]) for i in range(2)]
+        leaves = [rest[f"leave{i}"] for i in range(2)]
     else:
-        gw = [rest[f"stay{i}"].reshape(layers, n_dp, sz.shard, sz.own) for i in range(2)]
-        gw = [jnp.moveaxis(g, 1, 0)[jnp.array(e[1]) ^ me] for g, e in zip(gw, exchanges)]
-        gw = [halves(g) for g in gw]
-    gw, theirs, sent[:2] = lax.optimization_barrier((gw, theirs, sent[:2]))
-    alone_small = first["small"].astype(F32) + sent_small.astype(F32)
-    small = (alone_small + small_rest.astype(F32)).astype(BF)
-    small = [small[l] for l in range(layers)]
-    phases = len(exchanges[0][0])
-    for k in range(phases - 1):
-        gw = [scatter_step(*gw[i], exchanges[i][0][k]) for i in range(2)]
-        for l in range(layers):
-            other = swap(small[l], "dp", exchanges[l % 2][0][k])
-            small[l] = (small[l].astype(F32) + other.astype(F32)).astype(BF)
-        if k == 0:
-            theirs = swap(theirs.astype(F32).sum(axis=0).astype(BF), "hid", 1)
-        gw = [halves(g) for g in gw]
-    got = [swap(gw[i][1], "dp", exchanges[i][0][-1]) for i in range(2)]
-    got_small = [swap(small[l], "dp", exchanges[l % 2][0][-1]) for l in range(layers)]
-    out, tgrad, scale, shift, ls, gwc, gb, w1, b1, w2, b2 = finish(
-        sz,
-        jnp.stack([1 - half]).astype(jnp.int32),
-        [g[0] for g in gw],
-        got,
-        theirs,
-        jnp.stack(small),
-        got_small,
-        sent,
-        rest["out"],
-        rest["tgrad"],
-    )
+        whole = [g.reshape(layers, n_dp, sz.shard, sz.own) for g in stays]
+        whole = [jnp.moveaxis(g, 1, 0)[jnp.array(e[1]) ^ me] for g, e in zip(whole, exchanges)]
+        whole = [g.reshape(2, -1, sz.own) for g in whole]
+        stays, leaves = [g[0] for g in whole], [g[1] for g in whole]
+    leaves, theirs, sent[0] = lax.optimization_barrier((leaves, theirs, sent[0]))
+    small = sent[0][sent_spots(sz)[1][2] :].reshape(layers, sz.small, sz.width)
+    small = first["small"].astype(F32) + small.astype(F32)
+    small = (small + rest["small"].astype(F32)).astype(BF)
+    got_small = swap(small, "dp", 1)
+    gots = [swap(v, "dp", 1) for v in leaves]
+    n = n_dp // 2
+    keeps, pays, theirs = first_phase(sz, n, stays, gots, small, got_small, theirs)
+    theirs = swap(theirs, "hid", 1)
+    for k in range(1, len(exchanges[0][0]) - 1):
+        n //= 2
+        gots = [swap(pays[i], "dp", exchanges[i][0][k]) for i in range(2)]
+        keeps, pays = phase(sz, n, keeps, gots, pays, gots)
+    gots = [swap(pays[i], "dp", exchanges[i][0][-1]) for i in range(2)]
+    out, tgrad = place_images(sz, meta, sent, rest["out"], rest["tgrad"])
+    scale, shift, ls, gwc, gb, w1, b1, w2, b2 = finish(sz, keeps, pays, gots, theirs)
     return (
         out.transpose(1, 0, 2),
         tgrad.transpose(1, 0, 2),

time: 169 us -> 156 us (0.923)
  starting transfers between devices: 45 us -> 35.6 us
  other arithmetic: 8.31 us -> 1.57 us
    ppermute x35 -> x28, starting transfers between devices: 40.6 us -> 31.8 us  [swap(): return lax.ppermute(x, axis, [(i, i ^ k) for i in range(n)])]
    unnamed x19 -> x27, local copies, waits for them, and re-layouts: 1.06 us -> 3.58 us
    reduce_sum x1 -> x0, other arithmetic: 2.13 us -> none  [on_device(): theirs = swap(theirs.astype(F32).sum(axis=0).astype(BF), 'hid', 1)]
    add x4 -> x0, other arithmetic: 2.1 us -> none  [scatter_step(): return stay.astype(F32) + got.astype(F32)]
    ppermute x35 -> x28, waiting for transfers between devices: 22.9 us -> 24.5 us  [swap(): return lax.ppermute(x, axis, [(i, i ^ k) for i in range(n)])]
    pallas_call x1 -> x4, Pallas kernels: 2.88 us -> 3.98 us  [the longest x1 2.53 us: place_images(): pl.pallas_call(functools.partial(place_body, sz), grid_spec=pltpu.Prefetc...]
  transfers between devices with their start and end apart: 36 -> 29, of which waited for: 14 -> 12; matrix products, arithmetic and copies ran while one was open for 7% -> 2% of each run, Pallas kernels for 24% -> 28%
where the time goes in v2:
time: 156 us
  Pallas kernels  88 us (56%)
  starting transfers between devices  35.6 us (23%)
  waiting for transfers between devices  24.5 us (16%)
  local copies, waits for them, and re-layouts  5.19 us (3%)
  other arithmetic  1.57 us (1%)
    pallas_call x2, Pallas kernels, run(): pl.pallas_call(functools.partial(kernel_body, sz, kept, names), grid_spec...  84.1 us
    ppermute x28, starting transfers between devices, swap(): return lax.ppermute(x, axis, [(i, i ^ k) for i in range(n)])  31.8 us
    ppermute x28, waiting for transfers between devices, swap(): return lax.ppermute(x, axis, [(i, i ^ k) for i in range(n)])  24.5 us
    all_to_all x1, starting transfers between devices, on_device(): lax.all_to_all(theirs, 'dp', split_axis=0, concat_axis=0, tiled=True)  3.74 us
    unnamed x27, local copies, waits for them, and re-layouts  3.58 us
  transfers between devices with their start and end apart: 29, of which 12 were waited for; matrix products, arithmetic and copies ran while one was open for 2% of the time, Pallas kernels for 28%

profile of v2, /device:TPU:0, one launch (start us, length us, event | category | flops | bytes accessed | tf_op | source)
XLA Modules:
  0.0 155.8 jit_solution(401169253835853173)
XLA Ops:
  0.6 0.8 fusion.4
  1.5 4.1 %collective-permute-start.10 = (bf16[2,48,384]{2,1,0:T(8,128)(2,1)S(1)}, bf16[2,48,384]{2,1,0:T(8,128)(2,1)S(1)}, u32[]{:S(2)}, u32[]{:S(2)}) collective-permute-start(bf16[2,48,384]{2,1,0:T(8,128)(2,1)S(1)} %pad_maximum_fusion.11), channel_id=1, source_target_pairs={{0,2},{1,3},{2,0},{3,1},{4,6},{5,7},{6,4},{7,5},{8,10},{9,11},{10,... | collective-permute-start | bytes 221192 | tf_op jit(solution)/shard_map/ppermute | solution.py:449
  5.6 1.6 %collective-permute-start.11 = (bf16[2,48,384]{2,1,0:T(8,128)(2,1)S(1)}, bf16[2,48,384]{2,1,0:T(8,128)(2,1)S(1)}, u32[]{:S(2)}, u32[]{:S(2)}) collective-permute-start(bf16[2,48,384]{2,1,0:T(8,128)(2,1)S(1)} %pad_maximum_fusion.11), channel_id=1, source_target_pairs={{0,1},{1,0},{2,3},{3,2},{4,5},{5,4},{6,7},{7,6},{8,9},{9,8},{10,11... | collective-permute-start | bytes 221192 | tf_op jit(solution)/shard_map/ppermute | solution.py:449
  7.2 3.9 %collective-permute-start = (bf16[2,48,384]{2,1,0:T(8,128)(2,1)S(1)}, bf16[2,48,384]{2,1,0:T(8,128)(2,1)S(1)}, u32[]{:S(2)}, u32[]{:S(2)}) collective-permute-start(bf16[2,48,384]{2,1,0:T(8,128)(2,1)S(1)} %pad_maximum_fusion.10), channel_id=1, source_target_pairs={{0,3},{1,2},{2,1},{3,0},{4,7},{5,6},{6,5},{7,4},{8,11},{9,10},{10,... | collective-permute-start | bytes 221192 | tf_op jit(solution)/shard_map/ppermute | solution.py:449
  11.1 0.7 stack.82.args_0_.meta
  11.8 0.6 collective-permute-start.2
  12.4 1.8 %collective-permute-done.9 = bf16[2,48,384]{2,1,0:T(8,128)(2,1)S(1)} collective-permute-done((bf16[2,48,384]{2,1,0:T(8,128)(2,1)S(1)}, bf16[2,48,384]{2,1,0:T(8,128)(2,1)S(1)}, u32[]{:S(2)}, u32[]{:S(2)}) %collective-permute-start.9) | collective-permute-done | bytes 73760 | tf_op jit(solution)/shard_map/ppermute | solution.py:449
  14.3 1.6 %collective-permute-start.15 = (bf16[1,48,1536]{2,1,0:T(8,128)(2,1)S(1)}, bf16[1,48,1536]{2,1,0:T(8,128)(2,1)S(1)}, u32[]{:S(2)}, u32[]{:S(2)}) collective-permute-start(bf16[1,48,1536]{2,1,0:T(8,128)(2,1)S(1)} %get-tuple-element.89), channel_id=1, source_target_pairs={{0,16},{4,20},{8,24},{12,28},{16,0},{20,4},{24,8},{28,12},{1,17},{... | collective-permute-start | bytes 442376 | tf_op jit(solution)/shard_map/ppermute | solution.py:449
  15.9 1.5 collective-permute-start.12
  17.4 1.6 %collective-permute-done.1 = bf16[2,48,384]{2,1,0:T(8,128)(2,1)S(1)} collective-permute-done((bf16[2,48,384]{2,1,0:T(8,128)(2,1)S(1)}, bf16[2,48,384]{2,1,0:T(8,128)(2,1)S(1)}, u32[]{:S(2)}, u32[]{:S(2)}) %collective-permute-start.1) | collective-permute-done | bytes 73760 | tf_op jit(solution)/shard_map/ppermute | solution.py:449
  19.1 1.8 %collective-permute-start.5 = (bf16[1,48,1536]{2,1,0:T(8,128)(2,1)S(1)}, bf16[1,48,1536]{2,1,0:T(8,128)(2,1)S(1)}, u32[]{:S(2)}, u32[]{:S(2)}) collective-permute-start(bf16[1,48,1536]{2,1,0:T(8,128)(2,1)S(1)} %get-tuple-element.95), channel_id=1, source_target_pairs={{0,16},{4,20},{8,24},{12,28},{16,0},{20,4},{24,8},{28,12},{1,17},{... | collective-permute-start | bytes 442376 | tf_op jit(solution)/shard_map/ppermute | solution.py:449
  20.9 1.5 collective-permute-start.3
  22.5 0.6 collective-permute-start.16
  23.1 0.4 collective-permute-start.13
  23.5 1.6 %collective-permute-done.5 = bf16[1,48,1536]{2,1,0:T(8,128)(2,1)S(1)} collective-permute-done((bf16[1,48,1536]{2,1,0:T(8,128)(2,1)S(1)}, bf16[1,48,1536]{2,1,0:T(8,128)(2,1)S(1)}, u32[]{:S(2)}, u32[]{:S(2)}) %collective-permute-start.5) | collective-permute-done | bytes 147488 | tf_op jit(solution)/shard_map/ppermute | solution.py:449
  25.1 1.9 %collective-permute-start.6 = (bf16[2,48,1536]{2,1,0:T(8,128)(2,1)S(1)}, bf16[2,48,1536]{2,1,0:T(8,128)(2,1)S(1)}, u32[]{:S(2)}, u32[]{:S(2)}) collective-permute-start(bf16[2,48,1536]{2,1,0:T(8,128)(2,1)S(1)} %pad_maximum_fusion.6), channel_id=1, source_target_pairs={{0,8},{4,12},{8,0},{12,4},{16,24},{20,28},{24,16},{28,20},{1,9},{5... | collective-permute-start | bytes 884744 | tf_op jit(solution)/shard_map/ppermute | solution.py:449
  27.0 0.7 collective-permute-done.3
  27.8 1.6 %collective-permute-start.4 = (bf16[2,48,1536]{2,1,0:T(8,128)(2,1)S(1)}, bf16[2,48,1536]{2,1,0:T(8,128)(2,1)S(1)}, u32[]{:S(2)}, u32[]{:S(2)}) collective-permute-start(bf16[2,48,1536]{2,1,0:T(8,128)(2,1)S(1)} %pad_maximum_fusion.5), channel_id=1, source_target_pairs={{0,16},{4,20},{8,24},{12,28},{16,0},{20,4},{24,8},{28,12},{1,17},{... | collective-permute-start | bytes 884744 | tf_op jit(solution)/shard_map/ppermute | solution.py:449
  29.3 4.7 %collective-permute-done.16 = bf16[2,48,1536]{2,1,0:T(8,128)(2,1)S(1)} collective-permute-done((bf16[2,48,1536]{2,1,0:T(8,128)(2,1)S(1)}, bf16[2,48,1536]{2,1,0:T(8,128)(2,1)S(1)}, u32[]{:S(2)}, u32[]{:S(2)}) %collective-permute-start.16) | collective-permute-done | bytes 294944 | tf_op jit(solution)/shard_map/ppermute | solution.py:449
  34.3 0.5 collective-permute-start.14
  34.8 3.1 %collective-permute-done.6 = bf16[2,48,1536]{2,1,0:T(8,128)(2,1)S(1)} collective-permute-done((bf16[2,48,1536]{2,1,0:T(8,128)(2,1)S(1)}, bf16[2,48,1536]{2,1,0:T(8,128)(2,1)S(1)}, u32[]{:S(2)}, u32[]{:S(2)}) %collective-permute-start.6) | collective-permute-done | bytes 294944 | tf_op jit(solution)/shard_map/ppermute | solution.py:449
  38.1 0.5 collective-permute-start.8
  38.6 0.7 copy.26.args_7_
  39.4 0.8 collective-permute-done.7.args_12_
  40.1 0.8 collective-permute-done.8.args_14_
  41.0 0.9 copy-done.12
  41.9 43.8 %shard_map.203 = (bf16[330,8,384]{2,1,0:T(8,128)(2,1)}, bf16[98,8,384]{2,1,0:T(8,128)(2,1)}, bf16[2,144,384]{2,1,0:T(8,128)(2,1)}, bf16[8,2,2,48,384]{4,3,2,1,0:T(8,128)(2,1)}, f32[2,2,384,384]{3,2,1,0:T(8,128)}) custom-call(s32[36]{0:T(128)} %stack.82.args_0_.meta, bf16[196,24,384]{2,1,0:T(8,128)(2,1)} %bitcast.26, bf16[196,24,384]{2,1,0:T(8,128)(2,1)} %bitcast.28, ...), custom_call_target="tpu_custom_call" | custom-call | flops 22649241600 | bytes 56623104 | tf_op jit(solution)/shard_map/pallas_call | solution.py:431
  85.7 2.4 %collective-permute-start.18 = (bf16[330,8,384]{2,1,0:T(8,128)(2,1)}, bf16[330,8,384]{2,1,0:T(8,128)(2,1)S(1)}, u32[]{:S(2)}, u32[]{:S(2)}) collective-permute-start(bf16[330,8,384]{2,1,0:T(8,128)(2,1)} %get-tuple-element.54.args_20_), channel_id=1, source_target_pairs={{0,1},{1,0},{2,3},{3,2},{4,5},{5,4},{6,7},{7,6},{8,9},{9,8},{10,11... | collective-permute-start | bytes 6082568 | tf_op jit(solution)/shard_map/ppermute | solution.py:449
  88.1 3.7 %all-to-all-start = ((bf16[8,2,2,48,384]{4,3,2,1,0:T(8,128)(2,1)}), bf16[8,2,2,48,384]{4,3,2,1,0:T(8,128)(2,1)S(1)}, u32[]{:S(2)}, u32[]{:S(2)}) async-start(bf16[8,2,2,48,384]{4,3,2,1,0:T(8,128)(2,1)} %get-tuple-element.58), calls=%async_computation | async-start | bytes 2359296 | tf_op jit(solution)/shard_map/all_to_all | solution.py:719
  91.9 40.3 %shard_map.204 = (bf16[196,24,384]{2,1,0:T(8,128)(2,1)}, bf16[196,24,384]{2,1,0:T(8,128)(2,1)}, bf16[2,144,384]{2,1,0:T(8,128)(2,1)}, bf16[384,384]{1,0:T(8,128)...) custom-call(s32[36]{0:T(128)} %stack.82.args_0_.meta, ...), custom_call_target="tpu_custom_call" | custom-call | flops 22649241600 | bytes 56623104 | tf_op jit(solution)/shard_map/pallas_call | solution.py:431
  132.2 0.6 collective-permute-done.18.sent0
  132.9 0.5 collective-permute-start.21
  133.4 1.0 fusion.1.refs_4_
  134.4 0.1 collective-permute-start.22
  134.5 1.7 %collective-permute-start.19 = (bf16[98,8,384]{2,1,0:T(8,128)(2,1)}, bf16[98,8,384]{2,1,0:T(8,128)(2,1)S(1)}, u32[]{:S(2)}, u32[]{:S(2)}) collective-permute-start(bf16[98,8,384]{2,1,0:T(8,128)(2,1)} %get-tuple-element.55.args_21_), channel_id=1, source_target_pairs={{0,1},{1,0},{2,3},{3,2},{4,5},{5,4},{6,7},{7,6},{8,9},{9,8},{10,11... | collective-permute-start | bytes 1806344 | tf_op jit(solution)/shard_map/ppermute | solution.py:449
  136.3 1.0 copy-done
  137.3 1.0 copy-done.1
  138.2 0.3 shard_map.206
  138.6 1.6 collective-permute-start.23
  140.1 0.8 collective-permute-start.24
  140.9 6.0 %collective-permute-done.23.refs_2_.refs_6_ = bf16[336,384]{1,0:T(8,128)(2,1)S(1)} collective-permute-done((bf16[336,384]{1,0:T(8,128)(2,1)S(1)}, bf16[336,384]{1,0:T(8,128)(2,1)S(1)}, u32[]{:S(2)}, u32[]{:S(2)}) %collective-permute-start.23) | collective-permute-done | bytes 258080 | tf_op jit(solution)/shard_map/ppermute | solution.py:449
  146.9 1.2 collective-permute-done.24.refs_3_.refs_7_
  148.2 0.8 collective-permute-start.25
  149.1 0.6 collective-permute-start.26
  149.7 1.0 collective-permute-start.27
  150.7 2.5 %shard_map.205 = (bf16[196,24,384]{2,1,0:T(8,128)(2,1)}, bf16[196,24,384]{2,1,0:T(8,128)(2,1)}) custom-call(s32[36]{0:T(128)S(1)} %copy-done.2, bf16[330,8,384]{2,1,0:T(8,128)(2,1)S(1)} %collective-permute-done.18.sent0, bf16[98,8,384]{2,1,0:T(8,128)(2,1)S(1)} %collective-permute-done.19.sent1, ...), custom_call_target="tpu_custom_call", output_to_operand_aliasing={{0}: (3, {}), {1}: (4, {})} | custom-call | bytes 4816896 | tf_op jit(solution)/shard_map/pallas_call | solution.py:521
  153.2 1.6 collective-permute-done.27.refs_6_
  154.8 1.0 shard_map.208
  (63 shorter events, 1.1 us)
Async XLA Ops:
  1.5 10.3 %collective-permute-start.10 = (bf16[2,48,384]{2,1,0:T(8,128)(2,1)S(1)}, bf16[2,48,384]{2,1,0:T(8,128)(2,1)S(1)}, u32[]{:S(2)}, u32[]{:S(2)}) collective-permute-start(bf16[2,48,384]{2,1,0:T(8,128)(2,1)S(1)} %pad_maximum_fusion.11), channel_id=1, source_target_pairs={{0,2},{1,3},{2,0},{3,1},{4,6},{5,7},{6,4},{7,5},{8,10},{9,11},{10,... | collective-permute-start | bytes 221192 | tf_op jit(solution)/shard_map/ppermute | solution.py:449
  5.6 6.8 %collective-permute-start.11 = (bf16[2,48,384]{2,1,0:T(8,128)(2,1)S(1)}, bf16[2,48,384]{2,1,0:T(8,128)(2,1)S(1)}, u32[]{:S(2)}, u32[]{:S(2)}) collective-permute-start(bf16[2,48,384]{2,1,0:T(8,128)(2,1)S(1)} %pad_maximum_fusion.11), channel_id=1, source_target_pairs={{0,1},{1,0},{2,3},{3,2},{4,5},{5,4},{6,7},{7,6},{8,9},{9,8},{10,11... | collective-permute-start | bytes 221192 | tf_op jit(solution)/shard_map/ppermute | solution.py:449
  7.2 7.0 %collective-permute-start.9 = (bf16[2,48,384]{2,1,0:T(8,128)(2,1)S(1)}, bf16[2,48,384]{2,1,0:T(8,128)(2,1)S(1)}, u32[]{:S(2)}, u32[]{:S(2)}) collective-permute-start(bf16[2,48,384]{2,1,0:T(8,128)(2,1)S(1)} %pad_maximum_fusion.11), channel_id=1, source_target_pairs={{0,3},{1,2},{2,1},{3,0},{4,7},{5,6},{6,5},{7,4},{8,11},{9,10},{10,... | collective-permute-start | bytes 221192 | tf_op jit(solution)/shard_map/ppermute | solution.py:449
  7.2 10.2 %collective-permute-start = (bf16[2,48,384]{2,1,0:T(8,128)(2,1)S(1)}, bf16[2,48,384]{2,1,0:T(8,128)(2,1)S(1)}, u32[]{:S(2)}, u32[]{:S(2)}) collective-permute-start(bf16[2,48,384]{2,1,0:T(8,128)(2,1)S(1)} %pad_maximum_fusion.10), channel_id=1, source_target_pairs={{0,3},{1,2},{2,1},{3,0},{4,7},{5,6},{6,5},{7,4},{8,11},{9,10},{10,... | collective-permute-start | bytes 221192 | tf_op jit(solution)/shard_map/ppermute | solution.py:449
  11.1 7.9 %collective-permute-start.1 = (bf16[2,48,384]{2,1,0:T(8,128)(2,1)S(1)}, bf16[2,48,384]{2,1,0:T(8,128)(2,1)S(1)}, u32[]{:S(2)}, u32[]{:S(2)}) collective-permute-start(bf16[2,48,384]{2,1,0:T(8,128)(2,1)S(1)} %pad_maximum_fusion.10), channel_id=1, source_target_pairs={{0,2},{1,3},{2,0},{3,1},{4,6},{5,7},{6,4},{7,5},{8,10},{9,11},{10,... | collective-permute-start | bytes 221192 | tf_op jit(solution)/shard_map/ppermute | solution.py:449
  11.8 7.2 %collective-permute-start.2 = (bf16[2,48,384]{2,1,0:T(8,128)(2,1)S(1)}, bf16[2,48,384]{2,1,0:T(8,128)(2,1)S(1)}, u32[]{:S(2)}, u32[]{:S(2)}) collective-permute-start(bf16[2,48,384]{2,1,0:T(8,128)(2,1)S(1)} %pad_maximum_fusion.10), channel_id=1, source_target_pairs={{0,1},{1,0},{2,3},{3,2},{4,5},{5,4},{6,7},{7,6},{8,9},{9,8},{10,11... | collective-permute-start | bytes 221192 | tf_op jit(solution)/shard_map/ppermute | solution.py:449
  14.3 8.1 %collective-permute-start.15 = (bf16[1,48,1536]{2,1,0:T(8,128)(2,1)S(1)}, bf16[1,48,1536]{2,1,0:T(8,128)(2,1)S(1)}, u32[]{:S(2)}, u32[]{:S(2)}) collective-permute-start(bf16[1,48,1536]{2,1,0:T(8,128)(2,1)S(1)} %get-tuple-element.89), channel_id=1, source_target_pairs={{0,16},{4,20},{8,24},{12,28},{16,0},{20,4},{24,8},{28,12},{1,17},{... | collective-permute-start | bytes 442376 | tf_op jit(solution)/shard_map/ppermute | solution.py:449
  15.9 7.1 %collective-permute-start.12 = (bf16[1,48,1536]{2,1,0:T(8,128)(2,1)S(1)}, bf16[1,48,1536]{2,1,0:T(8,128)(2,1)S(1)}, u32[]{:S(2)}, u32[]{:S(2)}) collective-permute-start(bf16[1,48,1536]{2,1,0:T(8,128)(2,1)S(1)} %get-tuple-element.90), channel_id=1, source_target_pairs={{0,8},{4,12},{8,0},{12,4},{16,24},{20,28},{24,16},{28,20},{1,9},{5... | collective-permute-start | bytes 442376 | tf_op jit(solution)/shard_map/ppermute | solution.py:449
  19.1 19.5 %copy-start.8 = (bf16[2,196,196]{2,0,1:T(2,128)(2,1)S(1)}, bf16[2,196,196]{2,0,1:T(2,128)(2,1)}, u32[]{:S(2)}) copy-start(bf16[2,196,196]{2,0,1:T(2,128)(2,1)} %param.18) | copy-start | bytes 460996
  19.1 5.9 %collective-permute-start.5 = (bf16[1,48,1536]{2,1,0:T(8,128)(2,1)S(1)}, bf16[1,48,1536]{2,1,0:T(8,128)(2,1)S(1)}, u32[]{:S(2)}, u32[]{:S(2)}) collective-permute-start(bf16[1,48,1536]{2,1,0:T(8,128)(2,1)S(1)} %get-tuple-element.95), channel_id=1, source_target_pairs={{0,16},{4,20},{8,24},{12,28},{16,0},{20,4},{24,8},{28,12},{1,17},{... | collective-permute-start | bytes 442376 | tf_op jit(solution)/shard_map/ppermute | solution.py:449
  20.9 6.8 %collective-permute-start.3 = (bf16[1,48,1536]{2,1,0:T(8,128)(2,1)S(1)}, bf16[1,48,1536]{2,1,0:T(8,128)(2,1)S(1)}, u32[]{:S(2)}, u32[]{:S(2)}) collective-permute-start(bf16[1,48,1536]{2,1,0:T(8,128)(2,1)S(1)} %get-tuple-element.96), channel_id=1, source_target_pairs={{0,8},{4,12},{8,0},{12,4},{16,24},{20,28},{24,16},{28,20},{1,9},{5... | collective-permute-start | bytes 442376 | tf_op jit(solution)/shard_map/ppermute | solution.py:449
  22.5 11.6 %collective-permute-start.16 = (bf16[2,48,1536]{2,1,0:T(8,128)(2,1)S(1)}, bf16[2,48,1536]{2,1,0:T(8,128)(2,1)S(1)}, u32[]{:S(2)}, u32[]{:S(2)}) collective-permute-start(bf16[2,48,1536]{2,1,0:T(8,128)(2,1)S(1)} %pad_maximum_fusion.9), channel_id=1, source_target_pairs={{0,8},{4,12},{8,0},{12,4},{16,24},{20,28},{24,16},{28,20},{1,9},{5... | collective-permute-start | bytes 884744 | tf_op jit(solution)/shard_map/ppermute | solution.py:449
  23.1 11.1 %collective-permute-start.13 = (bf16[2,48,1536]{2,1,0:T(8,128)(2,1)S(1)}, bf16[2,48,1536]{2,1,0:T(8,128)(2,1)S(1)}, u32[]{:S(2)}, u32[]{:S(2)}) collective-permute-start(bf16[2,48,1536]{2,1,0:T(8,128)(2,1)S(1)} %pad_maximum_fusion.8), channel_id=1, source_target_pairs={{0,16},{4,20},{8,24},{12,28},{16,0},{20,4},{24,8},{28,12},{1,17},{... | collective-permute-start | bytes 884744 | tf_op jit(solution)/shard_map/ppermute | solution.py:449
  25.1 12.8 %collective-permute-start.6 = (bf16[2,48,1536]{2,1,0:T(8,128)(2,1)S(1)}, bf16[2,48,1536]{2,1,0:T(8,128)(2,1)S(1)}, u32[]{:S(2)}, u32[]{:S(2)}) collective-permute-start(bf16[2,48,1536]{2,1,0:T(8,128)(2,1)S(1)} %pad_maximum_fusion.6), channel_id=1, source_target_pairs={{0,8},{4,12},{8,0},{12,4},{16,24},{20,28},{24,16},{28,20},{1,9},{5... | collective-permute-start | bytes 884744 | tf_op jit(solution)/shard_map/ppermute | solution.py:449
  27.8 10.2 %collective-permute-start.4 = (bf16[2,48,1536]{2,1,0:T(8,128)(2,1)S(1)}, bf16[2,48,1536]{2,1,0:T(8,128)(2,1)S(1)}, u32[]{:S(2)}, u32[]{:S(2)}) collective-permute-start(bf16[2,48,1536]{2,1,0:T(8,128)(2,1)S(1)} %pad_maximum_fusion.5), channel_id=1, source_target_pairs={{0,16},{4,20},{8,24},{12,28},{16,0},{20,4},{24,8},{28,12},{1,17},{... | collective-permute-start | bytes 884744 | tf_op jit(solution)/shard_map/ppermute | solution.py:449
  34.1 7.8 %copy-start.3 = (bf16[4,48,1536]{2,1,0:T(8,128)(2,1)}, bf16[4,48,1536]{2,1,0:T(8,128)(2,1)S(1)}, u32[]{:S(2)}) copy-start(bf16[4,48,1536]{2,1,0:T(8,128)(2,1)S(1)} %pad_maximum_fusion.3.args_17_) | copy-start | bytes 1769476
  34.1 5.2 %collective-permute-start.17 = (bf16[4,48,1536]{2,1,0:T(8,128)(2,1)S(1)}, bf16[4,48,1536]{2,1,0:T(8,128)(2,1)S(1)}, u32[]{:S(2)}, u32[]{:S(2)}) collective-permute-start(bf16[4,48,1536]{2,1,0:T(8,128)(2,1)S(1)} %pad_maximum_fusion.3.args_17_), channel_id=1, source_target_pairs={{0,4},{4,0},{8,12},{12,8},{16,20},{20,16},{24,28},{28,24},{1,5},{5... | collective-permute-start | bytes 1769480 | tf_op jit(solution)/shard_map/ppermute | solution.py:449
  34.3 7.6 %copy-start.4 = (bf16[4,48,1536]{2,1,0:T(8,128)(2,1)}, bf16[4,48,1536]{2,1,0:T(8,128)(2,1)S(1)}, u32[]{:S(2)}) copy-start(bf16[4,48,1536]{2,1,0:T(8,128)(2,1)S(1)} %pad_maximum_fusion.2.args_15_) | copy-start | bytes 1769476
  34.3 5.1 %collective-permute-start.14 = (bf16[4,48,1536]{2,1,0:T(8,128)(2,1)S(1)}, bf16[4,48,1536]{2,1,0:T(8,128)(2,1)S(1)}, u32[]{:S(2)}, u32[]{:S(2)}) collective-permute-start(bf16[4,48,1536]{2,1,0:T(8,128)(2,1)S(1)} %pad_maximum_fusion.2.args_15_), channel_id=1, source_target_pairs={{0,4},{4,0},{8,12},{12,8},{16,20},{20,16},{24,28},{28,24},{1,5},{5... | collective-permute-start | bytes 1769480 | tf_op jit(solution)/shard_map/ppermute | solution.py:449
  38.0 3.9 %copy-start.5 = (bf16[4,48,1536]{2,1,0:T(8,128)(2,1)}, bf16[4,48,1536]{2,1,0:T(8,128)(2,1)S(1)}, u32[]{:S(2)}) copy-start(bf16[4,48,1536]{2,1,0:T(8,128)(2,1)S(1)} %pad_maximum_fusion.1.args_13_) | copy-start | bytes 1769476
  38.0 3.8 %copy-start.6 = (bf16[4,48,1536]{2,1,0:T(8,128)(2,1)}, bf16[4,48,1536]{2,1,0:T(8,128)(2,1)S(1)}, u32[]{:S(2)}) copy-start(bf16[4,48,1536]{2,1,0:T(8,128)(2,1)S(1)} %pad_maximum_fusion.args_11_) | copy-start | bytes 1769476
  38.1 2.1 %collective-permute-start.7 = (bf16[4,48,1536]{2,1,0:T(8,128)(2,1)S(1)}, bf16[4,48,1536]{2,1,0:T(8,128)(2,1)S(1)}, u32[]{:S(2)}, u32[]{:S(2)}) collective-permute-start(bf16[4,48,1536]{2,1,0:T(8,128)(2,1)S(1)} %pad_maximum_fusion.args_11_), channel_id=1, source_target_pairs={{0,4},{4,0},{8,12},{12,8},{16,20},{20,16},{24,28},{28,24},{1,5},{5... | collective-permute-start | bytes 1769480 | tf_op jit(solution)/shard_map/ppermute | solution.py:449
  38.1 2.8 %collective-permute-start.8 = (bf16[4,48,1536]{2,1,0:T(8,128)(2,1)S(1)}, bf16[4,48,1536]{2,1,0:T(8,128)(2,1)S(1)}, u32[]{:S(2)}, u32[]{:S(2)}) collective-permute-start(bf16[4,48,1536]{2,1,0:T(8,128)(2,1)S(1)} %pad_maximum_fusion.1.args_13_), channel_id=1, source_target_pairs={{0,4},{4,0},{8,12},{12,8},{16,20},{20,16},{24,28},{28,24},{1,5},{5... | collective-permute-start | bytes 1769480 | tf_op jit(solution)/shard_map/ppermute | solution.py:449
  39.3 2.5 %copy-start.9 = (bf16[4,48,1536]{2,1,0:T(8,128)(2,1)}, bf16[4,48,1536]{2,1,0:T(8,128)(2,1)S(1)}, u32[]{:S(2)}) copy-start(bf16[4,48,1536]{2,1,0:T(8,128)(2,1)S(1)} %collective-permute-done.17.args_18_) | copy-start | bytes 1769476
  39.4 2.6 %copy-start.10 = (bf16[4,48,1536]{2,1,0:T(8,128)(2,1)}, bf16[4,48,1536]{2,1,0:T(8,128)(2,1)S(1)}, u32[]{:S(2)}) copy-start(bf16[4,48,1536]{2,1,0:T(8,128)(2,1)S(1)} %collective-permute-done.14.args_16_) | copy-start | bytes 1769476
  40.1 1.8 %copy-start.11 = (bf16[4,48,1536]{2,1,0:T(8,128)(2,1)}, bf16[4,48,1536]{2,1,0:T(8,128)(2,1)S(1)}, u32[]{:S(2)}) copy-start(bf16[4,48,1536]{2,1,0:T(8,128)(2,1)S(1)} %collective-permute-done.7.args_12_) | copy-start | bytes 1769476
  41.0 0.9 copy-start.12
  85.7 47.1 %collective-permute-start.18 = (bf16[330,8,384]{2,1,0:T(8,128)(2,1)}, bf16[330,8,384]{2,1,0:T(8,128)(2,1)S(1)}, u32[]{:S(2)}, u32[]{:S(2)}) collective-permute-start(bf16[330,8,384]{2,1,0:T(8,128)(2,1)} %get-tuple-element.54.args_20_), channel_id=1, source_target_pairs={{0,1},{1,0},{2,3},{3,2},{4,5},{5,4},{6,7},{7,6},{8,9},{9,8},{10,11... | collective-permute-start | bytes 6082568 | tf_op jit(solution)/shard_map/ppermute | solution.py:449
  88.1 44.1 %all-to-all-start = ((bf16[8,2,2,48,384]{4,3,2,1,0:T(8,128)(2,1)}), bf16[8,2,2,48,384]{4,3,2,1,0:T(8,128)(2,1)S(1)}, u32[]{:S(2)}, u32[]{:S(2)}) async-start(bf16[8,2,2,48,384]{4,3,2,1,0:T(8,128)(2,1)} %get-tuple-element.58), calls=%async_computation | async-start | bytes 2359296 | tf_op jit(solution)/shard_map/all_to_all | solution.py:719
  91.9 41.5 %copy-start.7 = (bf16[2,144,384]{2,1,0:T(8,128)(2,1)S(1)}, bf16[2,144,384]{2,1,0:T(8,128)(2,1)}, u32[]{:S(2)}) copy-start(bf16[2,144,384]{2,1,0:T(8,128)(2,1)} %get-tuple-element.68) | copy-start | bytes 663556
  132.2 18.5 %copy-start.2 = (s32[36]{0:T(128)S(1)}, s32[36]{0:T(128)}, u32[]{:S(2)}) copy-start(s32[36]{0:T(128)} %stack.82.args_0_.meta) | copy-start | bytes 436
  132.8 3.5 %collective-permute-start.20 = (bf16[384,384]{1,0:T(8,128)(2,1)}, bf16[384,384]{1,0:T(8,128)(2,1)S(1)}, u32[]{:S(2)}, u32[]{:S(2)}) collective-permute-start(bf16[384,384]{1,0:T(8,128)(2,1)} %get-tuple-element.66), channel_id=1, source_target_pairs={{0,4},{4,0},{8,12},{12,8},{16,20},{20,16},{24,28},{28,24},{1,5},{5... | collective-permute-start | bytes 884744 | tf_op jit(solution)/shard_map/ppermute | solution.py:449
  132.9 3.4 %collective-permute-start.21 = (bf16[384,384]{1,0:T(8,128)(2,1)}, bf16[384,384]{1,0:T(8,128)(2,1)S(1)}, u32[]{:S(2)}, u32[]{:S(2)}) collective-permute-start(bf16[384,384]{1,0:T(8,128)(2,1)} %get-tuple-element.67), channel_id=1, source_target_pairs={{0,4},{4,0},{8,12},{12,8},{16,20},{20,16},{24,28},{28,24},{1,5},{5... | collective-permute-start | bytes 884744 | tf_op jit(solution)/shard_map/ppermute | solution.py:449
  134.4 1.9 %collective-permute-start.22 = (bf16[2,144,384]{2,1,0:T(8,128)(2,1)S(1)}, bf16[2,144,384]{2,1,0:T(8,128)(2,1)S(1)}, u32[]{:S(2)}, u32[]{:S(2)}) collective-permute-start(bf16[2,144,384]{2,1,0:T(8,128)(2,1)S(1)} %fusion.1.refs_4_), channel_id=1, source_target_pairs={{0,4},{4,0},{8,12},{12,8},{16,20},{20,16},{24,28},{28,24},{1,5},{5... | collective-permute-start | bytes 663560 | tf_op jit(solution)/shard_map/ppermute | solution.py:449
  134.5 16.2 %collective-permute-start.19 = (bf16[98,8,384]{2,1,0:T(8,128)(2,1)}, bf16[98,8,384]{2,1,0:T(8,128)(2,1)S(1)}, u32[]{:S(2)}, u32[]{:S(2)}) collective-permute-start(bf16[98,8,384]{2,1,0:T(8,128)(2,1)} %get-tuple-element.55.args_21_), channel_id=1, source_target_pairs={{0,1},{1,0},{2,3},{3,2},{4,5},{5,4},{6,7},{7,6},{8,9},{9,8},{10,11... | collective-permute-start | bytes 1806344 | tf_op jit(solution)/shard_map/ppermute | solution.py:449
  136.3 1.0 copy-start
  137.3 1.0 copy-start.1
  138.6 8.4 %collective-permute-start.23 = (bf16[336,384]{1,0:T(8,128)(2,1)S(1)}, bf16[336,384]{1,0:T(8,128)(2,1)S(1)}, u32[]{:S(2)}, u32[]{:S(2)}) collective-permute-start(bf16[336,384]{1,0:T(8,128)(2,1)S(1)} %get-tuple-element.73.refs_4_), channel_id=1, source_target_pairs={{0,8},{4,12},{8,0},{12,4},{16,24},{20,28},{24,16},{28,20},{1,9},{5... | collective-permute-start | bytes 774152 | tf_op jit(solution)/shard_map/ppermute | solution.py:449
  140.1 8.0 %collective-permute-start.24 = (bf16[336,384]{1,0:T(8,128)(2,1)S(1)}, bf16[336,384]{1,0:T(8,128)(2,1)S(1)}, u32[]{:S(2)}, u32[]{:S(2)}) collective-permute-start(bf16[336,384]{1,0:T(8,128)(2,1)S(1)} %get-tuple-element.74.refs_5_), channel_id=1, source_target_pairs={{0,16},{4,20},{8,24},{12,28},{16,0},{20,4},{24,8},{28,12},{1,17},{... | collective-permute-start | bytes 774152 | tf_op jit(solution)/shard_map/ppermute | solution.py:449
  148.2 6.6 %collective-permute-start.25 = (bf16[240,384]{1,0:T(8,128)(2,1)S(1)}, bf16[240,384]{1,0:T(8,128)(2,1)S(1)}, u32[]{:S(2)}, u32[]{:S(2)}) collective-permute-start(bf16[240,384]{1,0:T(8,128)(2,1)S(1)} %get-tuple-element.77.refs_2_), channel_id=1, source_target_pairs={{0,16},{4,20},{8,24},{12,28},{16,0},{20,4},{24,8},{28,12},{1,17},{... | collective-permute-start | bytes 552968 | tf_op jit(solution)/shard_map/ppermute | solution.py:449
  149.1 5.7 %collective-permute-start.26 = (bf16[240,384]{1,0:T(8,128)(2,1)S(1)}, bf16[240,384]{1,0:T(8,128)(2,1)S(1)}, u32[]{:S(2)}, u32[]{:S(2)}) collective-permute-start(bf16[240,384]{1,0:T(8,128)(2,1)S(1)} %get-tuple-element.78.refs_3_), channel_id=1, source_target_pairs={{0,8},{4,12},{8,0},{12,4},{16,24},{20,28},{24,16},{28,20},{1,9},{5... | collective-permute-start | bytes 552968 | tf_op jit(solution)/shard_map/ppermute | solution.py:449
  149.7 5.1 %collective-permute-start.27 = (bf16[2,96,384]{2,1,0:T(8,128)(2,1)S(1)}, bf16[2,96,384]{2,1,0:T(8,128)(2,1)S(1)}, u32[]{:S(2)}, u32[]{:S(2)}) collective-permute-start(bf16[2,96,384]{2,1,0:T(8,128)(2,1)S(1)} %get-tuple-element.79), channel_id=1, source_target_pairs={{0,1},{1,0},{2,3},{3,2},{4,5},{5,4},{6,7},{7,6},{8,9},{9,8},{10,11... | collective-permute-start | bytes 442376 | tf_op jit(solution)/shard_map/ppermute | solution.py:449

commit v3 on v2

--- a/solution.py
+++ b/solution.py
@@ -116,7 +116,7 @@
                         src = r[f"w{i}part{half}_{l}"]
                         n_part = src.shape[0]
                         for k in range(n_part):
-                            at = meta[4 + i * sz.n_dp + half * n_part + k] * sz.shard
+                            at = meta[4 + l * sz.n_dp + half * n_part + k] * sz.shard
                             at = pl.ds(pl.multiple_of(at, 16), sz.shard)
                             pltpu.make_async_copy(
                                 src.at[k], r["w"].at[i, l, at], r["arrive"].at[i, l]
@@ -453,17 +453,17 @@
     return [2**k for k in range(1, n.bit_length() - 1)]
 
 
-def gather_columns(sz, w1, w2):
-    both = jnp.stack([w1, w2])
+def gather_columns(sz, both, later, hid):
     parts = [both] + [swap(both, "hid", k) for k in range(1, sz.n_hid)]
-    hid = lax.axis_index("hid")
+    if later is not None:
+        parts[1:3], later = lax.optimization_barrier((parts[1:3], later))
     columns = []
     for j in range(sz.n_hid):
         v = parts[j]
         for h in range(1, sz.n_hid):
             v = jnp.where(hid == h, parts[j ^ h], v)
         columns.append(v)
-    return jnp.concatenate(columns, axis=2)
+    return jnp.concatenate(columns, axis=2), later
 
 
 def gather_rows(sz, full):
@@ -679,18 +679,23 @@
     meta = jnp.stack(places).astype(jnp.int32)
 
     weights = []
+    gathered, later, chip = [], fc2_weight, hid
+    for i in range(2):
+        full, later = gather_columns(sz, later if i else fc1_weight, None if i else later, chip)
+        full, chip = lax.optimization_barrier((full, chip))
+        got = gather_rows(sz, full)
+        if i == 0:
+            got, meta = lax.optimization_barrier((got, meta))
+        gathered.append((got, [swap(g, "dp", 1) for g in got]))
     for l in range(layers):
-        got = gather_rows(sz, gather_columns(sz, fc1_weight[l], fc2_weight[l]))
-        if l == 0:
-            got, meta = lax.optimization_barrier((got, meta))
-        other = [swap(g, "dp", 1) for g in got]
+        got, other = ([gathered[i][part][l] for i in range(2)] for part in range(2))
         if sz.blocks:
             weights.append([(got[i], other[i]) for i in range(2)])
         else:
             ready = []
             for i in range(2):
                 w = jnp.concatenate([got[i], other[i]])
-                at = jnp.zeros(n_dp, jnp.int32).at[jnp.array(orders[i])].set(jnp.arange(n_dp))
+                at = jnp.zeros(n_dp, jnp.int32).at[jnp.array(orders[l])].set(jnp.arange(n_dp))
                 w = w[at[jnp.arange(n_dp) ^ me]]
                 ready.append(w.reshape(sz.width, sz.hidden))
             weights.append(jnp.stack(ready))

time: 156 us -> 156 us (level)
  starting transfers between devices: 35.6 us -> 30.9 us
  waiting for transfers between devices: 24.5 us -> 27.8 us
  other arithmetic: 1.57 us -> 3.31 us
    ppermute x28, starting transfers between devices: 31.8 us -> 27.2 us  [swap(): return lax.ppermute(x, axis, [(i, i ^ k) for i in range(n)])]
    ppermute x28, waiting for transfers between devices: 24.5 us -> 27.8 us  [swap(): return lax.ppermute(x, axis, [(i, i ^ k) for i in range(n)])]
    select_n x2, other arithmetic: 0.11 us -> 1.88 us  [gather_columns(): v = jnp.where(hid == h, parts[j ^ h], v)]
  transfers between devices with their start and end apart: 29 -> 29, of which waited for: 12 -> 13; matrix products, arithmetic and copies ran while one was open for 2% -> 3% of each run, Pallas kernels for 28% -> 28%
where the time goes in v3:
time: 156 us; the launch traced here: 155 us
  Pallas kernels  88 us (56%)
  starting transfers between devices  30.9 us (20%)
  waiting for transfers between devices  27.8 us (18%)
  local copies, waits for them, and re-layouts  4.28 us (3%)
  other arithmetic  3.31 us (2%)
    pallas_call x2, Pallas kernels, run(): pl.pallas_call(functools.partial(kernel_body, sz, kept, names), grid_spec...  84 us
    ppermute x28, waiting for transfers between devices, swap(): return lax.ppermute(x, axis, [(i, i ^ k) for i in range(n)])  27.8 us
    ppermute x28, starting transfers between devices, swap(): return lax.ppermute(x, axis, [(i, i ^ k) for i in range(n)])  27.2 us
    all_to_all x1, starting transfers between devices, on_device(): lax.all_to_all(theirs, 'dp', split_axis=0, concat_axis=0, tiled=True)  3.76 us
    unnamed x27, local copies, waits for them, and re-layouts  3.57 us
  transfers between devices with their start and end apart: 29, of which 13 were waited for; matrix products, arithmetic and copies ran while one was open for 3% of the time, Pallas kernels for 28%

profile of v3, /device:TPU:0, one launch (start us, length us, event | category | flops | bytes accessed | tf_op | source)
XLA Modules:
  0.0 155.2 jit_solution(15305053940532589540)
XLA Ops:
  0.6 3.1 %collective-permute-start.1 = (bf16[2,48,384]{2,1,0:T(8,128)(2,1)}, bf16[2,48,384]{2,1,0:T(8,128)(2,1)S(1)}, u32[]{:S(2)}, u32[]{:S(2)}) collective-permute-start(bf16[2,48,384]{2,1,0:T(8,128)(2,1)} %param.20), channel_id=1, source_target_pairs={{0,1},{1,0},{2,3},{3,2},{4,5},{5,4},{6,7},{7,6},{8,9},{9,8},{10,11... | collective-permute-start | bytes 221192 | tf_op jit(solution)/shard_map/ppermute | solution.py:449
  3.7 2.6 %collective-permute-start.2 = (bf16[2,48,384]{2,1,0:T(8,128)(2,1)}, bf16[2,48,384]{2,1,0:T(8,128)(2,1)S(1)}, u32[]{:S(2)}, u32[]{:S(2)}) collective-permute-start(bf16[2,48,384]{2,1,0:T(8,128)(2,1)} %param.20), channel_id=1, source_target_pairs={{0,2},{1,3},{2,0},{3,1},{4,6},{5,7},{6,4},{7,5},{8,10},{9,11},{10,... | collective-permute-start | bytes 221192 | tf_op jit(solution)/shard_map/ppermute | solution.py:449
  6.3 0.6 stack.75.args_0_.meta
  7.0 4.8 %collective-permute-done.2 = bf16[2,48,384]{2,1,0:T(8,128)(2,1)S(1)} collective-permute-done((bf16[2,48,384]{2,1,0:T(8,128)(2,1)}, bf16[2,48,384]{2,1,0:T(8,128)(2,1)S(1)}, u32[]{:S(2)}, u32[]{:S(2)}) %collective-permute-start.2) | collective-permute-done | bytes 73760 | tf_op jit(solution)/shard_map/ppermute | solution.py:449
  11.8 0.9 collective-permute-start.10
  12.7 2.7 %collective-permute-start.8 = (bf16[2,48,384]{2,1,0:T(8,128)(2,1)}, bf16[2,48,384]{2,1,0:T(8,128)(2,1)S(1)}, u32[]{:S(2)}, u32[]{:S(2)}) collective-permute-start(bf16[2,48,384]{2,1,0:T(8,128)(2,1)} %param.22), channel_id=1, source_target_pairs={{0,3},{1,2},{2,1},{3,0},{4,7},{5,6},{6,5},{7,4},{8,11},{9,10},{10,... | collective-permute-start | bytes 221192 | tf_op jit(solution)/shard_map/ppermute | solution.py:449
  15.4 0.6 collective-permute-start.9
  15.9 0.9 select_select_fusion.7
  17.0 1.6 %collective-permute-start.5 = (bf16[1,48,1536]{2,1,0:T(8,128)(2,1)S(1)}, bf16[1,48,1536]{2,1,0:T(8,128)(2,1)S(1)}, u32[]{:S(2)}, u32[]{:S(2)}) collective-permute-start(bf16[1,48,1536]{2,1,0:T(8,128)(2,1)S(1)} %get-tuple-element.107), channel_id=1, source_target_pairs={{0,16},{4,20},{8,24},{12,28},{16,0},{20,4},{24,8},{28,12},{1,17},{... | collective-permute-start | bytes 442376 | tf_op jit(solution)/shard_map/ppermute | solution.py:449
  18.5 1.5 collective-permute-start.3
  20.0 1.6 %collective-permute-done.9 = bf16[2,48,384]{2,1,0:T(8,128)(2,1)S(1)} collective-permute-done((bf16[2,48,384]{2,1,0:T(8,128)(2,1)}, bf16[2,48,384]{2,1,0:T(8,128)(2,1)S(1)}, u32[]{:S(2)}, u32[]{:S(2)}) %collective-permute-start.9) | collective-permute-done | bytes 73760 | tf_op jit(solution)/shard_map/ppermute | solution.py:449
  21.6 0.9 select_select_fusion.3
  22.6 1.6 %collective-permute-start.15 = (bf16[1,48,1536]{2,1,0:T(8,128)(2,1)S(1)}, bf16[1,48,1536]{2,1,0:T(8,128)(2,1)S(1)}, u32[]{:S(2)}, u32[]{:S(2)}) collective-permute-start(bf16[1,48,1536]{2,1,0:T(8,128)(2,1)S(1)} %get-tuple-element.101), channel_id=1, source_target_pairs={{0,16},{4,20},{8,24},{12,28},{16,0},{20,4},{24,8},{28,12},{1,17},{... | collective-permute-start | bytes 442376 | tf_op jit(solution)/shard_map/ppermute | solution.py:449
  24.2 1.5 collective-permute-start.11
  25.8 0.6 collective-permute-start.6
  26.4 0.6 collective-permute-start.4
  27.0 2.1 %collective-permute-done.15 = bf16[1,48,1536]{2,1,0:T(8,128)(2,1)S(1)} collective-permute-done((bf16[1,48,1536]{2,1,0:T(8,128)(2,1)S(1)}, bf16[1,48,1536]{2,1,0:T(8,128)(2,1)S(1)}, u32[]{:S(2)}, u32[]{:S(2)}) %collective-permute-start.15) | collective-permute-done | bytes 147488 | tf_op jit(solution)/shard_map/ppermute | solution.py:449
  29.1 1.9 %collective-permute-start.16 = (bf16[2,48,1536]{2,1,0:T(8,128)(2,1)S(1)}, bf16[2,48,1536]{2,1,0:T(8,128)(2,1)S(1)}, u32[]{:S(2)}, u32[]{:S(2)}) collective-permute-start(bf16[2,48,1536]{2,1,0:T(8,128)(2,1)S(1)} %pad_maximum_fusion.9), channel_id=1, source_target_pairs={{0,8},{4,12},{8,0},{12,4},{16,24},{20,28},{24,16},{28,20},{1,9},{5... | collective-permute-start | bytes 884744 | tf_op jit(solution)/shard_map/ppermute | solution.py:449
  31.0 1.7 %collective-permute-start.12 = (bf16[2,48,1536]{2,1,0:T(8,128)(2,1)S(1)}, bf16[2,48,1536]{2,1,0:T(8,128)(2,1)S(1)}, u32[]{:S(2)}, u32[]{:S(2)}) collective-permute-start(bf16[2,48,1536]{2,1,0:T(8,128)(2,1)S(1)} %pad_maximum_fusion.8), channel_id=1, source_target_pairs={{0,16},{4,20},{8,24},{12,28},{16,0},{20,4},{24,8},{28,12},{1,17},{... | collective-permute-start | bytes 884744 | tf_op jit(solution)/shard_map/ppermute | solution.py:449
  32.7 2.8 %collective-permute-done.6 = bf16[2,48,1536]{2,1,0:T(8,128)(2,1)S(1)} collective-permute-done((bf16[2,48,1536]{2,1,0:T(8,128)(2,1)S(1)}, bf16[2,48,1536]{2,1,0:T(8,128)(2,1)S(1)}, u32[]{:S(2)}, u32[]{:S(2)}) %collective-permute-start.6) | collective-permute-done | bytes 294944 | tf_op jit(solution)/shard_map/ppermute | solution.py:449
  35.8 0.5 collective-permute-start.7
  36.3 2.4 %collective-permute-done.16 = bf16[2,48,1536]{2,1,0:T(8,128)(2,1)S(1)} collective-permute-done((bf16[2,48,1536]{2,1,0:T(8,128)(2,1)S(1)}, bf16[2,48,1536]{2,1,0:T(8,128)(2,1)S(1)}, u32[]{:S(2)}, u32[]{:S(2)}) %collective-permute-start.16) | collective-permute-done | bytes 294944 | tf_op jit(solution)/shard_map/ppermute | solution.py:449
  39.0 0.5 collective-permute-start.13
  39.5 0.7 copy.26.args_7_
  40.2 0.6 collective-permute-done.17.args_18_
  40.9 0.8 collective-permute-done.13.args_14_
  41.7 0.9 copy-done.12
  42.6 43.8 %shard_map.203 = (bf16[330,8,384]{2,1,0:T(8,128)(2,1)}, bf16[98,8,384]{2,1,0:T(8,128)(2,1)}, bf16[2,144,384]{2,1,0:T(8,128)(2,1)}, bf16[8,2,2,48,384]{4,3,2,1,0:T(8,128)(2,1)}, f32[2,2,384,384]{3,2,1,0:T(8,128)}) custom-call(s32[36]{0:T(128)} %stack.75.args_0_.meta, bf16[196,24,384]{2,1,0:T(8,128)(2,1)} %bitcast.26, bf16[196,24,384]{2,1,0:T(8,128)(2,1)} %bitcast.28, ...), custom_call_target="tpu_custom_call" | custom-call | flops 22649241600 | bytes 56623104 | tf_op jit(solution)/shard_map/pallas_call | solution.py:431
  86.5 3.8 %all-to-all-start = ((bf16[8,2,2,48,384]{4,3,2,1,0:T(8,128)(2,1)}), bf16[8,2,2,48,384]{4,3,2,1,0:T(8,128)(2,1)S(1)}, u32[]{:S(2)}, u32[]{:S(2)}) async-start(bf16[8,2,2,48,384]{4,3,2,1,0:T(8,128)(2,1)} %get-tuple-element.70), calls=%async_computation | async-start | bytes 2359296 | tf_op jit(solution)/shard_map/all_to_all | solution.py:724
  90.3 40.3 %shard_map.204 = (bf16[196,24,384]{2,1,0:T(8,128)(2,1)}, bf16[196,24,384]{2,1,0:T(8,128)(2,1)}, bf16[2,144,384]{2,1,0:T(8,128)(2,1)}, bf16[384,384]{1,0:T(8,128)...) custom-call(s32[36]{0:T(128)} %stack.75.args_0_.meta, ...), custom_call_target="tpu_custom_call" | custom-call | flops 22649241600 | bytes 56623104 | tf_op jit(solution)/shard_map/pallas_call | solution.py:431
  130.6 2.3 %collective-permute-done.18.sent0 = bf16[330,8,384]{2,1,0:T(8,128)(2,1)S(1)} collective-permute-done((bf16[330,8,384]{2,1,0:T(8,128)(2,1)}, bf16[330,8,384]{2,1,0:T(8,128)(2,1)S(1)}, u32[]{:S(2)}, u32[]{:S(2)}) %collective-permute-start.18) | collective-permute-done | bytes 2027552 | tf_op jit(solution)/shard_map/ppermute | solution.py:449
  133.0 0.5 collective-permute-start.21
  133.5 1.0 fusion.1.refs_4_
  134.9 1.1 collective-permute-done.22.refs_5_
  136.0 1.0 copy-done
  137.0 1.0 copy-done.1
  138.0 0.3 shard_map.206
  138.3 1.6 %collective-permute-start.23 = (bf16[336,384]{1,0:T(8,128)(2,1)S(1)}, bf16[336,384]{1,0:T(8,128)(2,1)S(1)}, u32[]{:S(2)}, u32[]{:S(2)}) collective-permute-start(bf16[336,384]{1,0:T(8,128)(2,1)S(1)} %get-tuple-element.85.refs_4_), channel_id=1, source_target_pairs={{0,8},{4,12},{8,0},{12,4},{16,24},{20,28},{24,16},{28,20},{1,9},{5... | collective-permute-start | bytes 774152 | tf_op jit(solution)/shard_map/ppermute | solution.py:449
  139.9 0.5 collective-permute-start.24
  140.4 6.3 %collective-permute-done.23.refs_2_.refs_6_ = bf16[336,384]{1,0:T(8,128)(2,1)S(1)} collective-permute-done((bf16[336,384]{1,0:T(8,128)(2,1)S(1)}, bf16[336,384]{1,0:T(8,128)(2,1)S(1)}, u32[]{:S(2)}, u32[]{:S(2)}) %collective-permute-start.23) | collective-permute-done | bytes 258080 | tf_op jit(solution)/shard_map/ppermute | solution.py:449
  146.6 1.2 collective-permute-done.24.refs_3_.refs_7_
  148.0 0.6 collective-permute-start.25
  148.5 0.5 collective-permute-start.26
  149.1 1.0 collective-permute-start.27
  150.1 1.2 collective-permute-done.19.sent1
  151.2 2.5 %shard_map.205 = (bf16[196,24,384]{2,1,0:T(8,128)(2,1)}, bf16[196,24,384]{2,1,0:T(8,128)(2,1)}) custom-call(s32[36]{0:T(128)S(1)} %copy-done.2, bf16[330,8,384]{2,1,0:T(8,128)(2,1)S(1)} %collective-permute-done.18.sent0, bf16[98,8,384]{2,1,0:T(8,128)(2,1)S(1)} %collective-permute-done.19.sent1, ...), custom_call_target="tpu_custom_call", output_to_operand_aliasing={{0}: (3, {}), {1}: (4, {})} | custom-call | bytes 4816896 | tf_op jit(solution)/shard_map/pallas_call | solution.py:521
  153.8 0.4 collective-permute-done.27.refs_6_
  154.2 1.0 shard_map.208
  (60 shorter events, 1.4 us)
Async XLA Ops:
  0.6 6.3 %collective-permute-start.1 = (bf16[2,48,384]{2,1,0:T(8,128)(2,1)}, bf16[2,48,384]{2,1,0:T(8,128)(2,1)S(1)}, u32[]{:S(2)}, u32[]{:S(2)}) collective-permute-start(bf16[2,48,384]{2,1,0:T(8,128)(2,1)} %param.20), channel_id=1, source_target_pairs={{0,1},{1,0},{2,3},{3,2},{4,5},{5,4},{6,7},{7,6},{8,9},{9,8},{10,11... | collective-permute-start | bytes 221192 | tf_op jit(solution)/shard_map/ppermute | solution.py:449
  3.7 8.0 %collective-permute-start.2 = (bf16[2,48,384]{2,1,0:T(8,128)(2,1)}, bf16[2,48,384]{2,1,0:T(8,128)(2,1)S(1)}, u32[]{:S(2)}, u32[]{:S(2)}) collective-permute-start(bf16[2,48,384]{2,1,0:T(8,128)(2,1)} %param.20), channel_id=1, source_target_pairs={{0,2},{1,3},{2,0},{3,1},{4,6},{5,7},{6,4},{7,5},{8,10},{9,11},{10,... | collective-permute-start | bytes 221192 | tf_op jit(solution)/shard_map/ppermute | solution.py:449
  6.3 9.6 %collective-permute-start = (bf16[2,48,384]{2,1,0:T(8,128)(2,1)}, bf16[2,48,384]{2,1,0:T(8,128)(2,1)S(1)}, u32[]{:S(2)}, u32[]{:S(2)}) collective-permute-start(bf16[2,48,384]{2,1,0:T(8,128)(2,1)} %param.20), channel_id=1, source_target_pairs={{0,3},{1,2},{2,1},{3,0},{4,7},{5,6},{6,5},{7,4},{8,11},{9,10},{10,... | collective-permute-start | bytes 221192 | tf_op jit(solution)/shard_map/ppermute | solution.py:449
  11.8 8.3 %collective-permute-start.10 = (bf16[2,48,384]{2,1,0:T(8,128)(2,1)}, bf16[2,48,384]{2,1,0:T(8,128)(2,1)S(1)}, u32[]{:S(2)}, u32[]{:S(2)}) collective-permute-start(bf16[2,48,384]{2,1,0:T(8,128)(2,1)} %param.22), channel_id=1, source_target_pairs={{0,1},{1,0},{2,3},{3,2},{4,5},{5,4},{6,7},{7,6},{8,9},{9,8},{10,11... | collective-permute-start | bytes 221192 | tf_op jit(solution)/shard_map/ppermute | solution.py:449
  12.7 7.4 %collective-permute-start.8 = (bf16[2,48,384]{2,1,0:T(8,128)(2,1)}, bf16[2,48,384]{2,1,0:T(8,128)(2,1)S(1)}, u32[]{:S(2)}, u32[]{:S(2)}) collective-permute-start(bf16[2,48,384]{2,1,0:T(8,128)(2,1)} %param.22), channel_id=1, source_target_pairs={{0,3},{1,2},{2,1},{3,0},{4,7},{5,6},{6,5},{7,4},{8,11},{9,10},{10,... | collective-permute-start | bytes 221192 | tf_op jit(solution)/shard_map/ppermute | solution.py:449
  15.4 6.3 %collective-permute-start.9 = (bf16[2,48,384]{2,1,0:T(8,128)(2,1)}, bf16[2,48,384]{2,1,0:T(8,128)(2,1)S(1)}, u32[]{:S(2)}, u32[]{:S(2)}) collective-permute-start(bf16[2,48,384]{2,1,0:T(8,128)(2,1)} %param.22), channel_id=1, source_target_pairs={{0,2},{1,3},{2,0},{3,1},{4,6},{5,7},{6,4},{7,5},{8,10},{9,11},{10,... | collective-permute-start | bytes 221192 | tf_op jit(solution)/shard_map/ppermute | solution.py:449
  17.0 8.8 %collective-permute-start.5 = (bf16[1,48,1536]{2,1,0:T(8,128)(2,1)S(1)}, bf16[1,48,1536]{2,1,0:T(8,128)(2,1)S(1)}, u32[]{:S(2)}, u32[]{:S(2)}) collective-permute-start(bf16[1,48,1536]{2,1,0:T(8,128)(2,1)S(1)} %get-tuple-element.107), channel_id=1, source_target_pairs={{0,16},{4,20},{8,24},{12,28},{16,0},{20,4},{24,8},{28,12},{1,17},{... | collective-permute-start | bytes 442376 | tf_op jit(solution)/shard_map/ppermute | solution.py:449
  18.5 7.8 %collective-permute-start.3 = (bf16[1,48,1536]{2,1,0:T(8,128)(2,1)S(1)}, bf16[1,48,1536]{2,1,0:T(8,128)(2,1)S(1)}, u32[]{:S(2)}, u32[]{:S(2)}) collective-permute-start(bf16[1,48,1536]{2,1,0:T(8,128)(2,1)S(1)} %get-tuple-element.108), channel_id=1, source_target_pairs={{0,8},{4,12},{8,0},{12,4},{16,24},{20,28},{24,16},{28,20},{1,9},{5... | collective-permute-start | bytes 442376 | tf_op jit(solution)/shard_map/ppermute | solution.py:449
  22.6 16.9 %copy-start.8 = (bf16[2,196,196]{2,0,1:T(2,128)(2,1)S(1)}, bf16[2,196,196]{2,0,1:T(2,128)(2,1)}, u32[]{:S(2)}) copy-start(bf16[2,196,196]{2,0,1:T(2,128)(2,1)} %param.18) | copy-start | bytes 460996
  22.6 6.4 %collective-permute-start.15 = (bf16[1,48,1536]{2,1,0:T(8,128)(2,1)S(1)}, bf16[1,48,1536]{2,1,0:T(8,128)(2,1)S(1)}, u32[]{:S(2)}, u32[]{:S(2)}) collective-permute-start(bf16[1,48,1536]{2,1,0:T(8,128)(2,1)S(1)} %get-tuple-element.101), channel_id=1, source_target_pairs={{0,16},{4,20},{8,24},{12,28},{16,0},{20,4},{24,8},{28,12},{1,17},{... | collective-permute-start | bytes 442376 | tf_op jit(solution)/shard_map/ppermute | solution.py:449
  24.2 6.8 %collective-permute-start.11 = (bf16[1,48,1536]{2,1,0:T(8,128)(2,1)S(1)}, bf16[1,48,1536]{2,1,0:T(8,128)(2,1)S(1)}, u32[]{:S(2)}, u32[]{:S(2)}) collective-permute-start(bf16[1,48,1536]{2,1,0:T(8,128)(2,1)S(1)} %get-tuple-element.102), channel_id=1, source_target_pairs={{0,8},{4,12},{8,0},{12,4},{16,24},{20,28},{24,16},{28,20},{1,9},{5... | collective-permute-start | bytes 442376 | tf_op jit(solution)/shard_map/ppermute | solution.py:449
  25.8 9.8 %collective-permute-start.6 = (bf16[2,48,1536]{2,1,0:T(8,128)(2,1)S(1)}, bf16[2,48,1536]{2,1,0:T(8,128)(2,1)S(1)}, u32[]{:S(2)}, u32[]{:S(2)}) collective-permute-start(bf16[2,48,1536]{2,1,0:T(8,128)(2,1)S(1)} %pad_maximum_fusion.6), channel_id=1, source_target_pairs={{0,8},{4,12},{8,0},{12,4},{16,24},{20,28},{24,16},{28,20},{1,9},{5... | collective-permute-start | bytes 884744 | tf_op jit(solution)/shard_map/ppermute | solution.py:449
  26.4 9.2 %collective-permute-start.4 = (bf16[2,48,1536]{2,1,0:T(8,128)(2,1)S(1)}, bf16[2,48,1536]{2,1,0:T(8,128)(2,1)S(1)}, u32[]{:S(2)}, u32[]{:S(2)}) collective-permute-start(bf16[2,48,1536]{2,1,0:T(8,128)(2,1)S(1)} %pad_maximum_fusion.5), channel_id=1, source_target_pairs={{0,16},{4,20},{8,24},{12,28},{16,0},{20,4},{24,8},{28,12},{1,17},{... | collective-permute-start | bytes 884744 | tf_op jit(solution)/shard_map/ppermute | solution.py:449
  29.1 9.6 %collective-permute-start.16 = (bf16[2,48,1536]{2,1,0:T(8,128)(2,1)S(1)}, bf16[2,48,1536]{2,1,0:T(8,128)(2,1)S(1)}, u32[]{:S(2)}, u32[]{:S(2)}) collective-permute-start(bf16[2,48,1536]{2,1,0:T(8,128)(2,1)S(1)} %pad_maximum_fusion.9), channel_id=1, source_target_pairs={{0,8},{4,12},{8,0},{12,4},{16,24},{20,28},{24,16},{28,20},{1,9},{5... | collective-permute-start | bytes 884744 | tf_op jit(solution)/shard_map/ppermute | solution.py:449
  31.0 7.8 %collective-permute-start.12 = (bf16[2,48,1536]{2,1,0:T(8,128)(2,1)S(1)}, bf16[2,48,1536]{2,1,0:T(8,128)(2,1)S(1)}, u32[]{:S(2)}, u32[]{:S(2)}) collective-permute-start(bf16[2,48,1536]{2,1,0:T(8,128)(2,1)S(1)} %pad_maximum_fusion.8), channel_id=1, source_target_pairs={{0,16},{4,20},{8,24},{12,28},{16,0},{20,4},{24,8},{28,12},{1,17},{... | collective-permute-start | bytes 884744 | tf_op jit(solution)/shard_map/ppermute | solution.py:449
  35.6 7.0 %copy-start.3 = (bf16[4,48,1536]{2,1,0:T(8,128)(2,1)}, bf16[4,48,1536]{2,1,0:T(8,128)(2,1)S(1)}, u32[]{:S(2)}) copy-start(bf16[4,48,1536]{2,1,0:T(8,128)(2,1)S(1)} %pad_maximum_fusion.1.args_15_) | copy-start | bytes 1769476
  35.7 6.9 %copy-start.4 = (bf16[4,48,1536]{2,1,0:T(8,128)(2,1)}, bf16[4,48,1536]{2,1,0:T(8,128)(2,1)S(1)}, u32[]{:S(2)}) copy-start(bf16[4,48,1536]{2,1,0:T(8,128)(2,1)S(1)} %pad_maximum_fusion.args_11_) | copy-start | bytes 1769476
  35.7 4.5 %collective-permute-start.14 = (bf16[4,48,1536]{2,1,0:T(8,128)(2,1)S(1)}, bf16[4,48,1536]{2,1,0:T(8,128)(2,1)S(1)}, u32[]{:S(2)}, u32[]{:S(2)}) collective-permute-start(bf16[4,48,1536]{2,1,0:T(8,128)(2,1)S(1)} %pad_maximum_fusion.1.args_15_), channel_id=1, source_target_pairs={{0,4},{4,0},{8,12},{12,8},{16,20},{20,16},{24,28},{28,24},{1,5},{5... | collective-permute-start | bytes 1769480 | tf_op jit(solution)/shard_map/ppermute | solution.py:449
  35.8 4.4 %collective-permute-start.7 = (bf16[4,48,1536]{2,1,0:T(8,128)(2,1)S(1)}, bf16[4,48,1536]{2,1,0:T(8,128)(2,1)S(1)}, u32[]{:S(2)}, u32[]{:S(2)}) collective-permute-start(bf16[4,48,1536]{2,1,0:T(8,128)(2,1)S(1)} %pad_maximum_fusion.args_11_), channel_id=1, source_target_pairs={{0,4},{4,0},{8,12},{12,8},{16,20},{20,16},{24,28},{28,24},{1,5},{5... | collective-permute-start | bytes 1769480 | tf_op jit(solution)/shard_map/ppermute | solution.py:449
  38.8 3.8 %copy-start.5 = (bf16[4,48,1536]{2,1,0:T(8,128)(2,1)}, bf16[4,48,1536]{2,1,0:T(8,128)(2,1)S(1)}, u32[]{:S(2)}) copy-start(bf16[4,48,1536]{2,1,0:T(8,128)(2,1)S(1)} %pad_maximum_fusion.3.args_17_) | copy-start | bytes 1769476
  38.8 2.1 %collective-permute-start.17 = (bf16[4,48,1536]{2,1,0:T(8,128)(2,1)S(1)}, bf16[4,48,1536]{2,1,0:T(8,128)(2,1)S(1)}, u32[]{:S(2)}, u32[]{:S(2)}) collective-permute-start(bf16[4,48,1536]{2,1,0:T(8,128)(2,1)S(1)} %pad_maximum_fusion.3.args_17_), channel_id=1, source_target_pairs={{0,4},{4,0},{8,12},{12,8},{16,20},{20,16},{24,28},{28,24},{1,5},{5... | collective-permute-start | bytes 1769480 | tf_op jit(solution)/shard_map/ppermute | solution.py:449
  38.9 3.7 %copy-start.6 = (bf16[4,48,1536]{2,1,0:T(8,128)(2,1)}, bf16[4,48,1536]{2,1,0:T(8,128)(2,1)S(1)}, u32[]{:S(2)}) copy-start(bf16[4,48,1536]{2,1,0:T(8,128)(2,1)S(1)} %pad_maximum_fusion.2.args_13_) | copy-start | bytes 1769476
  39.0 2.7 %collective-permute-start.13 = (bf16[4,48,1536]{2,1,0:T(8,128)(2,1)S(1)}, bf16[4,48,1536]{2,1,0:T(8,128)(2,1)S(1)}, u32[]{:S(2)}, u32[]{:S(2)}) collective-permute-start(bf16[4,48,1536]{2,1,0:T(8,128)(2,1)S(1)} %pad_maximum_fusion.2.args_13_), channel_id=1, source_target_pairs={{0,4},{4,0},{8,12},{12,8},{16,20},{20,16},{24,28},{28,24},{1,5},{5... | collective-permute-start | bytes 1769480 | tf_op jit(solution)/shard_map/ppermute | solution.py:449
  40.2 2.4 %copy-start.9 = (bf16[4,48,1536]{2,1,0:T(8,128)(2,1)}, bf16[4,48,1536]{2,1,0:T(8,128)(2,1)S(1)}, u32[]{:S(2)}) copy-start(bf16[4,48,1536]{2,1,0:T(8,128)(2,1)S(1)} %collective-permute-done.14.args_16_) | copy-start | bytes 1769476
  40.2 2.4 %copy-start.10 = (bf16[4,48,1536]{2,1,0:T(8,128)(2,1)}, bf16[4,48,1536]{2,1,0:T(8,128)(2,1)S(1)}, u32[]{:S(2)}) copy-start(bf16[4,48,1536]{2,1,0:T(8,128)(2,1)S(1)} %collective-permute-done.7.args_12_) | copy-start | bytes 1769476
  40.9 0.8 copy-start.11
  41.7 0.9 copy-start.12
  86.4 46.5 %collective-permute-start.18 = (bf16[330,8,384]{2,1,0:T(8,128)(2,1)}, bf16[330,8,384]{2,1,0:T(8,128)(2,1)S(1)}, u32[]{:S(2)}, u32[]{:S(2)}) collective-permute-start(bf16[330,8,384]{2,1,0:T(8,128)(2,1)} %get-tuple-element.66.args_20_), channel_id=1, source_target_pairs={{0,1},{1,0},{2,3},{3,2},{4,5},{5,4},{6,7},{7,6},{8,9},{9,8},{10,11... | collective-permute-start | bytes 6082568 | tf_op jit(solution)/shard_map/ppermute | solution.py:449
  86.5 44.1 %all-to-all-start = ((bf16[8,2,2,48,384]{4,3,2,1,0:T(8,128)(2,1)}), bf16[8,2,2,48,384]{4,3,2,1,0:T(8,128)(2,1)S(1)}, u32[]{:S(2)}, u32[]{:S(2)}) async-start(bf16[8,2,2,48,384]{4,3,2,1,0:T(8,128)(2,1)} %get-tuple-element.70), calls=%async_computation | async-start | bytes 2359296 | tf_op jit(solution)/shard_map/all_to_all | solution.py:724
  90.2 43.2 %copy-start.7 = (bf16[2,144,384]{2,1,0:T(8,128)(2,1)S(1)}, bf16[2,144,384]{2,1,0:T(8,128)(2,1)}, u32[]{:S(2)}) copy-start(bf16[2,144,384]{2,1,0:T(8,128)(2,1)} %get-tuple-element.80) | copy-start | bytes 663556
  130.5 20.7 %copy-start.2 = (s32[36]{0:T(128)S(1)}, s32[36]{0:T(128)}, u32[]{:S(2)}) copy-start(s32[36]{0:T(128)} %stack.75.args_0_.meta) | copy-start | bytes 436
  132.9 3.1 %collective-permute-start.20 = (bf16[384,384]{1,0:T(8,128)(2,1)}, bf16[384,384]{1,0:T(8,128)(2,1)S(1)}, u32[]{:S(2)}, u32[]{:S(2)}) collective-permute-start(bf16[384,384]{1,0:T(8,128)(2,1)} %get-tuple-element.78), channel_id=1, source_target_pairs={{0,4},{4,0},{8,12},{12,8},{16,20},{20,16},{24,28},{28,24},{1,5},{5... | collective-permute-start | bytes 884744 | tf_op jit(solution)/shard_map/ppermute | solution.py:449
  133.0 3.1 %collective-permute-start.21 = (bf16[384,384]{1,0:T(8,128)(2,1)}, bf16[384,384]{1,0:T(8,128)(2,1)S(1)}, u32[]{:S(2)}, u32[]{:S(2)}) collective-permute-start(bf16[384,384]{1,0:T(8,128)(2,1)} %get-tuple-element.79), channel_id=1, source_target_pairs={{0,4},{4,0},{8,12},{12,8},{16,20},{20,16},{24,28},{28,24},{1,5},{5... | collective-permute-start | bytes 884744 | tf_op jit(solution)/shard_map/ppermute | solution.py:449
  134.5 1.5 collective-permute-start.22
  134.6 16.6 %collective-permute-start.19 = (bf16[98,8,384]{2,1,0:T(8,128)(2,1)}, bf16[98,8,384]{2,1,0:T(8,128)(2,1)S(1)}, u32[]{:S(2)}, u32[]{:S(2)}) collective-permute-start(bf16[98,8,384]{2,1,0:T(8,128)(2,1)} %get-tuple-element.67.args_21_), channel_id=1, source_target_pairs={{0,1},{1,0},{2,3},{3,2},{4,5},{5,4},{6,7},{7,6},{8,9},{9,8},{10,11... | collective-permute-start | bytes 1806344 | tf_op jit(solution)/shard_map/ppermute | solution.py:449
  136.0 1.0 copy-start
  137.0 1.0 copy-start.1
  138.3 8.3 %collective-permute-start.23 = (bf16[336,384]{1,0:T(8,128)(2,1)S(1)}, bf16[336,384]{1,0:T(8,128)(2,1)S(1)}, u32[]{:S(2)}, u32[]{:S(2)}) collective-permute-start(bf16[336,384]{1,0:T(8,128)(2,1)S(1)} %get-tuple-element.85.refs_4_), channel_id=1, source_target_pairs={{0,8},{4,12},{8,0},{12,4},{16,24},{20,28},{24,16},{28,20},{1,9},{5... | collective-permute-start | bytes 774152 | tf_op jit(solution)/shard_map/ppermute | solution.py:449
  139.9 8.0 %collective-permute-start.24 = (bf16[336,384]{1,0:T(8,128)(2,1)S(1)}, bf16[336,384]{1,0:T(8,128)(2,1)S(1)}, u32[]{:S(2)}, u32[]{:S(2)}) collective-permute-start(bf16[336,384]{1,0:T(8,128)(2,1)S(1)} %get-tuple-element.86.refs_5_), channel_id=1, source_target_pairs={{0,16},{4,20},{8,24},{12,28},{16,0},{20,4},{24,8},{28,12},{1,17},{... | collective-permute-start | bytes 774152 | tf_op jit(solution)/shard_map/ppermute | solution.py:449
  148.0 6.2 %collective-permute-start.25 = (bf16[240,384]{1,0:T(8,128)(2,1)S(1)}, bf16[240,384]{1,0:T(8,128)(2,1)S(1)}, u32[]{:S(2)}, u32[]{:S(2)}) collective-permute-start(bf16[240,384]{1,0:T(8,128)(2,1)S(1)} %get-tuple-element.89.refs_2_), channel_id=1, source_target_pairs={{0,16},{4,20},{8,24},{12,28},{16,0},{20,4},{24,8},{28,12},{1,17},{... | collective-permute-start | bytes 552968 | tf_op jit(solution)/shard_map/ppermute | solution.py:449
  148.5 5.7 %collective-permute-start.26 = (bf16[240,384]{1,0:T(8,128)(2,1)S(1)}, bf16[240,384]{1,0:T(8,128)(2,1)S(1)}, u32[]{:S(2)}, u32[]{:S(2)}) collective-permute-start(bf16[240,384]{1,0:T(8,128)(2,1)S(1)} %get-tuple-element.90.refs_3_), channel_id=1, source_target_pairs={{0,8},{4,12},{8,0},{12,4},{16,24},{20,28},{24,16},{28,20},{1,9},{5... | collective-permute-start | bytes 552968 | tf_op jit(solution)/shard_map/ppermute | solution.py:449
  149.1 5.1 %collective-permute-start.27 = (bf16[2,96,384]{2,1,0:T(8,128)(2,1)S(1)}, bf16[2,96,384]{2,1,0:T(8,128)(2,1)S(1)}, u32[]{:S(2)}, u32[]{:S(2)}) collective-permute-start(bf16[2,96,384]{2,1,0:T(8,128)(2,1)S(1)} %get-tuple-element.91), channel_id=1, source_target_pairs={{0,1},{1,0},{2,3},{3,2},{4,5},{5,4},{6,7},{7,6},{8,9},{9,8},{10,11... | collective-permute-start | bytes 442376 | tf_op jit(solution)/shard_map/ppermute | solution.py:449

commit v4 on v3

--- a/solution.py
+++ b/solution.py
@@ -100,7 +100,7 @@
         for c in range(sz.width // 128):
             part = r[name][:, :, c * 128 : (c + 1) * 128].astype(F32)
             staged[c, : patches * GROUP, :] = part.reshape(patches * GROUP, 128)
-            staged[c, patches * GROUP :, :] = jnp.zeros(((rows - patches) * GROUP, 128), F32)
+            staged[c, patches * GROUP :, :] = jnp.zeros(((rows - patches + 1) * GROUP, 128), F32)
 
     def from_staging(name):
         for c in range(sz.width // 128):
@@ -421,8 +421,8 @@
         ("b2s", (layers, 1, w), F32),
         ("tokb", images, BF),
         ("cotb", images, BF),
-        ("tokf", (w // 128, GROUP * sz.rows, 128), F32),
-        ("cotf", (w // 128, GROUP * sz.rows, 128), F32),
+        ("tokf", (w // 128, GROUP * (sz.rows + 1), 128), F32),
+        ("cotf", (w // 128, GROUP * (sz.rows + 1), 128), F32),
     ):
         scratch.append((name, pltpu.VMEM(shape, dtype)))
     scratch.append(("moved", pltpu.SemaphoreType.DMA((4,))))

time: 156 us -> 156 us (level)
  no operation moved by 1% of the time
where the time goes in v4:
time: 156 us; the launch traced here: 155 us
  Pallas kernels  88.1 us (56%)
  starting transfers between devices  31 us (20%)
  waiting for transfers between devices  27.7 us (18%)
  local copies, waits for them, and re-layouts  4.28 us (3%)
  other arithmetic  3.31 us (2%)
    pallas_call x2, Pallas kernels, run(): pl.pallas_call(functools.partial(kernel_body, sz, kept, names), grid_spec...  84.1 us
    ppermute x28, waiting for transfers between devices, swap(): return lax.ppermute(x, axis, [(i, i ^ k) for i in range(n)])  27.7 us
    ppermute x28, starting transfers between devices, swap(): return lax.ppermute(x, axis, [(i, i ^ k) for i in range(n)])  27.2 us
    all_to_all x1, starting transfers between devices, on_device(): lax.all_to_all(theirs, 'dp', split_axis=0, concat_axis=0, tiled=True)  3.76 us
    unnamed x27, local copies, waits for them, and re-layouts  3.57 us
  transfers between devices with their start and end apart: 29, of which 13 were waited for; matrix products, arithmetic and copies ran while one was open for 3% of the time, Pallas kernels for 28%

profile of v4, /device:TPU:0, one launch (start us, length us, event | category | flops | bytes accessed | tf_op | source)
XLA Modules:
  0.0 155.2 jit_solution(16958851060155404300)
XLA Ops:
  0.6 3.1 %collective-permute-start.1 = (bf16[2,48,384]{2,1,0:T(8,128)(2,1)}, bf16[2,48,384]{2,1,0:T(8,128)(2,1)S(1)}, u32[]{:S(2)}, u32[]{:S(2)}) collective-permute-start(bf16[2,48,384]{2,1,0:T(8,128)(2,1)} %param.20), channel_id=1, source_target_pairs={{0,1},{1,0},{2,3},{3,2},{4,5},{5,4},{6,7},{7,6},{8,9},{9,8},{10,11... | collective-permute-start | bytes 221192 | tf_op jit(solution)/shard_map/ppermute | solution.py:449
  3.7 2.6 %collective-permute-start.2 = (bf16[2,48,384]{2,1,0:T(8,128)(2,1)}, bf16[2,48,384]{2,1,0:T(8,128)(2,1)S(1)}, u32[]{:S(2)}, u32[]{:S(2)}) collective-permute-start(bf16[2,48,384]{2,1,0:T(8,128)(2,1)} %param.20), channel_id=1, source_target_pairs={{0,2},{1,3},{2,0},{3,1},{4,6},{5,7},{6,4},{7,5},{8,10},{9,11},{10,... | collective-permute-start | bytes 221192 | tf_op jit(solution)/shard_map/ppermute | solution.py:449
  6.3 0.6 stack.75.args_0_.meta
  7.0 4.8 %collective-permute-done.2 = bf16[2,48,384]{2,1,0:T(8,128)(2,1)S(1)} collective-permute-done((bf16[2,48,384]{2,1,0:T(8,128)(2,1)}, bf16[2,48,384]{2,1,0:T(8,128)(2,1)S(1)}, u32[]{:S(2)}, u32[]{:S(2)}) %collective-permute-start.2) | collective-permute-done | bytes 73760 | tf_op jit(solution)/shard_map/ppermute | solution.py:449
  11.8 0.9 collective-permute-start.10
  12.7 2.7 %collective-permute-start.8 = (bf16[2,48,384]{2,1,0:T(8,128)(2,1)}, bf16[2,48,384]{2,1,0:T(8,128)(2,1)S(1)}, u32[]{:S(2)}, u32[]{:S(2)}) collective-permute-start(bf16[2,48,384]{2,1,0:T(8,128)(2,1)} %param.22), channel_id=1, source_target_pairs={{0,3},{1,2},{2,1},{3,0},{4,7},{5,6},{6,5},{7,4},{8,11},{9,10},{10,... | collective-permute-start | bytes 221192 | tf_op jit(solution)/shard_map/ppermute | solution.py:449
  15.4 0.6 collective-permute-start.9
  15.9 0.9 select_select_fusion.7
  17.0 1.6 %collective-permute-start.5 = (bf16[1,48,1536]{2,1,0:T(8,128)(2,1)S(1)}, bf16[1,48,1536]{2,1,0:T(8,128)(2,1)S(1)}, u32[]{:S(2)}, u32[]{:S(2)}) collective-permute-start(bf16[1,48,1536]{2,1,0:T(8,128)(2,1)S(1)} %get-tuple-element.107), channel_id=1, source_target_pairs={{0,16},{4,20},{8,24},{12,28},{16,0},{20,4},{24,8},{28,12},{1,17},{... | collective-permute-start | bytes 442376 | tf_op jit(solution)/shard_map/ppermute | solution.py:449
  18.5 1.5 collective-permute-start.3
  20.0 1.6 %collective-permute-done.9 = bf16[2,48,384]{2,1,0:T(8,128)(2,1)S(1)} collective-permute-done((bf16[2,48,384]{2,1,0:T(8,128)(2,1)}, bf16[2,48,384]{2,1,0:T(8,128)(2,1)S(1)}, u32[]{:S(2)}, u32[]{:S(2)}) %collective-permute-start.9) | collective-permute-done | bytes 73760 | tf_op jit(solution)/shard_map/ppermute | solution.py:449
  21.6 0.9 select_select_fusion.3
  22.6 1.6 %collective-permute-start.15 = (bf16[1,48,1536]{2,1,0:T(8,128)(2,1)S(1)}, bf16[1,48,1536]{2,1,0:T(8,128)(2,1)S(1)}, u32[]{:S(2)}, u32[]{:S(2)}) collective-permute-start(bf16[1,48,1536]{2,1,0:T(8,128)(2,1)S(1)} %get-tuple-element.101), channel_id=1, source_target_pairs={{0,16},{4,20},{8,24},{12,28},{16,0},{20,4},{24,8},{28,12},{1,17},{... | collective-permute-start | bytes 442376 | tf_op jit(solution)/shard_map/ppermute | solution.py:449
  24.2 1.5 collective-permute-start.11
  25.8 0.6 collective-permute-start.6
  26.4 0.6 collective-permute-start.4
  27.0 2.1 %collective-permute-done.15 = bf16[1,48,1536]{2,1,0:T(8,128)(2,1)S(1)} collective-permute-done((bf16[1,48,1536]{2,1,0:T(8,128)(2,1)S(1)}, bf16[1,48,1536]{2,1,0:T(8,128)(2,1)S(1)}, u32[]{:S(2)}, u32[]{:S(2)}) %collective-permute-start.15) | collective-permute-done | bytes 147488 | tf_op jit(solution)/shard_map/ppermute | solution.py:449
  29.1 1.9 %collective-permute-start.16 = (bf16[2,48,1536]{2,1,0:T(8,128)(2,1)S(1)}, bf16[2,48,1536]{2,1,0:T(8,128)(2,1)S(1)}, u32[]{:S(2)}, u32[]{:S(2)}) collective-permute-start(bf16[2,48,1536]{2,1,0:T(8,128)(2,1)S(1)} %pad_maximum_fusion.9), channel_id=1, source_target_pairs={{0,8},{4,12},{8,0},{12,4},{16,24},{20,28},{24,16},{28,20},{1,9},{5... | collective-permute-start | bytes 884744 | tf_op jit(solution)/shard_map/ppermute | solution.py:449
  31.0 1.7 %collective-permute-start.12 = (bf16[2,48,1536]{2,1,0:T(8,128)(2,1)S(1)}, bf16[2,48,1536]{2,1,0:T(8,128)(2,1)S(1)}, u32[]{:S(2)}, u32[]{:S(2)}) collective-permute-start(bf16[2,48,1536]{2,1,0:T(8,128)(2,1)S(1)} %pad_maximum_fusion.8), channel_id=1, source_target_pairs={{0,16},{4,20},{8,24},{12,28},{16,0},{20,4},{24,8},{28,12},{1,17},{... | collective-permute-start | bytes 884744 | tf_op jit(solution)/shard_map/ppermute | solution.py:449
  32.7 2.8 %collective-permute-done.6 = bf16[2,48,1536]{2,1,0:T(8,128)(2,1)S(1)} collective-permute-done((bf16[2,48,1536]{2,1,0:T(8,128)(2,1)S(1)}, bf16[2,48,1536]{2,1,0:T(8,128)(2,1)S(1)}, u32[]{:S(2)}, u32[]{:S(2)}) %collective-permute-start.6) | collective-permute-done | bytes 294944 | tf_op jit(solution)/shard_map/ppermute | solution.py:449
  35.8 0.5 collective-permute-start.7
  36.3 2.4 %collective-permute-done.16 = bf16[2,48,1536]{2,1,0:T(8,128)(2,1)S(1)} collective-permute-done((bf16[2,48,1536]{2,1,0:T(8,128)(2,1)S(1)}, bf16[2,48,1536]{2,1,0:T(8,128)(2,1)S(1)}, u32[]{:S(2)}, u32[]{:S(2)}) %collective-permute-start.16) | collective-permute-done | bytes 294944 | tf_op jit(solution)/shard_map/ppermute | solution.py:449
  39.0 0.5 collective-permute-start.13
  39.5 0.7 copy.26.args_7_
  40.2 0.6 collective-permute-done.17.args_18_
  40.9 0.8 collective-permute-done.13.args_14_
  41.7 0.9 copy-done.12
  42.6 43.8 %shard_map.203 = (bf16[330,8,384]{2,1,0:T(8,128)(2,1)}, bf16[98,8,384]{2,1,0:T(8,128)(2,1)}, bf16[2,144,384]{2,1,0:T(8,128)(2,1)}, bf16[8,2,2,48,384]{4,3,2,1,0:T(8,128)(2,1)}, f32[2,2,384,384]{3,2,1,0:T(8,128)}) custom-call(s32[36]{0:T(128)} %stack.75.args_0_.meta, bf16[196,24,384]{2,1,0:T(8,128)(2,1)} %bitcast.26, bf16[196,24,384]{2,1,0:T(8,128)(2,1)} %bitcast.28, ...), custom_call_target="tpu_custom_call" | custom-call | flops 22649241600 | bytes 56623104 | tf_op jit(solution)/shard_map/pallas_call | solution.py:431
  86.5 3.8 %all-to-all-start = ((bf16[8,2,2,48,384]{4,3,2,1,0:T(8,128)(2,1)}), bf16[8,2,2,48,384]{4,3,2,1,0:T(8,128)(2,1)S(1)}, u32[]{:S(2)}, u32[]{:S(2)}) async-start(bf16[8,2,2,48,384]{4,3,2,1,0:T(8,128)(2,1)} %get-tuple-element.70), calls=%async_computation | async-start | bytes 2359296 | tf_op jit(solution)/shard_map/all_to_all | solution.py:724
  90.2 40.3 %shard_map.204 = (bf16[196,24,384]{2,1,0:T(8,128)(2,1)}, bf16[196,24,384]{2,1,0:T(8,128)(2,1)}, bf16[2,144,384]{2,1,0:T(8,128)(2,1)}, bf16[384,384]{1,0:T(8,128)...) custom-call(s32[36]{0:T(128)} %stack.75.args_0_.meta, ...), custom_call_target="tpu_custom_call" | custom-call | flops 22649241600 | bytes 56623104 | tf_op jit(solution)/shard_map/pallas_call | solution.py:431
  130.6 2.3 %collective-permute-done.18.sent0 = bf16[330,8,384]{2,1,0:T(8,128)(2,1)S(1)} collective-permute-done((bf16[330,8,384]{2,1,0:T(8,128)(2,1)}, bf16[330,8,384]{2,1,0:T(8,128)(2,1)S(1)}, u32[]{:S(2)}, u32[]{:S(2)}) %collective-permute-start.18) | collective-permute-done | bytes 2027552 | tf_op jit(solution)/shard_map/ppermute | solution.py:449
  133.0 0.5 collective-permute-start.21
  133.5 1.0 fusion.1.refs_4_
  134.9 1.1 collective-permute-done.22.refs_5_
  136.0 1.0 copy-done
  137.0 1.0 copy-done.1
  138.0 0.3 shard_map.206
  138.3 1.5 collective-permute-start.23
  139.8 0.5 collective-permute-start.24
  140.4 6.3 %collective-permute-done.23.refs_2_.refs_6_ = bf16[336,384]{1,0:T(8,128)(2,1)S(1)} collective-permute-done((bf16[336,384]{1,0:T(8,128)(2,1)S(1)}, bf16[336,384]{1,0:T(8,128)(2,1)S(1)}, u32[]{:S(2)}, u32[]{:S(2)}) %collective-permute-start.23) | collective-permute-done | bytes 258080 | tf_op jit(solution)/shard_map/ppermute | solution.py:449
  146.6 1.2 collective-permute-done.24.refs_3_.refs_7_
  148.0 0.6 collective-permute-start.25
  148.5 0.5 collective-permute-start.26
  149.1 1.0 collective-permute-start.27
  150.1 1.1 collective-permute-done.19.sent1
  151.2 2.5 %shard_map.205 = (bf16[196,24,384]{2,1,0:T(8,128)(2,1)}, bf16[196,24,384]{2,1,0:T(8,128)(2,1)}) custom-call(s32[36]{0:T(128)S(1)} %copy-done.2, bf16[330,8,384]{2,1,0:T(8,128)(2,1)S(1)} %collective-permute-done.18.sent0, bf16[98,8,384]{2,1,0:T(8,128)(2,1)S(1)} %collective-permute-done.19.sent1, ...), custom_call_target="tpu_custom_call", output_to_operand_aliasing={{0}: (3, {}), {1}: (4, {})} | custom-call | bytes 4816896 | tf_op jit(solution)/shard_map/pallas_call | solution.py:521
  153.8 0.4 collective-permute-done.27.refs_6_
  154.2 1.0 shard_map.208
  (60 shorter events, 1.4 us)
Async XLA Ops:
  0.6 6.3 %collective-permute-start.1 = (bf16[2,48,384]{2,1,0:T(8,128)(2,1)}, bf16[2,48,384]{2,1,0:T(8,128)(2,1)S(1)}, u32[]{:S(2)}, u32[]{:S(2)}) collective-permute-start(bf16[2,48,384]{2,1,0:T(8,128)(2,1)} %param.20), channel_id=1, source_target_pairs={{0,1},{1,0},{2,3},{3,2},{4,5},{5,4},{6,7},{7,6},{8,9},{9,8},{10,11... | collective-permute-start | bytes 221192 | tf_op jit(solution)/shard_map/ppermute | solution.py:449
  3.7 8.0 %collective-permute-start.2 = (bf16[2,48,384]{2,1,0:T(8,128)(2,1)}, bf16[2,48,384]{2,1,0:T(8,128)(2,1)S(1)}, u32[]{:S(2)}, u32[]{:S(2)}) collective-permute-start(bf16[2,48,384]{2,1,0:T(8,128)(2,1)} %param.20), channel_id=1, source_target_pairs={{0,2},{1,3},{2,0},{3,1},{4,6},{5,7},{6,4},{7,5},{8,10},{9,11},{10,... | collective-permute-start | bytes 221192 | tf_op jit(solution)/shard_map/ppermute | solution.py:449
  6.3 9.6 %collective-permute-start = (bf16[2,48,384]{2,1,0:T(8,128)(2,1)}, bf16[2,48,384]{2,1,0:T(8,128)(2,1)S(1)}, u32[]{:S(2)}, u32[]{:S(2)}) collective-permute-start(bf16[2,48,384]{2,1,0:T(8,128)(2,1)} %param.20), channel_id=1, source_target_pairs={{0,3},{1,2},{2,1},{3,0},{4,7},{5,6},{6,5},{7,4},{8,11},{9,10},{10,... | collective-permute-start | bytes 221192 | tf_op jit(solution)/shard_map/ppermute | solution.py:449
  11.8 8.3 %collective-permute-start.10 = (bf16[2,48,384]{2,1,0:T(8,128)(2,1)}, bf16[2,48,384]{2,1,0:T(8,128)(2,1)S(1)}, u32[]{:S(2)}, u32[]{:S(2)}) collective-permute-start(bf16[2,48,384]{2,1,0:T(8,128)(2,1)} %param.22), channel_id=1, source_target_pairs={{0,1},{1,0},{2,3},{3,2},{4,5},{5,4},{6,7},{7,6},{8,9},{9,8},{10,11... | collective-permute-start | bytes 221192 | tf_op jit(solution)/shard_map/ppermute | solution.py:449
  12.7 7.4 %collective-permute-start.8 = (bf16[2,48,384]{2,1,0:T(8,128)(2,1)}, bf16[2,48,384]{2,1,0:T(8,128)(2,1)S(1)}, u32[]{:S(2)}, u32[]{:S(2)}) collective-permute-start(bf16[2,48,384]{2,1,0:T(8,128)(2,1)} %param.22), channel_id=1, source_target_pairs={{0,3},{1,2},{2,1},{3,0},{4,7},{5,6},{6,5},{7,4},{8,11},{9,10},{10,... | collective-permute-start | bytes 221192 | tf_op jit(solution)/shard_map/ppermute | solution.py:449
  15.4 6.3 %collective-permute-start.9 = (bf16[2,48,384]{2,1,0:T(8,128)(2,1)}, bf16[2,48,384]{2,1,0:T(8,128)(2,1)S(1)}, u32[]{:S(2)}, u32[]{:S(2)}) collective-permute-start(bf16[2,48,384]{2,1,0:T(8,128)(2,1)} %param.22), channel_id=1, source_target_pairs={{0,2},{1,3},{2,0},{3,1},{4,6},{5,7},{6,4},{7,5},{8,10},{9,11},{10,... | collective-permute-start | bytes 221192 | tf_op jit(solution)/shard_map/ppermute | solution.py:449
  17.0 8.8 %collective-permute-start.5 = (bf16[1,48,1536]{2,1,0:T(8,128)(2,1)S(1)}, bf16[1,48,1536]{2,1,0:T(8,128)(2,1)S(1)}, u32[]{:S(2)}, u32[]{:S(2)}) collective-permute-start(bf16[1,48,1536]{2,1,0:T(8,128)(2,1)S(1)} %get-tuple-element.107), channel_id=1, source_target_pairs={{0,16},{4,20},{8,24},{12,28},{16,0},{20,4},{24,8},{28,12},{1,17},{... | collective-permute-start | bytes 442376 | tf_op jit(solution)/shard_map/ppermute | solution.py:449
  18.5 7.8 %collective-permute-start.3 = (bf16[1,48,1536]{2,1,0:T(8,128)(2,1)S(1)}, bf16[1,48,1536]{2,1,0:T(8,128)(2,1)S(1)}, u32[]{:S(2)}, u32[]{:S(2)}) collective-permute-start(bf16[1,48,1536]{2,1,0:T(8,128)(2,1)S(1)} %get-tuple-element.108), channel_id=1, source_target_pairs={{0,8},{4,12},{8,0},{12,4},{16,24},{20,28},{24,16},{28,20},{1,9},{5... | collective-permute-start | bytes 442376 | tf_op jit(solution)/shard_map/ppermute | solution.py:449
  22.6 16.9 %copy-start.8 = (bf16[2,196,196]{2,0,1:T(2,128)(2,1)S(1)}, bf16[2,196,196]{2,0,1:T(2,128)(2,1)}, u32[]{:S(2)}) copy-start(bf16[2,196,196]{2,0,1:T(2,128)(2,1)} %param.18) | copy-start | bytes 460996
  22.6 6.4 %collective-permute-start.15 = (bf16[1,48,1536]{2,1,0:T(8,128)(2,1)S(1)}, bf16[1,48,1536]{2,1,0:T(8,128)(2,1)S(1)}, u32[]{:S(2)}, u32[]{:S(2)}) collective-permute-start(bf16[1,48,1536]{2,1,0:T(8,128)(2,1)S(1)} %get-tuple-element.101), channel_id=1, source_target_pairs={{0,16},{4,20},{8,24},{12,28},{16,0},{20,4},{24,8},{28,12},{1,17},{... | collective-permute-start | bytes 442376 | tf_op jit(solution)/shard_map/ppermute | solution.py:449
  24.2 6.8 %collective-permute-start.11 = (bf16[1,48,1536]{2,1,0:T(8,128)(2,1)S(1)}, bf16[1,48,1536]{2,1,0:T(8,128)(2,1)S(1)}, u32[]{:S(2)}, u32[]{:S(2)}) collective-permute-start(bf16[1,48,1536]{2,1,0:T(8,128)(2,1)S(1)} %get-tuple-element.102), channel_id=1, source_target_pairs={{0,8},{4,12},{8,0},{12,4},{16,24},{20,28},{24,16},{28,20},{1,9},{5... | collective-permute-start | bytes 442376 | tf_op jit(solution)/shard_map/ppermute | solution.py:449
  25.8 9.8 %collective-permute-start.6 = (bf16[2,48,1536]{2,1,0:T(8,128)(2,1)S(1)}, bf16[2,48,1536]{2,1,0:T(8,128)(2,1)S(1)}, u32[]{:S(2)}, u32[]{:S(2)}) collective-permute-start(bf16[2,48,1536]{2,1,0:T(8,128)(2,1)S(1)} %pad_maximum_fusion.6), channel_id=1, source_target_pairs={{0,8},{4,12},{8,0},{12,4},{16,24},{20,28},{24,16},{28,20},{1,9},{5... | collective-permute-start | bytes 884744 | tf_op jit(solution)/shard_map/ppermute | solution.py:449
  26.4 9.2 %collective-permute-start.4 = (bf16[2,48,1536]{2,1,0:T(8,128)(2,1)S(1)}, bf16[2,48,1536]{2,1,0:T(8,128)(2,1)S(1)}, u32[]{:S(2)}, u32[]{:S(2)}) collective-permute-start(bf16[2,48,1536]{2,1,0:T(8,128)(2,1)S(1)} %pad_maximum_fusion.5), channel_id=1, source_target_pairs={{0,16},{4,20},{8,24},{12,28},{16,0},{20,4},{24,8},{28,12},{1,17},{... | collective-permute-start | bytes 884744 | tf_op jit(solution)/shard_map/ppermute | solution.py:449
  29.1 9.6 %collective-permute-start.16 = (bf16[2,48,1536]{2,1,0:T(8,128)(2,1)S(1)}, bf16[2,48,1536]{2,1,0:T(8,128)(2,1)S(1)}, u32[]{:S(2)}, u32[]{:S(2)}) collective-permute-start(bf16[2,48,1536]{2,1,0:T(8,128)(2,1)S(1)} %pad_maximum_fusion.9), channel_id=1, source_target_pairs={{0,8},{4,12},{8,0},{12,4},{16,24},{20,28},{24,16},{28,20},{1,9},{5... | collective-permute-start | bytes 884744 | tf_op jit(solution)/shard_map/ppermute | solution.py:449
  31.0 7.8 %collective-permute-start.12 = (bf16[2,48,1536]{2,1,0:T(8,128)(2,1)S(1)}, bf16[2,48,1536]{2,1,0:T(8,128)(2,1)S(1)}, u32[]{:S(2)}, u32[]{:S(2)}) collective-permute-start(bf16[2,48,1536]{2,1,0:T(8,128)(2,1)S(1)} %pad_maximum_fusion.8), channel_id=1, source_target_pairs={{0,16},{4,20},{8,24},{12,28},{16,0},{20,4},{24,8},{28,12},{1,17},{... | collective-permute-start | bytes 884744 | tf_op jit(solution)/shard_map/ppermute | solution.py:449
  35.6 7.0 %copy-start.3 = (bf16[4,48,1536]{2,1,0:T(8,128)(2,1)}, bf16[4,48,1536]{2,1,0:T(8,128)(2,1)S(1)}, u32[]{:S(2)}) copy-start(bf16[4,48,1536]{2,1,0:T(8,128)(2,1)S(1)} %pad_maximum_fusion.1.args_15_) | copy-start | bytes 1769476
  35.7 6.9 %copy-start.4 = (bf16[4,48,1536]{2,1,0:T(8,128)(2,1)}, bf16[4,48,1536]{2,1,0:T(8,128)(2,1)S(1)}, u32[]{:S(2)}) copy-start(bf16[4,48,1536]{2,1,0:T(8,128)(2,1)S(1)} %pad_maximum_fusion.args_11_) | copy-start | bytes 1769476
  35.7 4.5 %collective-permute-start.14 = (bf16[4,48,1536]{2,1,0:T(8,128)(2,1)S(1)}, bf16[4,48,1536]{2,1,0:T(8,128)(2,1)S(1)}, u32[]{:S(2)}, u32[]{:S(2)}) collective-permute-start(bf16[4,48,1536]{2,1,0:T(8,128)(2,1)S(1)} %pad_maximum_fusion.1.args_15_), channel_id=1, source_target_pairs={{0,4},{4,0},{8,12},{12,8},{16,20},{20,16},{24,28},{28,24},{1,5},{5... | collective-permute-start | bytes 1769480 | tf_op jit(solution)/shard_map/ppermute | solution.py:449
  35.8 4.4 %collective-permute-start.7 = (bf16[4,48,1536]{2,1,0:T(8,128)(2,1)S(1)}, bf16[4,48,1536]{2,1,0:T(8,128)(2,1)S(1)}, u32[]{:S(2)}, u32[]{:S(2)}) collective-permute-start(bf16[4,48,1536]{2,1,0:T(8,128)(2,1)S(1)} %pad_maximum_fusion.args_11_), channel_id=1, source_target_pairs={{0,4},{4,0},{8,12},{12,8},{16,20},{20,16},{24,28},{28,24},{1,5},{5... | collective-permute-start | bytes 1769480 | tf_op jit(solution)/shard_map/ppermute | solution.py:449
  38.8 3.8 %copy-start.5 = (bf16[4,48,1536]{2,1,0:T(8,128)(2,1)}, bf16[4,48,1536]{2,1,0:T(8,128)(2,1)S(1)}, u32[]{:S(2)}) copy-start(bf16[4,48,1536]{2,1,0:T(8,128)(2,1)S(1)} %pad_maximum_fusion.3.args_17_) | copy-start | bytes 1769476
  38.8 2.1 %collective-permute-start.17 = (bf16[4,48,1536]{2,1,0:T(8,128)(2,1)S(1)}, bf16[4,48,1536]{2,1,0:T(8,128)(2,1)S(1)}, u32[]{:S(2)}, u32[]{:S(2)}) collective-permute-start(bf16[4,48,1536]{2,1,0:T(8,128)(2,1)S(1)} %pad_maximum_fusion.3.args_17_), channel_id=1, source_target_pairs={{0,4},{4,0},{8,12},{12,8},{16,20},{20,16},{24,28},{28,24},{1,5},{5... | collective-permute-start | bytes 1769480 | tf_op jit(solution)/shard_map/ppermute | solution.py:449
  38.9 3.7 %copy-start.6 = (bf16[4,48,1536]{2,1,0:T(8,128)(2,1)}, bf16[4,48,1536]{2,1,0:T(8,128)(2,1)S(1)}, u32[]{:S(2)}) copy-start(bf16[4,48,1536]{2,1,0:T(8,128)(2,1)S(1)} %pad_maximum_fusion.2.args_13_) | copy-start | bytes 1769476
  39.0 2.7 %collective-permute-start.13 = (bf16[4,48,1536]{2,1,0:T(8,128)(2,1)S(1)}, bf16[4,48,1536]{2,1,0:T(8,128)(2,1)S(1)}, u32[]{:S(2)}, u32[]{:S(2)}) collective-permute-start(bf16[4,48,1536]{2,1,0:T(8,128)(2,1)S(1)} %pad_maximum_fusion.2.args_13_), channel_id=1, source_target_pairs={{0,4},{4,0},{8,12},{12,8},{16,20},{20,16},{24,28},{28,24},{1,5},{5... | collective-permute-start | bytes 1769480 | tf_op jit(solution)/shard_map/ppermute | solution.py:449
  40.2 2.4 %copy-start.9 = (bf16[4,48,1536]{2,1,0:T(8,128)(2,1)}, bf16[4,48,1536]{2,1,0:T(8,128)(2,1)S(1)}, u32[]{:S(2)}) copy-start(bf16[4,48,1536]{2,1,0:T(8,128)(2,1)S(1)} %collective-permute-done.14.args_16_) | copy-start | bytes 1769476
  40.2 2.4 %copy-start.10 = (bf16[4,48,1536]{2,1,0:T(8,128)(2,1)}, bf16[4,48,1536]{2,1,0:T(8,128)(2,1)S(1)}, u32[]{:S(2)}) copy-start(bf16[4,48,1536]{2,1,0:T(8,128)(2,1)S(1)} %collective-permute-done.7.args_12_) | copy-start | bytes 1769476
  40.9 0.8 copy-start.11
  41.7 0.9 copy-start.12
  86.4 46.5 %collective-permute-start.18 = (bf16[330,8,384]{2,1,0:T(8,128)(2,1)}, bf16[330,8,384]{2,1,0:T(8,128)(2,1)S(1)}, u32[]{:S(2)}, u32[]{:S(2)}) collective-permute-start(bf16[330,8,384]{2,1,0:T(8,128)(2,1)} %get-tuple-element.66.args_20_), channel_id=1, source_target_pairs={{0,1},{1,0},{2,3},{3,2},{4,5},{5,4},{6,7},{7,6},{8,9},{9,8},{10,11... | collective-permute-start | bytes 6082568 | tf_op jit(solution)/shard_map/ppermute | solution.py:449
  86.5 44.1 %all-to-all-start = ((bf16[8,2,2,48,384]{4,3,2,1,0:T(8,128)(2,1)}), bf16[8,2,2,48,384]{4,3,2,1,0:T(8,128)(2,1)S(1)}, u32[]{:S(2)}, u32[]{:S(2)}) async-start(bf16[8,2,2,48,384]{4,3,2,1,0:T(8,128)(2,1)} %get-tuple-element.70), calls=%async_computation | async-start | bytes 2359296 | tf_op jit(solution)/shard_map/all_to_all | solution.py:724
  90.2 43.2 %copy-start.7 = (bf16[2,144,384]{2,1,0:T(8,128)(2,1)S(1)}, bf16[2,144,384]{2,1,0:T(8,128)(2,1)}, u32[]{:S(2)}) copy-start(bf16[2,144,384]{2,1,0:T(8,128)(2,1)} %get-tuple-element.80) | copy-start | bytes 663556
  130.6 20.7 %copy-start.2 = (s32[36]{0:T(128)S(1)}, s32[36]{0:T(128)}, u32[]{:S(2)}) copy-start(s32[36]{0:T(128)} %stack.75.args_0_.meta) | copy-start | bytes 436
  132.9 3.1 %collective-permute-start.20 = (bf16[384,384]{1,0:T(8,128)(2,1)}, bf16[384,384]{1,0:T(8,128)(2,1)S(1)}, u32[]{:S(2)}, u32[]{:S(2)}) collective-permute-start(bf16[384,384]{1,0:T(8,128)(2,1)} %get-tuple-element.78), channel_id=1, source_target_pairs={{0,4},{4,0},{8,12},{12,8},{16,20},{20,16},{24,28},{28,24},{1,5},{5... | collective-permute-start | bytes 884744 | tf_op jit(solution)/shard_map/ppermute | solution.py:449
  133.0 3.1 %collective-permute-start.21 = (bf16[384,384]{1,0:T(8,128)(2,1)}, bf16[384,384]{1,0:T(8,128)(2,1)S(1)}, u32[]{:S(2)}, u32[]{:S(2)}) collective-permute-start(bf16[384,384]{1,0:T(8,128)(2,1)} %get-tuple-element.79), channel_id=1, source_target_pairs={{0,4},{4,0},{8,12},{12,8},{16,20},{20,16},{24,28},{28,24},{1,5},{5... | collective-permute-start | bytes 884744 | tf_op jit(solution)/shard_map/ppermute | solution.py:449
  134.5 1.5 collective-permute-start.22
  134.6 16.6 %collective-permute-start.19 = (bf16[98,8,384]{2,1,0:T(8,128)(2,1)}, bf16[98,8,384]{2,1,0:T(8,128)(2,1)S(1)}, u32[]{:S(2)}, u32[]{:S(2)}) collective-permute-start(bf16[98,8,384]{2,1,0:T(8,128)(2,1)} %get-tuple-element.67.args_21_), channel_id=1, source_target_pairs={{0,1},{1,0},{2,3},{3,2},{4,5},{5,4},{6,7},{7,6},{8,9},{9,8},{10,11... | collective-permute-start | bytes 1806344 | tf_op jit(solution)/shard_map/ppermute | solution.py:449
  136.0 1.0 copy-start
  137.0 1.0 copy-start.1
  138.3 8.3 %collective-permute-start.23 = (bf16[336,384]{1,0:T(8,128)(2,1)S(1)}, bf16[336,384]{1,0:T(8,128)(2,1)S(1)}, u32[]{:S(2)}, u32[]{:S(2)}) collective-permute-start(bf16[336,384]{1,0:T(8,128)(2,1)S(1)} %get-tuple-element.85.refs_4_), channel_id=1, source_target_pairs={{0,8},{4,12},{8,0},{12,4},{16,24},{20,28},{24,16},{28,20},{1,9},{5... | collective-permute-start | bytes 774152 | tf_op jit(solution)/shard_map/ppermute | solution.py:449
  139.8 8.0 %collective-permute-start.24 = (bf16[336,384]{1,0:T(8,128)(2,1)S(1)}, bf16[336,384]{1,0:T(8,128)(2,1)S(1)}, u32[]{:S(2)}, u32[]{:S(2)}) collective-permute-start(bf16[336,384]{1,0:T(8,128)(2,1)S(1)} %get-tuple-element.86.refs_5_), channel_id=1, source_target_pairs={{0,16},{4,20},{8,24},{12,28},{16,0},{20,4},{24,8},{28,12},{1,17},{... | collective-permute-start | bytes 774152 | tf_op jit(solution)/shard_map/ppermute | solution.py:449
  148.0 6.2 %collective-permute-start.25 = (bf16[240,384]{1,0:T(8,128)(2,1)S(1)}, bf16[240,384]{1,0:T(8,128)(2,1)S(1)}, u32[]{:S(2)}, u32[]{:S(2)}) collective-permute-start(bf16[240,384]{1,0:T(8,128)(2,1)S(1)} %get-tuple-element.89.refs_2_), channel_id=1, source_target_pairs={{0,16},{4,20},{8,24},{12,28},{16,0},{20,4},{24,8},{28,12},{1,17},{... | collective-permute-start | bytes 552968 | tf_op jit(solution)/shard_map/ppermute | solution.py:449
  148.5 5.7 %collective-permute-start.26 = (bf16[240,384]{1,0:T(8,128)(2,1)S(1)}, bf16[240,384]{1,0:T(8,128)(2,1)S(1)}, u32[]{:S(2)}, u32[]{:S(2)}) collective-permute-start(bf16[240,384]{1,0:T(8,128)(2,1)S(1)} %get-tuple-element.90.refs_3_), channel_id=1, source_target_pairs={{0,8},{4,12},{8,0},{12,4},{16,24},{20,28},{24,16},{28,20},{1,9},{5... | collective-permute-start | bytes 552968 | tf_op jit(solution)/shard_map/ppermute | solution.py:449
  149.1 5.1 %collective-permute-start.27 = (bf16[2,96,384]{2,1,0:T(8,128)(2,1)S(1)}, bf16[2,96,384]{2,1,0:T(8,128)(2,1)S(1)}, u32[]{:S(2)}, u32[]{:S(2)}) collective-permute-start(bf16[2,96,384]{2,1,0:T(8,128)(2,1)S(1)} %get-tuple-element.91), channel_id=1, source_target_pairs={{0,1},{1,0},{2,3},{3,2},{4,5},{5,4},{6,7},{7,6},{8,9},{9,8},{10,11... | collective-permute-start | bytes 442376 | tf_op jit(solution)/shard_map/ppermute | solution.py:449
